TPU v7x, 32 devices: a whole 2x2x4 slice. The times are simulated.
32 devices in a mesh: seq: 8 (over z, x), head: 4 (over y, core).
Axes of the slice: x: 2, y: 2, z: 4, core: 2. Of those that a mesh axis runs over, the one named last changes fastest.
Arguments:
- hidden: bfloat16 [4096, 2048], P(('seq', 'head')), may hold values from -6 to 6
- norm_gain: float32 [2048], replicated, may hold values from 0.5 to 1.5
- expert_choice: int32 [4096, 8], P(('seq', 'head')), may hold values from 0 to 15, all different within a row; in each aligned block of 128 rows (0 to 127, 128 to 255, ...) at most 72 rows name the same one
- route_weight: bfloat16 [4096, 8], P(('seq', 'head')), may hold values from 0.049804688 to 0.3984375
- gate_weight: bfloat16 [32, 2048, 384], P(('seq', 'head')), may hold values from -0.125 to 0.125
- up_weight: bfloat16 [32, 2048, 384], P(('seq', 'head')), may hold values from -0.125 to 0.125
- down_weight: bfloat16 [32, 384, 2048], P(('seq', 'head')), may hold values from -0.21875 to 0.21875
- layer_grad: bfloat16 [4096, 2048], P(('seq', 'head')), may hold values from -6 to 6
- scan_input: bfloat16 [4096, 2048], P('seq', 'head'), may hold values from -6 to 6
- state_input: bfloat16 [4096, 128], P('seq'), may hold values from -0.5 to 0.5
- state_output: bfloat16 [4096, 128], P('seq'), may hold values from -0.5 to 0.5
- log_decay: float32 [4096, 32], P('seq', 'head'), may hold values from -1.5 to 0
- skip_gain: float32 [32], P('head'), may hold values from 0.5 to 2
- out_weight: bfloat16 [2048, 2048], P(None, 'head'), may hold values from -0.125 to 0.125
Outputs:
- d_hidden: bfloat16 [4096, 2048], P(('seq', 'head'))
- d_norm_gain: float32 [2048], replicated
- d_route_weight: bfloat16 [4096, 8], P(('seq', 'head'))
- d_gate_weight: bfloat16 [32, 2048, 384], P(('seq', 'head'))
- d_up_weight: bfloat16 [32, 2048, 384], P(('seq', 'head'))
- d_down_weight: bfloat16 [32, 384, 2048], P(('seq', 'head'))
- d_out_weight: bfloat16 [2048, 2048], P('seq', 'head')
- d_scan_input: bfloat16 [4096, 2048], P('seq', 'head')
- d_state_input: float32 [4096, 128], P('seq')
- d_state_output: float32 [4096, 128], P('seq')
- d_log_decay: float32 [4096, 32], P('seq', 'head')
- d_skip_gain: float32 [32], P('head')
Inputs may be any that keep to these rules, and one draw needn't show every extreme that they name: `expert_choice`: each row names 8 different experts. In each aligned block of 128 rows (the rows of one device) no expert is named by more than 72 rows, and in some block some expert is named by exactly 72 rows.
All inputs are finite; a program needn't handle non-finite values.
Results may differ from a plain program's by a relative error of at most 0.015.
Values may be sent and summed in bfloat16 or wider, within the bound.
No kernel may reach another device: no remote copies, remote signals or barrier semaphores. Data moves between devices by JAX's collectives and lax.ppermute only.
A program may use at most 256 MiB of HBM per device.

v0:
```python
import jax
import jax.numpy as jnp
from jax import lax
from jax.sharding import PartitionSpec as P

highest = lax.Precision.HIGHEST
epsilon = 1e-06


def swapped(value, axis, distance):
    mask = 2**distance
    pairs = [(source, source ^ mask) for source in range(lax.axis_size(axis))]
    return lax.ppermute(value, axis, pairs)


def carried_in(part, axis, combine, identity, reverse):
    count = lax.axis_size(axis)
    place = lax.axis_index(axis)
    ahead = count - 1 - place if reverse else place
    gathered = jax.tree.map(lambda a: lax.all_gather(a, axis), part)
    state = jax.tree.map(lambda a, e: jnp.zeros_like(a) + jnp.asarray(e, a.dtype), part, identity)

    def one(turn, state):
        source = count - 1 - turn if reverse else turn
        return combine(
            state, jax.tree.map(lambda a: lax.dynamic_index_in_dim(a, source, 0, False), gathered)
        )

    return lax.fori_loop(0, ahead, one, state)


def inner_rows(left_side, right_side):
    return lax.dot_general(
        left_side, right_side, (((0,), (0,)), ((), ())), preferred_element_type=jnp.float32
    )


def inner_columns(left_side, right_side):
    return lax.dot_general(
        left_side, right_side, (((1,), (1,)), ((), ())), preferred_element_type=jnp.float32
    )


def expert_half(normed_rows, grad_rows, prob_rows, gate_half, up_half, down_half):
    gate_pre = jnp.dot(normed_rows, gate_half, preferred_element_type=jnp.float32)
    up_pre = jnp.dot(normed_rows, up_half, preferred_element_type=jnp.float32)
    gate_sig = jax.nn.sigmoid(gate_pre)
    active = (gate_pre * gate_sig * up_pre).astype(jnp.bfloat16)
    back_grad = inner_columns(grad_rows, down_half)
    weight_column = prob_rows.astype(jnp.float32)[:, None]
    prob_part = jnp.sum(active.astype(jnp.float32) * back_grad, axis=1)
    d_active = weight_column * back_grad
    scaled = (weight_column * grad_rows.astype(jnp.float32)).astype(jnp.bfloat16)
    d_gate = (d_active * up_pre * gate_sig * (1.0 + gate_pre * (1.0 - gate_sig))).astype(
        jnp.bfloat16
    )
    d_up = (d_active * gate_pre * gate_sig).astype(jnp.bfloat16)
    gate_term = inner_rows(normed_rows, d_gate)
    up_term = inner_rows(normed_rows, d_up)
    down_term = inner_rows(active, scaled)
    row_part = inner_columns(d_gate, gate_half) + inner_columns(d_up, up_half)
    return (gate_term, up_term, down_term, row_part, prob_part)


def combine_forward(earlier_part, later_part):
    return (
        earlier_part[0] * later_part[0],
        later_part[0][:, None, None] * earlier_part[1] + later_part[1],
    )


def combine_backward(earlier_part, later_part):
    return (
        later_part[0] * earlier_part[0],
        later_part[1] + later_part[0][:, None, None] * earlier_part[1],
    )


def one_hot_table(target, columns):
    return target[:, None] == jnp.arange(columns, dtype=jnp.int32)[None, :]


def shards(
    hidden,
    norm_gain,
    expert_choice,
    route_weight,
    gate_weight,
    up_weight,
    down_weight,
    layer_grad,
    scan_input,
    state_input,
    state_output,
    log_decay,
    skip_gain,
    out_weight,
):
    devices = lax.axis_size("seq") * lax.axis_size("head")
    experts = devices // 2
    tok_count, model_width = hidden.shape
    top_count = expert_choice.shape[1]
    half_rows = 9 * tok_count * top_count // (16 * experts)
    hidden_wide = hidden.astype(jnp.float32)
    inverse = lax.rsqrt(jnp.mean(hidden_wide * hidden_wide, axis=1, keepdims=True) + epsilon)
    normalized = hidden_wide * inverse
    normed = (normalized * norm_gain[None, :]).astype(jnp.bfloat16)
    flat_choice = expert_choice.reshape(-1)
    chosen = one_hot_table(flat_choice, experts).astype(jnp.int32)
    position = jnp.sum((jnp.cumsum(chosen, axis=0) - chosen) * chosen, axis=1)
    target = (2 * flat_choice + position // half_rows) * half_rows + position % half_rows
    slot_table = one_hot_table(target, devices * half_rows)
    slot_onehot = slot_table.astype(jnp.bfloat16)
    token_table = jnp.sum(
        slot_table.reshape(tok_count, top_count, devices * half_rows).astype(jnp.int32), axis=1
    ).astype(jnp.bfloat16)
    flat_weight = route_weight.reshape(-1, 1)
    send_normed = (
        inner_rows(token_table, normed)
        .astype(jnp.bfloat16)
        .reshape(devices, half_rows, model_width)
    )
    send_grad = (
        inner_rows(token_table, layer_grad)
        .astype(jnp.bfloat16)
        .reshape(devices, half_rows, model_width)
    )
    send_weight = (
        inner_rows(slot_onehot, flat_weight).astype(jnp.bfloat16).reshape(devices, half_rows)
    )
    received = (
        lax.all_to_all(send_normed, ("seq", "head"), split_axis=0, concat_axis=0, tiled=True),
        lax.all_to_all(send_grad, ("seq", "head"), split_axis=0, concat_axis=0, tiled=True),
        lax.all_to_all(send_weight, ("seq", "head"), split_axis=0, concat_axis=0, tiled=True),
    )
    normed_rows = received[0].reshape(devices * half_rows, model_width)
    grad_rows = received[1].reshape(devices * half_rows, model_width)
    prob_rows = received[2].reshape(devices * half_rows)
    partner = swapped((gate_weight[0], up_weight[0], down_weight[0]), "head", 0)
    own_terms = expert_half(
        normed_rows, grad_rows, prob_rows, gate_weight[0], up_weight[0], down_weight[0]
    )
    other_terms = expert_half(normed_rows, grad_rows, prob_rows, partner[0], partner[1], partner[2])
    returned = (
        swapped(other_terms[0].astype(jnp.bfloat16), "head", 0).astype(jnp.float32),
        swapped(other_terms[1].astype(jnp.bfloat16), "head", 0).astype(jnp.float32),
        swapped(other_terms[2].astype(jnp.bfloat16), "head", 0).astype(jnp.float32),
    )
    d_gate_weight = (own_terms[0] + returned[0]).astype(jnp.bfloat16)[None]
    d_up_weight = (own_terms[1] + returned[1]).astype(jnp.bfloat16)[None]
    d_down_weight = (own_terms[2] + returned[2]).astype(jnp.bfloat16)[None]
    row_grad = (
        (own_terms[3] + other_terms[3])
        .astype(jnp.bfloat16)
        .reshape(devices, half_rows, model_width)
    )
    prob_grad = (own_terms[4] + other_terms[4]).astype(jnp.bfloat16).reshape(devices, half_rows)
    back_rows = (
        lax.all_to_all(row_grad, ("seq", "head"), split_axis=0, concat_axis=0, tiled=True),
        lax.all_to_all(prob_grad, ("seq", "head"), split_axis=0, concat_axis=0, tiled=True),
    )
    slot_rows = back_rows[0].reshape(devices * half_rows, model_width)
    d_normed = jnp.dot(token_table, slot_rows, preferred_element_type=jnp.float32)
    d_route_weight = (
        jnp.dot(slot_onehot, back_rows[1].reshape(-1, 1), preferred_element_type=jnp.float32)
        .reshape(tok_count, top_count)
        .astype(jnp.bfloat16)
    )
    gain_scaled = norm_gain[None, :] * d_normed
    centered = jnp.mean(gain_scaled * normalized, axis=1, keepdims=True)
    d_hidden = (
        layer_grad.astype(jnp.float32) + inverse * (gain_scaled - normalized * centered)
    ).astype(jnp.bfloat16)
    d_norm_gain = lax.psum(jnp.sum(d_normed * normalized, axis=0), ("seq", "head"))
    seq_rows, inner_width = scan_input.shape
    heads_local = log_decay.shape[1]
    head_dim = inner_width // heads_local
    state_size = state_input.shape[1]
    scan_values = scan_input.astype(jnp.float32).reshape(seq_rows, heads_local, head_dim)
    input_rows = state_input.astype(jnp.float32)
    output_rows = state_output.astype(jnp.float32)
    cumulative = jnp.cumsum(log_decay, axis=0)
    total_decay = cumulative[-1]
    growth = jnp.exp(total_decay)
    lower_mask = jnp.arange(seq_rows)[:, None] >= jnp.arange(seq_rows)[None, :]
    spread = cumulative.T[:, :, None] - cumulative.T[:, None, :]
    decay_mask = jnp.where(lower_mask[None], jnp.exp(jnp.where(lower_mask[None], spread, 0.0)), 0.0)
    scores = jnp.dot(output_rows, input_rows.T, precision=highest)
    kernel = decay_mask * scores[None]
    to_end = jnp.exp(total_decay[None, :] - cumulative)
    from_start = jnp.exp(cumulative)
    local_state = jnp.einsum(
        "sn,shp->hnp", input_rows, scan_values * to_end[:, :, None], precision=highest
    )
    carried = carried_in(
        (growth, local_state),
        "seq",
        combine_forward,
        (jnp.ones_like(growth), jnp.zeros_like(local_state)),
        False,
    )
    state_in = carried[1]
    read_state = jnp.einsum("tn,hnp->thp", output_rows, state_in, precision=highest)
    y_values = (
        jnp.einsum("hts,shp->thp", kernel, scan_values, precision=highest)
        + from_start[:, :, None] * read_state
        + skip_gain[None, :, None] * scan_values
    )
    y_rounded = y_values.reshape(seq_rows, inner_width).astype(jnp.bfloat16)
    cotangent = lax.all_gather(d_hidden, "head", axis=0, tiled=True)
    grad_rounded = jnp.dot(cotangent, out_weight, preferred_element_type=jnp.float32).astype(
        jnp.bfloat16
    )
    grad_values = grad_rounded.astype(jnp.float32).reshape(seq_rows, heads_local, head_dim)
    d_out_weight = lax.psum_scatter(
        inner_rows(cotangent, y_rounded).astype(jnp.bfloat16),
        "seq",
        scatter_dimension=0,
        tiled=True,
    )
    d_skip_gain = lax.psum(jnp.sum(scan_values * grad_values, axis=(0, 2)), "seq")
    local_adjoint = jnp.einsum(
        "tn,thp->hnp", output_rows, grad_values * from_start[:, :, None], precision=highest
    )
    adjoint = carried_in(
        (growth, local_adjoint),
        "seq",
        combine_backward,
        (jnp.ones_like(growth), jnp.zeros_like(local_adjoint)),
        True,
    )[1]
    pair_grad = jnp.einsum("thp,shp->hts", grad_values, scan_values, precision=highest)
    masked_pair = decay_mask * pair_grad
    read_adjoint = jnp.einsum("sn,hnp->shp", input_rows, adjoint, precision=highest)
    d_scan = (
        jnp.einsum("hts,thp->shp", kernel, grad_values, precision=highest)
        + to_end[:, :, None] * read_adjoint
        + skip_gain[None, :, None] * grad_values
    )
    d_scan_input = d_scan.reshape(seq_rows, inner_width).astype(jnp.bfloat16)
    input_part = jnp.einsum("hts,tn->sn", masked_pair, output_rows, precision=highest) + jnp.dot(
        (scan_values * to_end[:, :, None]).reshape(seq_rows, inner_width),
        adjoint.transpose(0, 2, 1).reshape(inner_width, state_size),
        precision=highest,
    )
    output_part = jnp.einsum("hts,sn->tn", masked_pair, input_rows, precision=highest) + jnp.dot(
        (grad_values * from_start[:, :, None]).reshape(seq_rows, inner_width),
        state_in.transpose(0, 2, 1).reshape(inner_width, state_size),
        precision=highest,
    )
    shared = (
        lax.psum(input_part.astype(jnp.bfloat16), "head").astype(jnp.float32),
        lax.psum(output_part.astype(jnp.bfloat16), "head").astype(jnp.float32),
    )
    pair_full = kernel * pair_grad
    row_sums = jnp.sum(pair_full, axis=2).T
    column_sums = jnp.sum(pair_full, axis=1).T
    from_past = from_start * jnp.sum(read_state * grad_values, axis=2)
    to_future = to_end * jnp.sum(read_adjoint * scan_values, axis=2)
    corner = growth * jnp.sum(state_in * adjoint, axis=(1, 2))
    forward_part = row_sums - column_sums + from_past
    reverse_sum = jnp.flip(jnp.cumsum(jnp.flip(forward_part, 0), axis=0), 0)
    d_log_decay = reverse_sum + jnp.cumsum(to_future, axis=0) - to_future + corner[None, :]
    return (
        d_hidden,
        d_norm_gain,
        d_route_weight,
        d_gate_weight,
        d_up_weight,
        d_down_weight,
        d_out_weight,
        d_scan_input,
        shared[0],
        shared[1],
        d_log_decay,
        d_skip_gain,
    )


def solution(mesh):
    in_specs = (
        P(("seq", "head"), None),
        P(),
        P(("seq", "head"), None),
        P(("seq", "head"), None),
        P(("seq", "head"), None, None),
        P(("seq", "head"), None, None),
        P(("seq", "head"), None, None),
        P(("seq", "head"), None),
        P("seq", "head"),
        P("seq", None),
        P("seq", None),
        P("seq", "head"),
        P("head"),
        P(None, "head"),
    )
    out_specs = (
        P(("seq", "head"), None),
        P(),
        P(("seq", "head"), None),
        P(("seq", "head"), None, None),
        P(("seq", "head"), None, None),
        P(("seq", "head"), None, None),
        P("seq", "head"),
        P("seq", "head"),
        P("seq", None),
        P("seq", None),
        P("seq", "head"),
        P("head"),
    )
    return jax.shard_map(shards, mesh=mesh, in_specs=in_specs, out_specs=out_specs, check_vma=False)
```

profile of v0, /device:TPU:8, one launch (start us, length us, event | category | flops | bytes accessed | tf_op | source)
XLA Modules:
  0.0 798.0 jit_solution(10801294782229076773)
XLA Ops:
  9.3 4.5 reduce-window.26
  15.9 6.0 all-to-all-start
  22.8 1.4 convert_reduce_fusion
  24.2 3.6 convolution_convert_fusion
  27.9 7.3 reshape.287
  35.1 5.9 all-to-all-start.2
  41.0 4.6 convolution_convert_fusion.1
  45.6 7.2 reshape.285
  52.8 101.8 %all-to-all-done.2 = bf16[32,36,2048]{2,1,0:T(8,128)(2,1)} async-done(((bf16[32,36,2048]{2,1,0:T(8,128)(2,1)}), bf16[32,36,2048]{2,1,0:T(8,128)(2,1)}, u32[]{:S(2)}, u32[]{:S(2)}) %all-to-all-start.2) | async-done | bytes 4718624 | tf_op jit(solution)/shard_map/all_to_all | solution.py:132
  154.6 8.8 %all-to-all-start.1 = ((bf16[32,36,2048]{2,1,0:T(8,128)(2,1)}), bf16[32,36,2048]{2,1,0:T(8,128)(2,1)}, u32[]{:S(2)}, u32[]{:S(2)}) async-start(bf16[32,36,2048]{2,1,0:T(8,128)(2,1)} %reshape.285), calls=%async_computation.1 | async-start | bytes 10485760 | tf_op jit(solution)/shard_map/all_to_all | solution.py:133
  164.5 7.2 reshape.288
  171.7 6.5 fusion.100
  178.3 3.6 fusion.103
  181.9 5.0 fusion.116
  186.9 90.0 %all-to-all-done.1 = bf16[32,36,2048]{2,1,0:T(8,128)(2,1)} async-done(((bf16[32,36,2048]{2,1,0:T(8,128)(2,1)}), bf16[32,36,2048]{2,1,0:T(8,128)(2,1)}, u32[]{:S(2)}, u32[]{:S(2)}) %all-to-all-start.1) | async-done | bytes 4718624 | tf_op jit(solution)/shard_map/all_to_all | solution.py:133
  276.9 7.6 reshape.286
  284.6 8.3 %multiply_reduce_fusion.2 = (f32[1152]{0:T(1024)}, bf16[1152,384]{0,1:T(8,128)(2,1)}, bf16[1152,384]{0,1:T(8,128)(2,1)S(1)}, bf16[1152,384]{0,1:T(8,128)(2,1)S(1)}) fusion(f32[1152,384]{0,1:T(8,128)} %fusion.103, f32[1152,384]{0,1:T(8,128)} %fusion.100, f32[1152]{0:T(1024)S(1)} %reshape.302, bf16[1152,2048]{1,0:T(8,128)(2,1)} %reshape.286, ...), kind=kOutput, calls=%fused_computation.50 | convolution fusion | flops 1820785536 | bytes 12493824 | tf_op jit(solution)/shard_map/dot_general | solution.py:39
  292.9 2.7 fusion.98
  295.6 6.5 fusion.115
  302.1 2.7 convolution_add_fusion.1
  304.9 6.6 multiply_reduce_fusion.1
  311.6 8.4 %fusion.117 = f32[1152,2048]{1,0:T(8,128)} fusion(bf16[1152,384]{0,1:T(8,128)(2,1)S(1)} %get-tuple-element.318, bf16[2048,384]{1,0:T(8,128)(2,1)} %collective-permute-done.1), kind=kOutput, calls=%fused_computation.177 | convolution fusion | flops 1811939328 | bytes 11894784 | tf_op jit(solution)/shard_map/dot_general | solution.py:39
  319.9 9.5 %add_convert_fusion = bf16[1152,2048]{1,0:T(8,128)(2,1)} fusion(f32[1152,2048]{1,0:T(8,128)S(1)} %convolution_add_fusion.1, f32[1152,2048]{1,0:T(8,128)} %fusion.117, bf16[1152,384]{0,1:T(8,128)(2,1)S(1)} %get-tuple-element.315, bf16[2048,384]{1,0:T(8,128)(2,1)} %collective-permute-done.2), kind=kOutput, calls=%fused_computation.9 | convolution fusion | flops 1819017216 | bytes 26050560 | tf_op jit(solution)/shard_map/dot_general | solution.py:39
  329.4 7.2 reshape.289
  336.6 123.9 %all_to_all.31 = bf16[32,36,2048]{2,1,0:T(8,128)(2,1)} all-to-all(bf16[32,36,2048]{2,1,0:T(8,128)(2,1)} %reshape.289), channel_id=1, replica_groups=mesh['seq'=8,'head'=4] {'seq','head'}, dimensions={0} | all-to-all | bytes 9437184 | tf_op jit(solution)/shard_map/all_to_all | solution.py:159
  460.5 7.2 reshape.290
  467.8 4.1 fusion.65
  471.9 1.2 fusion.64
  475.6 20.1 %all-gather.7.cloned.1.call-done = bf16[512,2048]{1,0:T(8,128)(2,1)} async-done(((bf16[128,2048]{1,0:T(8,128)(2,1)}), bf16[512,2048]{1,0:T(8,128)(2,1)}) %all-gather.7.cloned.1.call-update) | async-done | bytes 2097168 | tf_op jit(solution)/shard_map/all_gather | solution.py:210
  495.7 3.7 fusion.114
  500.4 1.3 convolution_bitcast_fusion.2
  503.1 17.7 %all-gather.2 = f32[8,1,8]{2,1,0:T(1,128)} all-gather(f32[1,1,8]{2,1,0:T(1,128)S(1)} %bitcast.227), channel_id=1, replica_groups=mesh['seq'=8,'head'=4] {'seq'}, dimensions={0}, use_global_device_ids=true | all-gather | bytes 288 | tf_op jit(solution)/shard_map/all_gather | solution.py:20
  521.4 29.8 %all-gather.11.cloned.1.call-done = f32[64,128,64]{1,2,0:T(8,128)} async-done(((f32[8,128,64]{1,2,0:T(8,128)}), f32[64,128,64]{1,2,0:T(8,128)}) %all-gather.11.cloned.1.call-update) | async-done | bytes 2097168 | tf_op jit(solution)/shard_map/all_gather | solution.py:20
  551.3 16.0 %while.27 = (s32[]{:T(128)}, f32[8,128,64]{2,1,0:T(8,128)S(1)}, s32[]{:T(128)}, f32[8,8,128,64]{2,3,1,0:T(8,128)}, f32[8,8]{1,0:T(8,128)}, /*index=5*/s32[]{:T(128)}, s32[]{:T(128)}, s32[]{:T(128)}, s32[]{:T(128)}) while((s32[]{:T(128)}, f32[8,128,64]{2,1,0:T(8,128)S(1)}, s32[]{:T(128)}, f32[8,8,128,64]{2,3,1,0:T(8,128)}, ...), condition=%wide.region_16.17_spmd, body=%wide.region_15.16_spmd.sunk | while | flops 131078 | bytes 1835259 | solution.py:29
  551.3 1.2 dynamic-slice_bitcast_fusion.5
  554.5 1.2 dynamic-slice_bitcast_fusion.5
  567.3 3.1 multiply_reduce_fusion.4
  571.5 1.3 convolution_bitcast_fusion.3
  573.5 7.0 convolution_convert_fusion.4
  580.5 6.4 convolution_convert_fusion.5
  587.4 3.6 convolution_convert_fusion.3
  591.1 3.4 convolution_bitcast_fusion.5
  595.3 5.9 fusion.6
  602.2 1.7 fusion.56
  603.9 22.0 %all-gather.9.cloned.1.call-done = f32[64,128,64]{1,2,0:T(8,128)} async-done(((f32[8,128,64]{1,2,0:T(8,128)}), f32[64,128,64]{1,2,0:T(8,128)}) %all-gather.9.cloned.1.call-update) | async-done | bytes 2097168 | tf_op jit(solution)/shard_map/all_gather | solution.py:20
  626.8 8.7 %while.26 = (s32[]{:T(128)}, f32[8,128,64]{2,1,0:T(8,128)}, s32[]{:T(128)}, f32[8,8]{1,0:T(8,128)}, f32[8,8,128,64]{2,3,1,0:T(8,128)}, /*index=5*/s32[]{:T(128)}, s32[]{:T(128)}, s32[]{:T(128)}) while((s32[]{:T(128)}, f32[8,128,64]{2,1,0:T(8,128)}, s32[]{:T(128)}, f32[8,8]{1,0:T(8,128)}, f32[8,8,128,64]{2,3,1,0:T(8,128)}, ...), condition=%wide.region_13.14_spmd, body=%wide.region_12.13_spmd.sunk | while | flops 131077 | bytes 1835239 | solution.py:29
  629.2 2.0 bitcast_add_fusion.6
  633.5 2.0 bitcast_add_fusion.6
  635.6 4.9 convolution_bitcast_fusion.4
  640.6 2.6 multiply_reduce_fusion.5
  643.2 7.4 fusion.50
  650.6 1.3 fusion.57
  651.9 4.3 convolution_convert_fusion.2
  657.1 31.2 %all_to_all.32 = bf16[32,1,36]{2,1,0:T(2,128)(2,1)S(1)} all-to-all(bf16[32,1,36]{2,1,0:T(2,128)(2,1)S(1)} %convert_element_type.213), channel_id=1, replica_groups=mesh['seq'=8,'head'=4] {'seq','head'}, dimensions={0} | all-to-all | bytes 4608 | tf_op jit(solution)/shard_map/all_to_all | solution.py:160
  688.5 5.9 fusion.10
  695.1 7.2 fusion.27
  702.3 6.9 fusion.26
  709.3 5.0 fusion.25
  714.7 40.0 %psum.28 = f32[2048]{0:T(1024)} all-reduce(f32[2048]{0:T(1024)S(1)} %copy-done.48), channel_id=1, replica_groups=mesh['seq'=8,'head'=4] {'seq','head'}, use_global_device_ids=true, to_apply=%region_7.8 | all-reduce | flops 2048 | bytes 16384 | tf_op jit(solution)/shard_map/psum | solution.py:174
  754.7 18.3 %psum.31 = f32[8]{0:T(128)} all-reduce(f32[8]{0:T(128)S(1)} %reduce_sum.158), channel_id=1, replica_groups=mesh['seq'=8,'head'=4] {'seq'}, use_global_device_ids=true, to_apply=%region_31.32 | all-reduce | flops 8 | bytes 64 | tf_op jit(solution)/shard_map/psum | solution.py:221
  773.0 8.4 %fusion.53 = bf16[512,8,64]{0,2,1:T(8,128)(2,1)} fusion(bf16[512,8,64]{0,2,1:T(8,128)(2,1)} %bitcast.218, f32[512,512]{1,0:T(8,128)} %copy-done.25, f32[8,512]{1,0:T(8,128)S(1)} %copy-done.57, pred[512,512]{1,0:T(8,128)(4,1)S(1)} %copy-done.36, f32[512,8,64]{0,2,1:T(8,128)} %bitcast.202, f32[512,8,64]{0,2,1:T(8,128)} %get-tuple-element.324, ...), kind=kOutput, calls=%fused_computation.75 | convolution fusion | flops 1620312064 | bytes 4489248 | tf_op jit(solution)/shard_map/hts,thp->shp/dot_general | solution.py:236
  781.4 2.1 copy.144
  788.0 1.6 convert_element_type.209
  789.6 1.6 convert_element_type.211
  (272 shorter events, 41.1 us)
Async XLA Ops:
  7.2 488.6 %copy-start = (bf16[2048,512]{1,0:T(8,128)(2,1)S(1)}, bf16[2048,512]{1,0:T(8,128)(2,1)}, u32[]{:S(2)}) copy-start(bf16[2048,512]{1,0:T(8,128)(2,1)} %param.31) | copy-start | bytes 6291460
  7.2 15.5 %copy-start.53 = (s32[128,8]{0,1:T(8,128)S(1)}, s32[128,8]{0,1:T(8,128)}, u32[]{:S(2)}) copy-start(s32[128,8]{0,1:T(8,128)} %param.20) | copy-start | bytes 12292
  7.2 14.7 %copy-start.7 = (bf16[128,2048]{1,0:T(8,128)(2,1)S(1)}, bf16[128,2048]{1,0:T(8,128)(2,1)}, u32[]{:S(2)}) copy-start(bf16[128,2048]{1,0:T(8,128)(2,1)} %param.18) | copy-start | bytes 1572868
  7.2 17.0 %copy-start.45 = (f32[2048]{0:T(1024)S(1)}, f32[2048]{0:T(1024)}, u32[]{:S(2)}) copy-start(f32[2048]{0:T(1024)} %param.19) | copy-start | bytes 24580
  15.9 19.2 %all-to-all-start = ((bf16[32,1,36]{2,1,0:T(2,128)(2,1)}), bf16[32,1,36]{2,1,0:T(2,128)(2,1)S(1)}, u32[]{:S(2)}, u32[]{:S(2)}) async-start(bf16[32,1,36]{2,1,0:T(2,128)(2,1)} %all_to_all.25), calls=%async_computation | async-start | bytes 32768 | tf_op jit(solution)/shard_map/all_to_all | solution.py:134
  35.1 119.5 %all-to-all-start.2 = ((bf16[32,36,2048]{2,1,0:T(8,128)(2,1)}), bf16[32,36,2048]{2,1,0:T(8,128)(2,1)}, u32[]{:S(2)}, u32[]{:S(2)}) async-start(bf16[32,36,2048]{2,1,0:T(8,128)(2,1)} %reshape.287), calls=%async_computation.2 | async-start | bytes 10485760 | tf_op jit(solution)/shard_map/all_to_all | solution.py:132
  154.6 122.3 %all-to-all-start.1 = ((bf16[32,36,2048]{2,1,0:T(8,128)(2,1)}), bf16[32,36,2048]{2,1,0:T(8,128)(2,1)}, u32[]{:S(2)}, u32[]{:S(2)}) async-start(bf16[32,36,2048]{2,1,0:T(8,128)(2,1)} %reshape.285), calls=%async_computation.1 | async-start | bytes 10485760 | tf_op jit(solution)/shard_map/all_to_all | solution.py:133
  163.4 332.4 %all-gather.7.cloned.1.call-start = ((), (), s32[]{:S(2)}) async-start(), calls=%async_computation.6 | async-start | bytes 2621440 | tf_op jit(solution)/shard_map/all_gather | solution.py:210
  163.6 18.3 %collective-permute-start.2 = (bf16[2048,384]{1,0:T(8,128)(2,1)}, bf16[2048,384]{1,0:T(8,128)(2,1)}, u32[]{:S(2)}, u32[]{:S(2)}) collective-permute-start(bf16[2048,384]{1,0:T(8,128)(2,1)} %bitcast.215), channel_id=1, source_target_pairs={{0,1},{1,0},{2,3},{3,2},{4,5},{5,4},{6,7},{7,6},{8,9},{9,8},{10,11... | collective-permute-start | bytes 4718600 | tf_op jit(solution)/shard_map/ppermute | solution.py:13
  163.8 131.8 %collective-permute-start.1 = (bf16[2048,384]{1,0:T(8,128)(2,1)}, bf16[2048,384]{1,0:T(8,128)(2,1)}, u32[]{:S(2)}, u32[]{:S(2)}) collective-permute-start(bf16[2048,384]{1,0:T(8,128)(2,1)} %bitcast.214), channel_id=1, source_target_pairs={{0,1},{1,0},{2,3},{3,2},{4,5},{5,4},{6,7},{7,6},{8,9},{9,8},{10,11... | collective-permute-start | bytes 4718600 | tf_op jit(solution)/shard_map/ppermute | solution.py:13
  164.2 140.7 %collective-permute-start = (bf16[384,2048]{1,0:T(8,128)(2,1)}, bf16[384,2048]{1,0:T(8,128)(2,1)}, u32[]{:S(2)}, u32[]{:S(2)}) collective-permute-start(bf16[384,2048]{1,0:T(8,128)(2,1)} %bitcast.228), channel_id=1, source_target_pairs={{0,1},{1,0},{2,3},{3,2},{4,5},{5,4},{6,7},{7,6},{8,9},{9,8},{10,11... | collective-permute-start | bytes 4718600 | tf_op jit(solution)/shard_map/ppermute | solution.py:13
  164.5 140.4 %copy-start.61 = (f32[1152]{0:T(1024)}, f32[1152]{0:T(1024)S(1)}, u32[]{:S(2)}) copy-start(f32[1152]{0:T(1024)S(1)} %reshape.302) | copy-start | bytes 13828
  171.7 6.5 copy-start.11
  171.7 6.5 copy-start.19
  284.6 8.3 %copy-start.21 = (bf16[1,2048,384]{2,1,0:T(8,128)(2,1)S(1)}, bf16[1,2048,384]{2,1,0:T(8,128)(2,1)}, u32[]{:S(2)}) copy-start(bf16[1,2048,384]{2,1,0:T(8,128)(2,1)} %param.22) | copy-start | bytes 4718596
  292.9 9.2 %copy-start.14 = (bf16[1152,384]{0,1:T(8,128)(2,1)}, bf16[1152,384]{0,1:T(8,128)(2,1)S(1)}, u32[]{:S(2)}) copy-start(bf16[1152,384]{0,1:T(8,128)(2,1)S(1)} %get-tuple-element.317) | copy-start | bytes 2654212
  295.6 6.5 copy-start.20
  295.6 9.3 %slice-start = ((s8[4718592]{0:T(1024)(128)(4,1)}), s8[4194304]{0:T(1024)(128)(4,1)S(1)}, s32[]{:S(2)}) async-start(s8[4718592]{0:T(1024)(128)(4,1)} %bitcast.208), calls=%async_computation.11 | async-start | bytes 8388608
  311.5 8.4 %copy-start.24 = (bf16[1152,384]{0,1:T(8,128)(2,1)}, bf16[1152,384]{0,1:T(8,128)(2,1)S(1)}, u32[]{:S(2)}) copy-start(bf16[1152,384]{0,1:T(8,128)(2,1)S(1)} %get-tuple-element.318) | copy-start | bytes 2654212
  311.6 8.4 %copy-start.27 = (bf16[1152,384]{0,1:T(8,128)(2,1)}, bf16[1152,384]{0,1:T(8,128)(2,1)S(1)}, u32[]{:S(2)}) copy-start(bf16[1152,384]{0,1:T(8,128)(2,1)S(1)} %get-tuple-element.315) | copy-start | bytes 2654212
  473.1 78.1 %all-gather.11.cloned.1.call-start = ((), (), s32[]{:S(2)}) async-start(), calls=%async_computation.9 | async-start | bytes 2359296 | tf_op jit(solution)/shard_map/all_gather | solution.py:20
  475.6 23.9 %copy-start.39 = (f32[512,8]{0,1:T(8,128)}, f32[512,8]{0,1:T(8,128)S(1)}, u32[]{:S(2)}) copy-start(f32[512,8]{0,1:T(8,128)S(1)} %get-tuple-element.307) | copy-start | bytes 49156
  475.6 24.9 %copy-start.17 = (bf16[512,128]{1,0:T(8,128)(2,1)S(1)}, bf16[512,128]{1,0:T(8,128)(2,1)}, u32[]{:S(2)}) copy-start(bf16[512,128]{1,0:T(8,128)(2,1)} %param.28) | copy-start | bytes 393220
  501.8 124.1 %all-gather.9.cloned.1.call-start = ((), (), s32[]{:S(2)}) async-start(), calls=%async_computation.8 | async-start | bytes 2359296 | tf_op jit(solution)/shard_map/all_gather | solution.py:20
  503.1 17.7 %copy-start.58 = (f32[8]{0:T(128)}, f32[8]{0:T(128)S(1)}, u32[]{:S(2)}) copy-start(f32[8]{0:T(128)S(1)} %get-tuple-element.279) | copy-start | bytes 100
  551.3 16.0 %copy-start.16 = (bf16[512,128]{1,0:T(8,128)(2,1)S(1)}, bf16[512,128]{1,0:T(8,128)(2,1)}, u32[]{:S(2)}) copy-start(bf16[512,128]{1,0:T(8,128)(2,1)} %param.27) | copy-start | bytes 393220
  570.5 24.1 %copy-start.43 = (f32[512,8]{0,1:T(8,128)}, f32[512,8]{0,1:T(8,128)S(1)}, u32[]{:S(2)}) copy-start(f32[512,8]{0,1:T(8,128)S(1)} %get-tuple-element.305) | copy-start | bytes 49156
  572.8 215.1 %all-reduce.3.cloned.1.call-start = ((), (), s32[]{:S(2)}) async-start(), calls=%async_computation.10 | async-start | bytes 524288 | tf_op jit(solution)/shard_map/psum | solution.py:252
  573.2 22.1 %copy-start.34 = (pred[512,512]{1,0:T(8,128)(4,1)}, pred[512,512]{1,0:T(8,128)(4,1)S(1)}, u32[]{:S(2)}) copy-start(pred[512,512]{1,0:T(8,128)(4,1)S(1)} %iota_compare_fusion.6) | copy-start | bytes 786436
  573.5 21.8 %copy-start.25 = (f32[512,512]{1,0:T(8,128)}, f32[512,512]{1,0:T(8,128)S(1)}, u32[]{:S(2)}) copy-start(f32[512,512]{1,0:T(8,128)S(1)} %fusion.118) | copy-start | bytes 3145732
  573.5 7.0 copy-start.28
  573.5 13.8 %slice-start.2 = ((s8[4718592]{0:T(1024)(128)(4,1)}), s8[4194304]{0:T(1024)(128)(4,1)S(1)}, s32[]{:S(2)}) async-start(s8[4718592]{0:T(1024)(128)(4,1)} %bitcast.210), calls=%async_computation.13 | async-start | bytes 8388608
  580.5 6.8 slice-start.3
  580.5 6.8 copy-start.62
  580.5 6.8 copy-start.69
  580.5 114.6 %collective-permute-start.4 = (bf16[2048,384]{1,0:T(8,128)(2,1)}, bf16[2048,384]{1,0:T(8,128)(2,1)}, u32[]{:S(2)}, u32[]{:S(2)}) collective-permute-start(bf16[2048,384]{1,0:T(8,128)(2,1)} %convolution_convert_fusion.4), channel_id=1, source_target_pairs={{0,1},{1,0},{2,3},{3,2},{4,5},{5,4},{6,7},{7,6},{8,9},{9,8},{10,11... | collective-permute-start | bytes 4718600 | tf_op jit(solution)/shard_map/ppermute | solution.py:13
  586.9 115.4 %collective-permute-start.3 = (bf16[2048,384]{1,0:T(8,128)(2,1)}, bf16[2048,384]{1,0:T(8,128)(2,1)}, u32[]{:S(2)}, u32[]{:S(2)}) collective-permute-start(bf16[2048,384]{1,0:T(8,128)(2,1)} %convolution_convert_fusion.5), channel_id=1, source_target_pairs={{0,1},{1,0},{2,3},{3,2},{4,5},{5,4},{6,7},{7,6},{8,9},{9,8},{10,11... | collective-permute-start | bytes 4718600 | tf_op jit(solution)/shard_map/ppermute | solution.py:13
  587.4 7.2 copy-start.38
  587.4 7.2 copy-start.50
  587.4 7.2 copy-start.59
  587.4 7.9 copy-start.8
  587.4 7.9 copy-start.30
  591.0 118.2 %collective-permute-start.5 = (bf16[384,2048]{1,0:T(8,128)(2,1)}, bf16[384,2048]{1,0:T(8,128)(2,1)}, u32[]{:S(2)}, u32[]{:S(2)}) collective-permute-start(bf16[384,2048]{1,0:T(8,128)(2,1)} %convolution_convert_fusion.3), channel_id=1, source_target_pairs={{0,1},{1,0},{2,3},{3,2},{4,5},{5,4},{6,7},{7,6},{8,9},{9,8},{10,11... | collective-permute-start | bytes 4718600 | tf_op jit(solution)/shard_map/ppermute | solution.py:13
  595.3 5.9 copy-start.55
  635.6 7.6 copy-start.6
  635.6 7.6 copy-start.9
  635.6 7.6 copy-start.26
  635.6 7.6 copy-start.35
  635.6 7.6 copy-start.40
  635.6 7.6 copy-start.56
  635.6 7.6 copy-start.66
  643.2 7.4 copy-start.13
  651.9 139.3 %reduce-scatter.2.cloned.1.call-start = ((), (), s32[]{:S(2)}) async-start(), calls=%async_computation.7 | async-start | bytes 2359296 | tf_op jit(solution)/shard_map/reduce_scatter | solution.py:215
  656.3 32.2 %copy-start.33 = (s32[128,8]{1,0:T(8,128)S(1)}, s32[128,8]{1,0:T(8,128)}, u32[]{:S(2)}) copy-start(s32[128,8]{1,0:T(8,128)} %copy-done.32) | copy-start | bytes 12292
  695.1 7.2 copy-start.23
  695.1 14.1 %slice-start.4 = ((s8[4718592]{0:T(1024)(128)(4,1)}), s8[4194304]{0:T(1024)(128)(4,1)S(1)}, s32[]{:S(2)}) async-start(s8[4718592]{0:T(1024)(128)(4,1)} %bitcast.212), calls=%async_computation.15 | async-start | bytes 8388608
  702.3 6.9 slice-start.5
  702.3 6.9 copy-start.63
  702.3 6.9 copy-start.68
  709.3 63.6 %copy-start.36 = (pred[512,512]{1,0:T(8,128)(4,1)S(1)}, pred[512,512]{1,0:T(8,128)(4,1)}, u32[]{:S(2)}) copy-start(pred[512,512]{1,0:T(8,128)(4,1)} %copy-done.34) | copy-start | bytes 786436
  709.3 63.6 %copy-start.42 = (f32[512,8]{0,1:T(8,128)S(1)}, f32[512,8]{0,1:T(8,128)}, u32[]{:S(2)}) copy-start(f32[512,8]{0,1:T(8,128)} %subtract_exponential_fusion) | copy-start | bytes 49156
  709.3 63.6 %copy-start.57 = (f32[8,512]{1,0:T(8,128)S(1)}, f32[8,512]{1,0:T(8,128)}, u32[]{:S(2)}) copy-start(f32[8,512]{1,0:T(8,128)} %copy-done.55) | copy-start | bytes 49156
  709.3 63.6 %copy-start.67 = (f32[8]{0:T(128)S(1)}, f32[8]{0:T(128)}, u32[]{:S(2)}) copy-start(f32[8]{0:T(128)} %param.30) | copy-start | bytes 100
  772.9 10.5 %copy-start.47 = (f32[8,4,128]{2,0,1:T(8,128)S(1)}, f32[8,4,128]{2,0,1:T(8,128)}, u32[]{:S(2)}) copy-start(f32[8,4,128]{2,0,1:T(8,128)} %get-tuple-element.303) | copy-start | bytes 49156
  (27 other events, 88.8 us)
Sparse Core Ops, SparseCore 0:
  473.2 22.4 all-gather.6
  501.9 49.2 all-gather.10
  572.9 52.9 all-gather.8
  652.0 52.5 all-reduce.2
  708.9 67.3 reduce-scatter.1
where the time goes:
time: 810 us; the launch traced here: 798 us
  waiting for transfers between devices  264 us (33%)
  blocking collectives  231 us (29%)
  matrix products  165 us (20%)
  local copies, waits for them, and re-layouts  75.2 us (9%)
  other arithmetic  25.4 us (3%)
  starting transfers between devices  22.5 us (3%)
  between operations  14.9 us (2%)
    all_to_all x1, blocking collectives, shards(): lax.all_to_all(row_grad, ('seq', 'head'), split_axis=0, concat_axis=0, ti...  124 us
    all_to_all x1, waiting for transfers between devices, shards(): lax.all_to_all(send_normed, ('seq', 'head'), split_axis=0, concat_axis=0,...  102 us
    all_to_all x1, waiting for transfers between devices, shards(): lax.all_to_all(send_grad, ('seq', 'head'), split_axis=0, concat_axis=0, t...  90 us
    all_gather x2, waiting for transfers between devices, carried_in(): gathered = jax.tree.map(lambda a: lax.all_gather(a, axis), part)  51.8 us
    dot_general x10, matrix products, inner_rows(): lax.dot_general(left_side, right_side, (((0,), (0,)), ((), ())), preferre...  49.4 us
    psum x1, blocking collectives, shards(): lax.psum(jnp.sum(d_normed * normalized, axis=0), ('seq', 'head'))  40 us
    dot_general x6, matrix products, inner_columns(): lax.dot_general(left_side, right_side, (((1,), (1,)), ((), ())), preferre...  38.2 us
    all_to_all x1, blocking collectives, shards(): lax.all_to_all(prob_grad, ('seq', 'head'), split_axis=0, concat_axis=0, t...  31.2 us
  transfers between devices with their start and end apart: 14, of which 5 were waited for; matrix products, arithmetic and copies ran while one was open for 23% of the time, Pallas kernels for 0%

commit v1 on v0

v1 whole, which is shorter than its diff:
```python
import functools

import jax
import jax.numpy as jnp
from jax import lax
from jax.experimental import pallas as pl
from jax.experimental.pallas import tpu as pltpu
from jax.sharding import PartitionSpec as P

highest = lax.Precision.HIGHEST
epsilon = 1e-06
wide = jnp.float32
short = jnp.bfloat16
both = ("seq", "head")
parts_count = 2


def log2(number):
    return number.bit_length() - 1


def flipped(value, axis, mask):
    names = axis if isinstance(axis, tuple) else (axis,)
    size = 1
    for name in names:
        size = size * lax.axis_size(name)
    return lax.ppermute(value, axis, [(i, i ^ mask) for i in range(size)])


def shifted(value, axis, distance):
    size = lax.axis_size(axis)
    pairs = [(i, i + distance) for i in range(size) if 0 <= i + distance < size]
    return lax.ppermute(value, axis, pairs)


def summed(value, axis):
    size = lax.axis_size(axis)
    for bit in range(log2(size)):
        value = value + flipped(value, axis, 1 << bit)
    return value


def dot_nn(a, b, out=wide):
    return lax.dot_general(a, b, (((1,), (0,)), ((), ())), preferred_element_type=out)


def dot_nt(a, b, out=wide):
    return lax.dot_general(a, b, (((1,), (1,)), ((), ())), preferred_element_type=out)


def dot_tn(a, b, out=wide):
    return lax.dot_general(a, b, (((0,), (0,)), ((), ())), preferred_element_type=out)


def forward_kernel(heads, b_ref, c_ref, x_ref, row_ref, col_ref, y_ref, score_ref):
    step = pl.program_id(0)
    rows = b_ref.shape[0]

    @pl.when(step == 0)
    def _():
        score_ref[...] = dot_nt(c_ref[...], b_ref[...])

    scores = score_ref[...]
    keep = lax.broadcasted_iota(jnp.int32, (rows, rows), 0) >= lax.broadcasted_iota(
        jnp.int32, (rows, rows), 1
    )
    block = x_ref[...]
    width = block.shape[1]
    lane = lax.broadcasted_iota(jnp.int32, (rows, width), 1)
    head_lane = lax.broadcasted_iota(jnp.int32, col_ref.shape, 1)
    total = jnp.zeros((rows, width), wide)
    for k in range(heads):
        head = step * heads + k
        column = jnp.sum(jnp.where(head_lane == head, col_ref[...], 0.0), axis=1, keepdims=True)
        line = row_ref[pl.ds(head, 1), :]
        decay = jnp.where(keep, jnp.exp(jnp.minimum(column - line, 0.0)), 0.0)
        mine = (lane // (width // heads)) == k
        total = total + dot_nn(
            (decay * scores).astype(short), jnp.where(mine, block, jnp.zeros_like(block))
        )
    y_ref[...] = total


def backward_kernel(
    heads, b_ref, c_ref, x_ref, g_ref, row_ref, col_ref,
    dx_ref, tsum_ref, ssum_ref, db_ref, dc_ref, score_ref, mask_ref,
):
    step = pl.program_id(0)
    rows = b_ref.shape[0]

    @pl.when(step == 0)
    def _():
        score_ref[...] = dot_nt(b_ref[...], c_ref[...])
        mask_ref[...] = jnp.zeros_like(mask_ref)
        ssum_ref[...] = jnp.zeros_like(ssum_ref)

    scores = score_ref[...]
    keep = lax.broadcasted_iota(jnp.int32, (rows, rows), 0) <= lax.broadcasted_iota(
        jnp.int32, (rows, rows), 1
    )
    values = x_ref[...]
    grads = g_ref[...]
    width = values.shape[1]
    lane = lax.broadcasted_iota(jnp.int32, (rows, width), 1)
    head_lane = lax.broadcasted_iota(jnp.int32, col_ref.shape, 1)
    total = jnp.zeros((rows, width), wide)
    for k in range(heads):
        head = step * heads + k
        column = jnp.sum(jnp.where(head_lane == head, col_ref[...], 0.0), axis=1, keepdims=True)
        line = row_ref[pl.ds(head, 1), :]
        decay = jnp.where(keep, jnp.exp(jnp.minimum(line - column, 0.0)), 0.0)
        mine = (lane // (width // heads)) == k
        head_grads = jnp.where(mine, grads, jnp.zeros_like(grads))
        pair = decay * dot_nt(values, head_grads)
        mask_ref[...] += pair
        full = pair * scores
        tsum_ref[pl.ds(head, 1), :] = jnp.sum(full, axis=0, keepdims=True)
        ssum_ref[...] += jnp.where(head_lane == head, jnp.sum(full, axis=1, keepdims=True), 0.0)
        total = total + dot_nn((decay * scores).astype(short), head_grads)
    dx_ref[...] = total

    @pl.when(step == pl.num_programs(0) - 1)
    def _():
        mask = mask_ref[...].astype(short)
        db_ref[...] = dot_nn(mask, c_ref[...])
        dc_ref[...] = dot_tn(mask, b_ref[...])


def scan_blocks(rows, state, width, heads_local):
    whole = pl.BlockSpec((rows, state), lambda i: (0, 0))
    column = pl.BlockSpec((rows, width), lambda i: (0, i))
    lines = pl.BlockSpec((heads_local, rows), lambda i: (0, 0))
    columns = pl.BlockSpec((rows, heads_local), lambda i: (0, 0))
    return whole, column, lines, columns


def scan_forward(b, c, x, lines, columns):
    rows, state = b.shape
    inner = x.shape[1]
    heads_local = columns.shape[1]
    width = 2 * (inner // heads_local)
    whole, column, line_spec, column_spec = scan_blocks(rows, state, width, heads_local)
    return pl.pallas_call(
        functools.partial(forward_kernel, 2),
        grid=(heads_local // 2,),
        in_specs=[whole, whole, column, line_spec, column_spec],
        out_specs=column,
        out_shape=jax.ShapeDtypeStruct((rows, inner), wide),
        scratch_shapes=[pltpu.VMEM((rows, rows), wide)],
        compiler_params=pltpu.CompilerParams(vmem_limit_bytes=24 * 1024 * 1024),
        cost_estimate=pl.CostEstimate(
            flops=4 * rows * rows * 128 * heads_local,
            bytes_accessed=rows * inner * 6 + rows * state * 4,
            transcendentals=rows * rows * heads_local,
        ),
    )(b, c, x, lines, columns)


def scan_backward(b, c, x, g, lines, columns):
    rows, state = b.shape
    inner = x.shape[1]
    heads_local = columns.shape[1]
    width = 2 * (inner // heads_local)
    whole, column, line_spec, column_spec = scan_blocks(rows, state, width, heads_local)
    return pl.pallas_call(
        functools.partial(backward_kernel, 2),
        grid=(heads_local // 2,),
        in_specs=[whole, whole, column, column, line_spec, column_spec],
        out_specs=[column, line_spec, column_spec, whole, whole],
        out_shape=[
            jax.ShapeDtypeStruct((rows, inner), wide),
            jax.ShapeDtypeStruct((heads_local, rows), wide),
            jax.ShapeDtypeStruct((rows, heads_local), wide),
            jax.ShapeDtypeStruct((rows, state), wide),
            jax.ShapeDtypeStruct((rows, state), wide),
        ],
        scratch_shapes=[pltpu.VMEM((rows, rows), wide), pltpu.VMEM((rows, rows), wide)],
        compiler_params=pltpu.CompilerParams(vmem_limit_bytes=32 * 1024 * 1024),
        cost_estimate=pl.CostEstimate(
            flops=8 * rows * rows * 128 * heads_local,
            bytes_accessed=rows * inner * 8 + rows * state * 12,
            transcendentals=rows * rows * heads_local,
        ),
    )(b, c, x, g, lines, columns)


def shards(
    hidden,
    norm_gain,
    expert_choice,
    route_weight,
    gate_weight,
    up_weight,
    down_weight,
    layer_grad,
    scan_input,
    state_input,
    state_output,
    log_decay,
    skip_gain,
    out_weight,
):
    seq_size, head_size = lax.axis_size("seq"), lax.axis_size("head")
    devices = seq_size * head_size
    experts = devices // 2
    tok, model_width = hidden.shape
    top_count = expert_choice.shape[1]
    half = 9 * tok * top_count // (16 * experts)
    groups = 1 << ((log2(devices)) // 2)
    plane = devices // groups
    plane_experts = plane // 2
    seq_place, head_place = lax.axis_index("seq"), lax.axis_index("head")
    place = seq_place * head_size + head_place
    group = place // plane
    plane_lists = [[z * plane + j for j in range(plane)] for z in range(groups)]

    def across(value, mask):
        return flipped(value, both, mask * plane)

    def spread(first):
        rows = [first]
        for m in range(1, groups):
            low = m & -m
            rows.append(across(rows[m ^ low], low))
        return rows

    def exchanged(value):
        return lax.all_to_all(
            value, both, split_axis=0, concat_axis=0, tiled=True, axis_index_groups=plane_lists
        )

    choice_t = expert_choice.T
    named = choice_t[None, :, :] == jnp.arange(experts, dtype=jnp.int32)[:, None, None]
    chosen = jnp.any(named, axis=1)
    before = jnp.arange(tok)[:, None] < jnp.arange(tok)[None, :]
    rank = dot_nn(chosen.astype(short), before.astype(short))
    rank = jnp.where(chosen, rank, -1.0)
    prob = jnp.sum(jnp.where(named, route_weight.T.astype(wide)[None], 0.0), axis=1)
    tables = spread(jnp.concatenate([rank, prob], axis=0))

    hidden_wide = hidden.astype(wide)
    inverse = lax.rsqrt(jnp.mean(hidden_wide * hidden_wide, axis=1, keepdims=True) + epsilon)
    normalized = hidden_wide * inverse
    normed = (normalized * norm_gain[None, :]).astype(short)
    normed_rows = spread(normed)
    grad_rows = spread(layer_grad)

    gate_up = jnp.concatenate([gate_weight[0], up_weight[0]], axis=1)
    weights = [(gate_up, down_weight[0])]
    weights.append((flipped(gate_up, "head", 1), flipped(down_weight[0], "head", 1)))
    hidden_half = down_weight.shape[1]

    per_part = groups // parts_count
    slot_rows = per_part * half
    onehots, probs, sent_normed, sent_grad = [], [], [], []
    for part in range(parts_count):
        members = range(part * per_part, (part + 1) * per_part)
        ranks, part_probs = [], []
        for b, m in enumerate(members):
            first = group * plane_experts
            mine = lax.dynamic_slice_in_dim(tables[m], first, plane_experts, 0)
            weight = lax.dynamic_slice_in_dim(tables[m], experts + first, plane_experts, 0)
            mine = jnp.stack([mine, mine - half], axis=1).reshape(plane, tok)
            ranks.append(jnp.where((mine >= 0) & (mine < half), mine + b * half, -1.0))
            part_probs.append(jnp.stack([weight, weight], axis=1).reshape(plane, tok))
        target = jnp.concatenate(ranks, axis=1).astype(jnp.int32)
        weight = jnp.concatenate(part_probs, axis=1)
        table = target[:, None, :] == jnp.arange(slot_rows, dtype=jnp.int32)[None, :, None]
        probs.append(jnp.sum(jnp.where(table, weight[:, None, :], 0.0), axis=2))
        onehot = table.astype(short).reshape(plane * slot_rows, per_part * tok)
        onehots.append(onehot)
        part_normed = jnp.concatenate([normed_rows[m] for m in members], axis=0)
        part_grad = jnp.concatenate([grad_rows[m] for m in members], axis=0)
        sent_normed.append(dot_nn(onehot, part_normed, short).reshape(plane, slot_rows, model_width))
        sent_grad.append(dot_nn(onehot, part_grad, short).reshape(plane, slot_rows, model_width))
    received = []
    for part in range(parts_count):
        received.append([exchanged(sent_normed[part]), exchanged(sent_grad[part])])
    prob_slots = exchanged(jnp.concatenate(probs, axis=1)[:, None, :])
    prob_slots = prob_slots.reshape(plane, parts_count, slot_rows).transpose(1, 0, 2)

    seq_rows, inner_width = scan_input.shape
    heads_local = log_decay.shape[1]
    head_dim = inner_width // heads_local
    lower = jnp.arange(seq_rows)[:, None] >= jnp.arange(seq_rows)[None, :]
    lower_ones = lower.astype(wide)
    cumulative = jnp.dot(lower_ones, log_decay, precision=highest)
    cumulative_t = cumulative.T
    total_decay = cumulative[-1]
    head_of = (jnp.arange(inner_width) // head_dim)[None, :] == jnp.arange(heads_local)[:, None]
    expand = head_of.astype(wide)

    def expanded(value):
        return jnp.repeat(value, head_dim, axis=1)

    from_start = expanded(jnp.exp(cumulative))
    to_end = expanded(jnp.exp(total_decay[None, :] - cumulative))
    skip_row = jnp.repeat(skip_gain, head_dim)[None, :]
    values = scan_input.astype(wide)
    values_end = (values * to_end).astype(short)
    inner_seq = 1 << (log2(seq_size) // 2)
    outer_seq = seq_size // inner_seq
    inner_place, outer_place = seq_place % inner_seq, seq_place // inner_seq

    line = total_decay[None, :]
    pieces = jnp.concatenate([line] + [flipped(line, "seq", m) for m in range(1, inner_seq)], axis=0)
    pieces = jnp.take(pieces, jnp.arange(inner_seq) ^ inner_place, axis=0)
    pieces = jnp.stack(
        [pieces] + [flipped(pieces, "seq", m * inner_seq) for m in range(1, outer_seq)], axis=0
    )
    totals = jnp.take(pieces, jnp.arange(outer_seq) ^ outer_place, axis=0).reshape(seq_size, heads_local)
    reached = jnp.cumsum(totals, axis=0)
    ended = jnp.concatenate([jnp.zeros((1, heads_local), wide), reached], axis=0)

    def before_of(index):
        return lax.dynamic_index_in_dim(ended, jnp.clip(index, 0, seq_size), 0, False)

    def factor(log_value):
        return jnp.repeat(jnp.exp(jnp.minimum(log_value, 0.0)), head_dim)[:, None]

    def carried(local, reverse):
        start = outer_place * inner_seq
        pieces = [local] + [flipped(local, "seq", m) for m in range(1, inner_seq)]
        nearby = jnp.zeros(local.shape, wide)
        joined = jnp.zeros(local.shape, wide)
        for m in range(inner_seq):
            source = start + (inner_place ^ m)
            value = pieces[m].astype(wide)
            if reverse:
                near = before_of(source) - before_of(seq_place + 1)
                far = before_of(source) - before_of(start)
                ahead = source > seq_place
            else:
                near = before_of(seq_place) - before_of(source + 1)
                far = before_of(start + inner_seq) - before_of(source + 1)
                ahead = source < seq_place
            nearby = nearby + jnp.where(ahead, factor(near), 0.0) * value
            joined = joined + factor(far) * value
        joined = joined.astype(short)
        for k in range(1, outer_seq):
            if reverse:
                other = shifted(joined, "seq", -k * inner_seq)
                log_value = before_of(start + k * inner_seq) - before_of(seq_place + 1)
            else:
                other = shifted(joined, "seq", k * inner_seq)
                log_value = before_of(seq_place) - before_of(start - (k - 1) * inner_seq)
            nearby = nearby + factor(log_value) * other.astype(wide)
        return nearby

    local_state = dot_tn(values_end, state_input, short)
    state_in = carried(local_state, False)
    state_short = state_in.astype(short)
    read_state = dot_nt(state_output, state_short) * from_start
    y_inner = scan_forward(state_input, state_output, scan_input, cumulative_t, cumulative)
    y_rounded = (y_inner + read_state + skip_row * values).astype(short)

    def activated(part):
        rows = received[part][0].reshape(plane * slot_rows, model_width)
        grads = received[part][1].reshape(plane * slot_rows, model_width)
        weight_column = prob_slots[part].reshape(-1)[:, None]
        prob_total, row_total, halves = 0.0, 0.0, []
        for gate_up_half, down_half in weights:
            pre = dot_nn(rows, gate_up_half)
            gate_pre, up_pre = pre[:, :hidden_half], pre[:, hidden_half:]
            sig = jax.nn.sigmoid(gate_pre)
            active = (gate_pre * sig * up_pre).astype(short)
            back = dot_nt(grads, down_half)
            prob_total = prob_total + jnp.sum(active.astype(wide) * back, axis=1)
            d_active = weight_column * back
            d_gate = (d_active * up_pre * sig * (1.0 + gate_pre * (1.0 - sig))).astype(short)
            d_up = (d_active * gate_pre * sig).astype(short)
            d_pre = jnp.concatenate([d_gate, d_up], axis=1)
            row_total = row_total + dot_nt(d_pre, gate_up_half)
            halves.append((active, d_pre))
        scaled = (weight_column * grads.astype(wide)).astype(short)
        return row_total.astype(short), prob_total, halves, rows, scaled

    done = [activated(part) for part in range(parts_count)]
    partial = [None] * groups
    prob_partial = [None] * groups
    returned_prob = exchanged(
        jnp.stack([done[part][1].reshape(plane, slot_rows) for part in range(parts_count)], axis=1)
    )
    for part in reversed(range(parts_count)):
        back = exchanged(done[part][0].reshape(plane, slot_rows, model_width))
        back = back.reshape(plane * slot_rows, model_width)
        token_sum = dot_tn(onehots[part], back)
        table = onehots[part].reshape(plane, slot_rows, per_part * tok).astype(wide)
        prob_sum = jnp.sum(table * returned_prob[:, part, :, None], axis=1)
        prob_sum = prob_sum.reshape(plane_experts, 2, per_part * tok).sum(axis=1)
        for b in range(per_part):
            index = part * per_part + b
            partial[index] = token_sum[b * tok : (b + 1) * tok]
            prob_partial[index] = prob_sum[:, b * tok : (b + 1) * tok]

    bit = 1
    tree = {m: partial[m] for m in range(groups)}
    while bit < groups:
        moved = {m: across(tree[m].astype(short), bit) for m in tree if m & bit}
        tree = {m: tree[m] + moved[m ^ bit].astype(wide) for m in tree if not m & bit}
        bit = bit * 2
    d_normed = tree[0]
    prob_all = jnp.stack(
        [prob_partial[0]] + [across(prob_partial[m], m) for m in range(1, groups)], axis=0
    )
    prob_all = jnp.take(prob_all, jnp.arange(groups) ^ group, axis=0).reshape(experts, tok)
    d_route_weight = jnp.sum(jnp.where(named, prob_all[:, None, :], 0.0), axis=0).T.astype(short)

    gain_scaled = norm_gain[None, :] * d_normed
    centered = jnp.mean(gain_scaled * normalized, axis=1, keepdims=True)
    d_hidden = (
        layer_grad.astype(wide) + inverse * (gain_scaled - normalized * centered)
    ).astype(short)
    d_norm_gain = jnp.sum(d_normed * normalized, axis=0)
    for axis in ("head", "seq"):
        d_norm_gain = summed(d_norm_gain, axis)

    rows_all = jnp.concatenate([done[part][3] for part in range(parts_count)], axis=0)
    scaled_all = jnp.concatenate([done[part][4] for part in range(parts_count)], axis=0)
    terms = []
    for side in (1, 0):
        active_all = jnp.concatenate([done[part][2][side][0] for part in range(parts_count)], axis=0)
        pre_all = jnp.concatenate([done[part][2][side][1] for part in range(parts_count)], axis=0)
        terms.append((dot_tn(rows_all, pre_all), dot_tn(active_all, scaled_all)))
    other_gate_up = flipped(terms[0][0].astype(short), "head", 1).astype(wide)
    other_down = flipped(terms[0][1].astype(short), "head", 1).astype(wide)
    d_gate_up = (terms[1][0] + other_gate_up).astype(short)
    d_gate_weight = d_gate_up[:, :hidden_half][None]
    d_up_weight = d_gate_up[:, hidden_half:][None]
    d_down_weight = (terms[1][1] + other_down).astype(short)[None]

    gathered = [d_hidden]
    order = [0]
    for k in reversed(range(log2(head_size))):
        gathered = gathered + [flipped(value, "head", 1 << k) for value in gathered]
        order = order + [m ^ (1 << k) for m in order]
    sorted_blocks = [None] * head_size
    for value, m in zip(gathered, order):
        sorted_blocks[m] = value
    cotangent = jnp.concatenate(sorted_blocks, axis=0)
    natural = jnp.arange(head_size) ^ head_place

    def reordered(value):
        shape = value.shape
        return jnp.take(value.reshape(head_size, tok, shape[1]), natural, axis=0).reshape(shape)

    grad = reordered(dot_nn(cotangent, out_weight, short))
    grad_wide = grad.astype(wide)
    grad_start = (grad_wide * from_start).astype(short)
    local_adjoint = dot_tn(grad_start, state_output, short)
    adjoint = carried(local_adjoint, True)
    adjoint_short = adjoint.astype(short)

    product = dot_tn(cotangent, reordered(y_rounded), short)
    product = product.reshape(outer_seq, inner_seq, model_width // seq_size, inner_width)

    def picked(index):
        return lax.dynamic_index_in_dim(product, index, 1, False)

    mine = picked(inner_place).astype(wide)
    for m in range(1, inner_seq):
        mine = mine + flipped(picked(inner_place ^ m), "seq", m).astype(wide)
    mine_short = mine.astype(short)
    d_out = lax.dynamic_index_in_dim(mine, outer_place, 0, False)
    for m in range(1, outer_seq):
        piece = lax.dynamic_index_in_dim(mine_short, outer_place ^ m, 0, False)
        d_out = d_out + flipped(piece, "seq", m * inner_seq).astype(wide)
    d_out_weight = d_out.astype(short)

    dx_inner, later_sum, earlier_sum, db_inner, dc_inner = scan_backward(
        state_input, state_output, scan_input, grad, cumulative_t, cumulative
    )
    read_adjoint = dot_nt(state_input, adjoint_short) * to_end
    d_scan_input = (dx_inner + read_adjoint + skip_row * grad_wide).astype(short)
    input_part = db_inner + dot_nn(values_end, adjoint_short)
    output_part = dc_inner + dot_nn(grad_start, state_short)
    d_state_output = summed(output_part.astype(short), "head").astype(wide)
    d_state_input = summed(input_part.astype(short), "head").astype(wide)

    def head_sum(value):
        return jnp.dot(value, expand.T, precision=highest)

    d_skip_gain = summed(jnp.sum(head_sum(values * grad_wide), axis=0), "seq")
    growth = jnp.exp(total_decay)
    from_past = head_sum(read_state * grad_wide)
    to_future = head_sum(read_adjoint * values)
    corner = growth * jnp.sum(
        (state_in * adjoint).reshape(heads_local, head_dim * state_input.shape[1]), axis=1
    )
    forward_part = later_sum.T - earlier_sum + from_past
    d_log_decay = (
        lax.dot_general(
            lower_ones, forward_part, (((0,), (0,)), ((), ())),
            precision=highest, preferred_element_type=wide,
        )
        + jnp.dot(lower_ones - jnp.eye(seq_rows, dtype=wide), to_future, precision=highest)
        + corner[None, :]
    )
    return (
        d_hidden,
        d_norm_gain,
        d_route_weight,
        d_gate_weight,
        d_up_weight,
        d_down_weight,
        d_out_weight,
        d_scan_input,
        d_state_input,
        d_state_output,
        d_log_decay,
        d_skip_gain,
    )


def solution(mesh):
    in_specs = (
        P(("seq", "head"), None),
        P(),
        P(("seq", "head"), None),
        P(("seq", "head"), None),
        P(("seq", "head"), None, None),
        P(("seq", "head"), None, None),
        P(("seq", "head"), None, None),
        P(("seq", "head"), None),
        P("seq", "head"),
        P("seq", None),
        P("seq", None),
        P("seq", "head"),
        P("head"),
        P(None, "head"),
    )
    out_specs = (
        P(("seq", "head"), None),
        P(),
        P(("seq", "head"), None),
        P(("seq", "head"), None, None),
        P(("seq", "head"), None, None),
        P(("seq", "head"), None, None),
        P("seq", "head"),
        P("seq", "head"),
        P("seq", None),
        P("seq", None),
        P("seq", "head"),
        P("head"),
    )
    return jax.shard_map(shards, mesh=mesh, in_specs=in_specs, out_specs=out_specs, check_vma=False)
```

time: 810 us -> 487 us (0.60)
  blocking collectives: 231 us -> 0 us
  waiting for transfers between devices: 264 us -> 142 us
  starting transfers between devices: 22.5 us -> 104 us
  matrix products: 165 us -> 117 us
  other arithmetic: 25.4 us -> 54.8 us
  local copies, waits for them, and re-layouts: 75.2 us -> 49.9 us
  between operations: 14.9 us -> 2.57 us
    all_to_all x3 -> x8, waiting for transfers between devices: 192 us -> 25.2 us  [exchanged(): lax.all_to_all(value, both, split_axis=0, concat_axis=0, tiled=True, axis...]
    all_to_all x2 -> x0, blocking collectives: 155 us -> none  [the longest x1 124 us: shards(): lax.all_to_all(row_grad, ('seq', 'head'), split_axis=0, concat_axis=0, ti...]
    ppermute x6 -> x50, waiting for transfers between devices: 0.02 us -> 117 us  [the longest x44 117 us: flipped(): return lax.ppermute(value, axis, [(i, i ^ mask) for i in range(size)])]
    all_gather x3 -> x0, waiting for transfers between devices: 72 us -> none  [the longest x2 51.8 us: carried_in(): gathered = jax.tree.map(lambda a: lax.all_gather(a, axis), part)]
    ppermute x6 -> x50, starting transfers between devices: 1.24 us -> 69.3 us  [the longest x44 50.2 us: flipped(): return lax.ppermute(value, axis, [(i, i ^ mask) for i in range(size)])]
    psum x2 -> x0, blocking collectives: 58.2 us -> none  [the longest x1 40 us: shards(): lax.psum(jnp.sum(d_normed * normalized, axis=0), ('seq', 'head'))]
    dot_general x35 -> x37, matrix products: 165 us -> 117 us  [the longest x10 41.5 us: dot_nt(): lax.dot_general(a, b, (((1,), (1,)), ((), ())), preferred_element_type=out)]
    reshape x6 -> x5, local copies, waits for them, and re-layouts: 43.7 us -> 5.21 us  [the longest x2 5.11 us: expanded(): return jnp.repeat(value, head_dim, axis=1)]
  transfers between devices with their start and end apart: 14 -> 58, of which waited for: 5 -> 23; matrix products, arithmetic and copies ran while one was open for 23% -> 42% of each run, Pallas kernels for 0% -> 2%
where the time goes in v1:
time: 487 us; the launch traced here: 478 us
  waiting for transfers between devices  142 us (29%)
  matrix products  117 us (24%)
  starting transfers between devices  104 us (21%)
  other arithmetic  54.8 us (11%)
  local copies, waits for them, and re-layouts  49.9 us (10%)
  Pallas kernels  7.86 us (2%)
    ppermute x44, waiting for transfers between devices, flipped(): return lax.ppermute(value, axis, [(i, i ^ mask) for i in range(size)])  117 us
    ppermute x44, starting transfers between devices, flipped(): return lax.ppermute(value, axis, [(i, i ^ mask) for i in range(size)])  50.2 us
    dot_general x10, matrix products, dot_nt(): lax.dot_general(a, b, (((1,), (1,)), ((), ())), preferred_element_type=out)  41.5 us
    dot_general x9, matrix products, dot_tn(): lax.dot_general(a, b, (((0,), (0,)), ((), ())), preferred_element_type=out)  36.7 us
    dot_general x12, matrix products, dot_nn(): lax.dot_general(a, b, (((1,), (0,)), ((), ())), preferred_element_type=out)  34.5 us
    all_to_all x8, starting transfers between devices, exchanged(): lax.all_to_all(value, both, split_axis=0, concat_axis=0, tiled=True, axis...  34.3 us
    all_to_all x8, waiting for transfers between devices, exchanged(): lax.all_to_all(value, both, split_axis=0, concat_axis=0, tiled=True, axis...  25.2 us
    ppermute x6, starting transfers between devices, shifted(): return lax.ppermute(value, axis, pairs)  19.1 us
  transfers between devices with their start and end apart: 58, of which 23 were waited for; matrix products, arithmetic and copies ran while one was open for 42% of the time, Pallas kernels for 2%

profile of v1, /device:TPU:8, one launch (start us, length us, event | category | flops | bytes accessed | tf_op | source)
XLA Modules:
  0.0 478.5 jit_solution(1544046483488860021)
XLA Ops:
  8.3 10.9 %collective-permute-done.4 = bf16[128,2048]{1,0:T(8,128)(2,1)S(1)} collective-permute-done((bf16[128,2048]{1,0:T(8,128)(2,1)S(1)}, bf16[128,2048]{1,0:T(8,128)(2,1)S(1)}, u32[]{:S(2)}, u32[]{:S(2)}) %collective-permute-start.4) | collective-permute-done | bytes 524320 | tf_op jit(solution)/shard_map/ppermute | solution.py:27
  21.5 4.4 all-to-all-start.2
  25.9 2.8 collective-permute-start.1
  30.6 2.6 collective-permute-start.8
  33.2 3.8 pad_maximum_fusion.2
  37.6 17.1 %collective-permute-done.3 = bf16[128,2048]{1,0:T(8,128)(2,1)S(1)} collective-permute-done((bf16[128,2048]{1,0:T(8,128)(2,1)}, bf16[128,2048]{1,0:T(8,128)(2,1)S(1)}, u32[]{:S(2)}, u32[]{:S(2)}) %collective-permute-start.3) | collective-permute-done | bytes 524320 | tf_op jit(solution)/shard_map/ppermute | solution.py:27
  54.7 3.3 fusion.45
  57.9 4.5 all-to-all-start.1
  67.7 8.8 %collective-permute-done.2 = f32[32,128]{1,0:T(8,128)S(1)} collective-permute-done((f32[32,128]{1,0:T(8,128)S(1)}, f32[32,128]{1,0:T(8,128)S(1)}, u32[]{:S(2)}, u32[]{:S(2)}) %collective-permute-start.2) | collective-permute-done | bytes 16416 | tf_op jit(solution)/shard_map/ppermute | solution.py:27
  78.9 9.0 %collective-permute-done.11 = bf16[128,2048]{1,0:T(8,128)(2,1)S(1)} collective-permute-done((bf16[128,2048]{1,0:T(8,128)(2,1)}, bf16[128,2048]{1,0:T(8,128)(2,1)S(1)}, u32[]{:S(2)}, u32[]{:S(2)}) %collective-permute-start.11) | collective-permute-done | bytes 524320 | tf_op jit(solution)/shard_map/ppermute | solution.py:27
  87.9 3.2 fusion.54
  91.2 4.5 all-to-all-start.5
  97.0 2.8 shard_map.229
  102.1 2.5 copy.94
  106.4 2.6 copy.93
  119.0 9.6 %collective-permute-done.28 = f32[2,8]{1,0:T(2,128)S(1)} collective-permute-done((f32[2,8]{1,0:T(2,128)S(1)}, f32[2,8]{1,0:T(2,128)S(1)}, u32[]{:S(2)}, u32[]{:S(2)}) %collective-permute-start.28) | collective-permute-done | bytes 96 | tf_op jit(solution)/shard_map/ppermute | solution.py:27
  134.7 3.3 fusion.51
  138.1 4.7 all-to-all-start.4
  143.6 4.7 fusion.155
  148.4 4.8 %multiply_reduce_fusion.3 = (f32[576]{0:T(1024)S(1)}, bf16[576,384]{1,0:T(8,128)(2,1)}, f32[576,384]{1,0:T(8,128)}) fusion(f32[576,768]{1,0:T(8,128)S(1)} %fusion.155, bf16[576,2048]{1,0:T(8,128)(2,1)} %bitcast.24, bf16[1,384,2048]{2,1,0:T(8,128)(2,1)S(1)} %copy-done.85), kind=kOutput, calls=%fused_computation.137 | convolution fusion | flops 907959744 | bytes 7031040 | tf_op jit(solution)/shard_map/dot_general | solution.py:48
  153.2 4.9 %fusion.154 = f32[576,768]{1,0:T(8,128)} fusion(bf16[576,2048]{1,0:T(8,128)(2,1)} %bitcast.35, bf16[2048,384]{1,0:T(8,128)(2,1)S(1)} %bitcast.218, bf16[2048,384]{1,0:T(8,128)(2,1)S(1)} %bitcast.223), kind=kOutput, calls=%fused_computation.345 | convolution fusion | flops 1818230784 | bytes 7274496 | tf_op jit(solution)/shard_map/dot_general | solution.py:44
  158.1 13.2 %all-to-all-done.4 = bf16[8,72,2048]{2,1,0:T(8,128)(2,1)} async-done(((bf16[8,72,2048]{2,1,0:T(8,128)(2,1)}), bf16[8,72,2048]{2,1,0:T(8,128)(2,1)}, u32[]{:S(2)}, u32[]{:S(2)}) %all-to-all-start.4) | async-done | bytes 2359328 | tf_op jit(solution)/shard_map/all_to_all | solution.py:228
  171.3 5.1 %multiply_reduce_fusion.1 = (f32[576]{0:T(1024)S(1)}, bf16[576,384]{1,0:T(8,128)(2,1)}, f32[576,384]{1,0:T(8,128)}) fusion(f32[576,768]{1,0:T(8,128)} %fusion.154, bf16[576,2048]{1,0:T(8,128)(2,1)} %bitcast.33, bf16[1,384,2048]{2,1,0:T(8,128)(2,1)} %param.22), kind=kOutput, calls=%fused_computation.133 | convolution fusion | flops 907959744 | bytes 7031040 | tf_op jit(solution)/shard_map/dot_general | solution.py:48
  176.4 4.6 fusion.162
  181.0 5.2 %multiply_reduce_fusion.2 = (f32[576]{0:T(1024)S(1)}, bf16[576,384]{1,0:T(8,128)(2,1)}, f32[576,384]{1,0:T(8,128)}) fusion(f32[576,768]{1,0:T(8,128)S(1)} %fusion.162, bf16[576,2048]{1,0:T(8,128)(2,1)} %bitcast.24, bf16[384,2048]{1,0:T(8,128)(2,1)} %collective-permute-done.5), kind=kOutput, calls=%fused_computation.135 | convolution fusion | flops 907959744 | bytes 7031040 | tf_op jit(solution)/shard_map/dot_general | solution.py:48
  186.4 4.6 fusion.163
  191.0 5.2 %multiply_reduce_fusion = (f32[576]{0:T(1024)S(1)}, bf16[576,384]{1,0:T(8,128)(2,1)}, f32[576,384]{1,0:T(8,128)}) fusion(f32[576,768]{1,0:T(8,128)S(1)} %fusion.163, bf16[576,2048]{1,0:T(8,128)(2,1)} %bitcast.33, bf16[384,2048]{1,0:T(8,128)(2,1)} %collective-permute-done.5), kind=kOutput, calls=%fused_computation.131 | convolution fusion | flops 907959744 | bytes 7031040 | tf_op jit(solution)/shard_map/dot_general | solution.py:48
  196.9 3.3 all-to-all-start.7
  200.3 4.6 all-to-all-done.7
  206.3 3.7 all-to-all-start
  214.9 3.5 multiply_convert_fusion.7
  220.5 5.4 %add_convert_fusion.1 = bf16[576,2048]{1,0:T(8,128)(2,1)} fusion(f32[576,2048]{1,0:T(8,128)S(1)} %fusion.69, bf16[2048,768]{1,0:T(8,128)(2,1)} %collective-permute-done.6, bf16[576,384]{1,0:T(8,128)(2,1)S(1)} %get-tuple-element.57, bf16[576,384]{1,0:T(8,128)(2,1)S(1)} %get-tuple-element.56), kind=kOutput, calls=%fused_computation.10 | convolution fusion | flops 1816068096 | bytes 11108352 | tf_op jit(solution)/shard_map/dot_general | solution.py:48
  225.9 4.5 all-to-all-start.6
  239.5 3.6 collective-permute-start.19
  243.8 3.5 multiply_convert_fusion.11
  249.5 5.4 %add_convert_fusion.2 = bf16[576,2048]{1,0:T(8,128)(2,1)} fusion(f32[576,2048]{1,0:T(8,128)S(1)} %fusion.62, bf16[2048,768]{1,0:T(8,128)(2,1)} %collective-permute-done.6, bf16[576,384]{1,0:T(8,128)(2,1)S(1)} %get-tuple-element.53, bf16[576,384]{1,0:T(8,128)(2,1)S(1)} %get-tuple-element.52), kind=kOutput, calls=%fused_computation.11 | convolution fusion | flops 1816068096 | bytes 11108352 | tf_op jit(solution)/shard_map/dot_general | solution.py:48
  254.8 4.1 all-to-all-done.6
  258.9 4.6 all-to-all-start.3
  263.5 8.7 %convolution_convert_fusion = bf16[2048,768]{1,0:T(8,128)(2,1)} fusion(bf16[576,2048]{1,0:T(8,128)(2,1)} %bitcast.35, bf16[576,2048]{1,0:T(8,128)(2,1)} %bitcast.27, bf16[576,384]{1,0:T(8,128)(2,1)} %copy-done.56, bf16[576,384]{1,0:T(8,128)(2,1)S(1)} %get-tuple-element.56, bf16[576,384]{1,0:T(8,128)(2,1)} %copy-done.58, bf16[576,384]{1,0:T(8,128)(2,1)} %copy-done.57), kind=kOutput, calls=%fused_computation.12 | convolution fusion | flops 3641966592 | bytes 9633792 | tf_op jit(solution)/shard_map/dot_general | solution.py:52
  274.7 3.0 multiply_convert_fusion
  277.7 3.6 convolution_bitcast_fusion
  283.5 3.5 collective-permute-start.12
  287.1 3.4 fusion.3
  292.0 2.8 convolution_bitcast_fusion.1
  297.0 2.5 collective-permute-done.12
  307.9 3.8 collective-permute-start.32
  315.9 10.6 %collective-permute-done.7 = bf16[128,2048]{1,0:T(8,128)(2,1)} collective-permute-done((bf16[128,2048]{1,0:T(8,128)(2,1)}, bf16[128,2048]{1,0:T(8,128)(2,1)}, u32[]{:S(2)}, u32[]{:S(2)}) %collective-permute-start.7) | collective-permute-done | bytes 524320 | tf_op jit(solution)/shard_map/ppermute | solution.py:27
  326.5 7.2 %collective-permute-start.33 = (bf16[512,128]{0,1:T(8,128)(2,1)}, bf16[512,128]{0,1:T(8,128)(2,1)}, u32[]{:S(2)}, u32[]{:S(2)}) collective-permute-start(bf16[512,128]{0,1:T(8,128)(2,1)} %fusion.100), channel_id=1, source_target_pairs={{0,16},{4,20},{8,24},{12,28},{1,17},{5,21},{9,25},{13,29},{2,18},{... | collective-permute-start | bytes 393224 | tf_op jit(solution)/shard_map/ppermute | solution.py:33
  339.0 5.9 %fusion.4 = bf16[1,384,2048]{2,1,0:T(8,128)(2,1)} fusion(bf16[384,2048]{1,0:T(8,128)(2,1)} %collective-permute-done.23, bf16[576,2048]{1,0:T(8,128)(2,1)} %copy-done.25, bf16[576,2048]{1,0:T(8,128)(2,1)S(1)} %copy-done.24, bf16[576,384]{1,0:T(8,128)(2,1)} %get-tuple-element.49, bf16[576,384]{1,0:T(8,128)(2,1)} %get-tuple-element.43), kind=kOutput, calls=%fused_computation.21 | convolution fusion | flops 1825505280 | bytes 8749056 | tf_op jit(solution)/shard_map/dot_general | solution.py:52
  352.5 7.7 %add_convert_fusion = bf16[2048,768]{1,0:T(8,128)(2,1)S(1)} fusion(bf16[2048,768]{1,0:T(8,128)(2,1)} %collective-permute-done.22, bf16[576,2048]{1,0:T(8,128)(2,1)} %bitcast.35, bf16[576,2048]{1,0:T(8,128)(2,1)} %bitcast.27, bf16[576,384]{1,0:T(8,128)(2,1)S(1)} %copy-done.49, bf16[576,384]{1,0:T(8,128)(2,1)S(1)} %copy-done.51, ...), kind=kOutput, calls=%fused_computation.5 | convolution fusion | flops 3645112320 | bytes 12779520 | tf_op jit(solution)/shard_map/dot_general | solution.py:52
  360.2 3.1 collective-permute-done.25
  377.8 2.7 collective-permute-start.48
  382.8 3.9 collective-permute-start.40
  390.2 5.1 %shard_map.230 = (f32[512,512]{1,0:T(8,128)S(1)}, f32[8,512]{1,0:T(8,128)S(1)}, f32[512,8]{1,0:T(8,128)S(1)}, f32[512,128]{1,0:T(8,128)S(1)}, f32[512,128]{1,0:T(8,128)S(1)}) custom-call(bf16[512,128]{1,0:T(8,128)(2,1)S(1)} %copy-done.4, bf16[512,128]{1,0:T(8,128)(2,1)S(1)} %copy-done.5, bf16[512,512]{1,0:T(8,128)(2,1)S(1)} %copy-done.1, ...), custom_call_target="tpu_custom_call" | custom-call | flops 2147483648 | bytes 2883584 | tf_op jit(solution)/shard_map/pallas_call | solution.py:165
  399.2 3.9 copy.106
  405.9 2.5 fusion.20
  412.2 3.8 fusion.42
  416.0 2.6 gather_fusion.3
  419.8 2.9 fusion.164
  431.2 17.3 %collective-permute-done.35 = bf16[4,256,512]{2,1,0:T(8,128)(2,1)S(1)} collective-permute-done((bf16[4,256,512]{2,1,0:T(8,128)(2,1)S(1)}, bf16[4,256,512]{2,1,0:T(8,128)(2,1)S(1)}, u32[]{:S(2)}, u32[]{:S(2)}) %collective-permute-start.35) | collective-permute-done | bytes 1048608 | tf_op jit(solution)/shard_map/ppermute | solution.py:27
  449.4 4.4 collective-permute-start.37
  455.8 3.8 collective-permute-done.36
  459.7 12.2 %collective-permute-done.37 = bf16[256,512]{1,0:T(8,128)(2,1)S(1)} collective-permute-done((bf16[256,512]{1,0:T(8,128)(2,1)S(1)}, bf16[256,512]{1,0:T(8,128)(2,1)S(1)}, u32[]{:S(2)}, u32[]{:S(2)}) %collective-permute-start.37) | collective-permute-done | bytes 262176 | tf_op jit(solution)/shard_map/ppermute | solution.py:27
  471.8 5.4 %collective-permute-done.38 = bf16[256,512]{1,0:T(8,128)(2,1)S(1)} collective-permute-done((bf16[256,512]{1,0:T(8,128)(2,1)S(1)}, bf16[256,512]{1,0:T(8,128)(2,1)S(1)}, u32[]{:S(2)}, u32[]{:S(2)}) %collective-permute-start.38) | collective-permute-done | bytes 262176 | tf_op jit(solution)/shard_map/ppermute | solution.py:27
  (439 shorter events, 140.8 us)
Async XLA Ops:
  0.6 366.6 %copy-start = (bf16[2048,512]{1,0:T(8,128)(2,1)S(1)}, bf16[2048,512]{1,0:T(8,128)(2,1)}, u32[]{:S(2)}) copy-start(bf16[2048,512]{1,0:T(8,128)(2,1)} %param.29) | copy-start | bytes 6291460
  3.1 4.6 collective-permute-start
  5.6 13.7 %collective-permute-start.4 = (bf16[128,2048]{1,0:T(8,128)(2,1)S(1)}, bf16[128,2048]{1,0:T(8,128)(2,1)S(1)}, u32[]{:S(2)}, u32[]{:S(2)}) collective-permute-start(bf16[128,2048]{1,0:T(8,128)(2,1)S(1)} %fusion.28), channel_id=1, source_target_pairs={{0,8},{1,9},{2,10},{3,11},{4,12},{5,13},{6,14},{7,15},{8,0},{9,1},... | collective-permute-start | bytes 1572872 | tf_op jit(solution)/shard_map/ppermute | solution.py:27
  8.3 46.3 %copy-start.59 = (s32[8,256]{1,0:T(8,128)}, s32[8,256]{1,0:T(8,128)S(1)}, u32[]{:S(2)}) copy-start(s32[8,256]{1,0:T(8,128)S(1)} %maximum_convert_fusion) | copy-start | bytes 24580
  21.5 36.4 %all-to-all-start.2 = ((bf16[8,72,2048]{2,1,0:T(8,128)(2,1)}), bf16[8,72,2048]{2,1,0:T(8,128)(2,1)}, u32[]{:S(2)}, u32[]{:S(2)}) async-start(bf16[8,72,2048]{2,1,0:T(8,128)(2,1)} %fusion.48), calls=%async_computation.2 | async-start | bytes 4718592 | tf_op jit(solution)/shard_map/all_to_all | solution.py:228
  25.9 39.1 %collective-permute-start.1 = (f32[32,128]{1,0:T(8,128)S(1)}, f32[32,128]{1,0:T(8,128)S(1)}, u32[]{:S(2)}, u32[]{:S(2)}) collective-permute-start(f32[32,128]{1,0:T(8,128)S(1)} %pad_maximum_fusion.17), channel_id=1, source_target_pairs={{0,16},{1,17},{2,18},{3,19},{4,20},{5,21},{6,22},{7,23},{8,24},{9,... | collective-permute-start | bytes 49160 | tf_op jit(solution)/shard_map/ppermute | solution.py:27
  28.7 37.0 %collective-permute-start.10 = (bf16[128,2048]{1,0:T(8,128)(2,1)S(1)}, bf16[128,2048]{1,0:T(8,128)(2,1)}, u32[]{:S(2)}, u32[]{:S(2)}) collective-permute-start(bf16[128,2048]{1,0:T(8,128)(2,1)S(1)} %fusion.28), channel_id=1, source_target_pairs={{0,16},{1,17},{2,18},{3,19},{4,20},{5,21},{6,22},{7,23},{8,24},{9,... | collective-permute-start | bytes 1572872 | tf_op jit(solution)/shard_map/ppermute | solution.py:27
  28.9 25.8 %collective-permute-start.3 = (bf16[128,2048]{1,0:T(8,128)(2,1)}, bf16[128,2048]{1,0:T(8,128)(2,1)S(1)}, u32[]{:S(2)}, u32[]{:S(2)}) collective-permute-start(bf16[128,2048]{1,0:T(8,128)(2,1)} %param.23), channel_id=1, source_target_pairs={{0,8},{1,9},{2,10},{3,11},{4,12},{5,13},{6,14},{7,15},{8,0},{9,1},... | collective-permute-start | bytes 1572872 | tf_op jit(solution)/shard_map/ppermute | solution.py:27
  30.6 83.0 %collective-permute-start.8 = (bf16[128,2048]{1,0:T(8,128)(2,1)}, bf16[128,2048]{1,0:T(8,128)(2,1)}, u32[]{:S(2)}, u32[]{:S(2)}) collective-permute-start(bf16[128,2048]{1,0:T(8,128)(2,1)} %param.23), channel_id=1, source_target_pairs={{0,16},{1,17},{2,18},{3,19},{4,20},{5,21},{6,22},{7,23},{8,24},{9,... | collective-permute-start | bytes 1572872 | tf_op jit(solution)/shard_map/ppermute | solution.py:27
  37.0 139.4 %collective-permute-start.6 = (bf16[2048,768]{1,0:T(8,128)(2,1)}, bf16[2048,768]{1,0:T(8,128)(2,1)}, u32[]{:S(2)}, u32[]{:S(2)}) collective-permute-start(bf16[2048,768]{1,0:T(8,128)(2,1)} %pad_maximum_fusion.2), channel_id=1, source_target_pairs={{0,1},{1,0},{2,3},{3,2},{4,5},{5,4},{6,7},{7,6},{8,9},{9,8},{10,11... | collective-permute-start | bytes 9437192 | tf_op jit(solution)/shard_map/ppermute | solution.py:27
  54.7 126.4 %collective-permute-start.5 = (bf16[384,2048]{1,0:T(8,128)(2,1)}, bf16[384,2048]{1,0:T(8,128)(2,1)}, u32[]{:S(2)}, u32[]{:S(2)}) collective-permute-start(bf16[384,2048]{1,0:T(8,128)(2,1)} %bitcast.256), channel_id=1, source_target_pairs={{0,1},{1,0},{2,3},{3,2},{4,5},{5,4},{6,7},{7,6},{8,9},{9,8},{10,11... | collective-permute-start | bytes 4718600 | tf_op jit(solution)/shard_map/ppermute | solution.py:27
  57.9 33.3 %all-to-all-start.1 = ((bf16[8,72,2048]{2,1,0:T(8,128)(2,1)}), bf16[8,72,2048]{2,1,0:T(8,128)(2,1)}, u32[]{:S(2)}, u32[]{:S(2)}) async-start(bf16[8,72,2048]{2,1,0:T(8,128)(2,1)} %fusion.45), calls=%async_computation.1 | async-start | bytes 4718592 | tf_op jit(solution)/shard_map/all_to_all | solution.py:228
  65.0 32.0 %copy-start.6 = (f32[512,8]{1,0:T(8,128)}, f32[512,8]{1,0:T(8,128)S(1)}, u32[]{:S(2)}) copy-start(f32[512,8]{1,0:T(8,128)S(1)} %copy.90.col_ref) | copy-start | bytes 49156
  65.7 10.9 %collective-permute-start.2 = (f32[32,128]{1,0:T(8,128)S(1)}, f32[32,128]{1,0:T(8,128)S(1)}, u32[]{:S(2)}, u32[]{:S(2)}) collective-permute-start(f32[32,128]{1,0:T(8,128)S(1)} %collective-permute-done.1), channel_id=1, source_target_pairs={{0,8},{1,9},{2,10},{3,11},{4,12},{5,13},{6,14},{7,15},{8,0},{9,1},... | collective-permute-start | bytes 49160 | tf_op jit(solution)/shard_map/ppermute | solution.py:27
  65.7 22.2 %collective-permute-start.11 = (bf16[128,2048]{1,0:T(8,128)(2,1)}, bf16[128,2048]{1,0:T(8,128)(2,1)S(1)}, u32[]{:S(2)}, u32[]{:S(2)}) collective-permute-start(bf16[128,2048]{1,0:T(8,128)(2,1)} %collective-permute-done.10), channel_id=1, source_target_pairs={{0,8},{1,9},{2,10},{3,11},{4,12},{5,13},{6,14},{7,15},{8,0},{9,1},... | collective-permute-start | bytes 1572872 | tf_op jit(solution)/shard_map/ppermute | solution.py:27
  76.5 35.8 %collective-permute-start.27 = (f32[1,8]{0,1:T(8,128)S(1)}, f32[1,8]{0,1:T(8,128)S(1)}, u32[]{:S(2)}, u32[]{:S(2)}) collective-permute-start(f32[1,8]{0,1:T(8,128)S(1)} %get-tuple-element.66), channel_id=1, source_target_pairs={{0,4},{4,0},{8,12},{12,8},{16,20},{20,16},{24,28},{28,24},{1,5},{5... | collective-permute-start | bytes 104 | tf_op jit(solution)/shard_map/ppermute | solution.py:27
  91.2 46.9 %all-to-all-start.5 = ((bf16[8,72,2048]{2,1,0:T(8,128)(2,1)}), bf16[8,72,2048]{2,1,0:T(8,128)(2,1)}, u32[]{:S(2)}, u32[]{:S(2)}) async-start(bf16[8,72,2048]{2,1,0:T(8,128)(2,1)} %fusion.54), calls=%async_computation.5 | async-start | bytes 4718592 | tf_op jit(solution)/shard_map/all_to_all | solution.py:228
  112.4 193.9 %copy-start.37 = (bf16[512,128]{0,1:T(8,128)(2,1)}, bf16[512,128]{0,1:T(8,128)(2,1)S(1)}, u32[]{:S(2)}) copy-start(bf16[512,128]{0,1:T(8,128)(2,1)S(1)} %fusion.152) | copy-start | bytes 393220
  113.6 21.2 %collective-permute-start.9 = (bf16[128,2048]{1,0:T(8,128)(2,1)}, bf16[128,2048]{1,0:T(8,128)(2,1)S(1)}, u32[]{:S(2)}, u32[]{:S(2)}) collective-permute-start(bf16[128,2048]{1,0:T(8,128)(2,1)} %collective-permute-done.8), channel_id=1, source_target_pairs={{0,8},{1,9},{2,10},{3,11},{4,12},{5,13},{6,14},{7,15},{8,0},{9,1},... | collective-permute-start | bytes 1572872 | tf_op jit(solution)/shard_map/ppermute | solution.py:27
  116.7 11.9 %collective-permute-start.28 = (f32[2,8]{1,0:T(2,128)S(1)}, f32[2,8]{1,0:T(2,128)S(1)}, u32[]{:S(2)}, u32[]{:S(2)}) collective-permute-start(f32[2,8]{1,0:T(2,128)S(1)} %broadcast_select_fusion.4), channel_id=1, source_target_pairs={{0,8},{4,12},{8,0},{12,4},{16,24},{20,28},{24,16},{28,20},{1,9},{5... | collective-permute-start | bytes 200 | tf_op jit(solution)/shard_map/ppermute | solution.py:27
  116.7 12.9 %collective-permute-start.29 = (f32[2,8]{1,0:T(2,128)S(1)}, f32[2,8]{1,0:T(2,128)S(1)}, u32[]{:S(2)}, u32[]{:S(2)}) collective-permute-start(f32[2,8]{1,0:T(2,128)S(1)} %broadcast_select_fusion.4), channel_id=1, source_target_pairs={{0,16},{4,20},{8,24},{12,28},{16,0},{20,4},{24,8},{28,12},{1,17},{... | collective-permute-start | bytes 200 | tf_op jit(solution)/shard_map/ppermute | solution.py:27
  128.6 3.6 collective-permute-start.30
  129.6 173.2 %collective-permute-start.31 = (bf16[512,128]{0,1:T(8,128)(2,1)S(1)}, bf16[512,128]{0,1:T(8,128)(2,1)}, u32[]{:S(2)}, u32[]{:S(2)}) collective-permute-start(bf16[512,128]{0,1:T(8,128)(2,1)S(1)} %fusion.152), channel_id=1, source_target_pairs={{0,4},{4,0},{8,12},{12,8},{16,20},{20,16},{24,28},{28,24},{1,5},{5... | collective-permute-start | bytes 393224 | tf_op jit(solution)/shard_map/ppermute | solution.py:27
  138.1 33.2 %all-to-all-start.4 = ((bf16[8,72,2048]{2,1,0:T(8,128)(2,1)}), bf16[8,72,2048]{2,1,0:T(8,128)(2,1)}, u32[]{:S(2)}, u32[]{:S(2)}) async-start(bf16[8,72,2048]{2,1,0:T(8,128)(2,1)} %fusion.51), calls=%async_computation.4 | async-start | bytes 4718592 | tf_op jit(solution)/shard_map/all_to_all | solution.py:228
  196.9 8.0 %all-to-all-start.7 = ((f32[8,2,72]{2,1,0:T(2,128)}), f32[8,2,72]{2,1,0:T(2,128)S(1)}, u32[]{:S(2)}, u32[]{:S(2)}) async-start(f32[8,2,72]{2,1,0:T(2,128)} %pad_maximum_fusion.21), calls=%async_computation.7 | async-start | bytes 16384 | tf_op jit(solution)/shard_map/all_to_all | solution.py:228
  206.3 8.4 %all-to-all-start = ((f32[8,1,144]{2,1,0:T(1,128)}), f32[8,1,144]{2,1,0:T(1,128)S(1)}, u32[]{:S(2)}, u32[]{:S(2)}) async-start(f32[8,1,144]{2,1,0:T(1,128)} %broadcast_in_dim.194), calls=%async_computation | async-start | bytes 16384 | tf_op jit(solution)/shard_map/all_to_all | solution.py:228
  225.9 33.0 %all-to-all-start.6 = ((bf16[8,72,2048]{2,1,0:T(8,128)(2,1)}), bf16[8,72,2048]{2,1,0:T(8,128)(2,1)}, u32[]{:S(2)}, u32[]{:S(2)}) async-start(bf16[8,72,2048]{2,1,0:T(8,128)(2,1)} %bitcast.212), calls=%async_computation.6 | async-start | bytes 4718592 | tf_op jit(solution)/shard_map/all_to_all | solution.py:228
  239.5 65.1 %collective-permute-start.19 = (f32[4,128]{1,0:T(4,128)}, f32[4,128]{1,0:T(4,128)}, u32[]{:S(2)}, u32[]{:S(2)}) collective-permute-start(f32[4,128]{1,0:T(4,128)} %get-tuple-element.94), channel_id=1, source_target_pairs={{0,8},{1,9},{2,10},{3,11},{4,12},{5,13},{6,14},{7,15},{8,0},{9,1},... | collective-permute-start | bytes 6152 | tf_op jit(solution)/shard_map/ppermute | solution.py:27
  258.9 33.1 %all-to-all-start.3 = ((bf16[8,72,2048]{2,1,0:T(8,128)(2,1)}), bf16[8,72,2048]{2,1,0:T(8,128)(2,1)}, u32[]{:S(2)}, u32[]{:S(2)}) async-start(bf16[8,72,2048]{2,1,0:T(8,128)(2,1)} %bitcast.213), calls=%async_computation.3 | async-start | bytes 4718592 | tf_op jit(solution)/shard_map/all_to_all | solution.py:228
  272.2 80.2 %collective-permute-start.22 = (bf16[2048,768]{1,0:T(8,128)(2,1)}, bf16[2048,768]{1,0:T(8,128)(2,1)}, u32[]{:S(2)}, u32[]{:S(2)}) collective-permute-start(bf16[2048,768]{1,0:T(8,128)(2,1)} %convolution_convert_fusion), channel_id=1, source_target_pairs={{0,1},{1,0},{2,3},{3,2},{4,5},{5,4},{6,7},{7,6},{8,9},{9,8},{10,11... | collective-permute-start | bytes 9437192 | tf_op jit(solution)/shard_map/ppermute | solution.py:27
  283.5 16.0 %collective-permute-start.12 = (bf16[128,2048]{1,0:T(8,128)(2,1)}, bf16[128,2048]{1,0:T(8,128)(2,1)}, u32[]{:S(2)}, u32[]{:S(2)}) collective-permute-start(bf16[128,2048]{1,0:T(8,128)(2,1)} %slice.168), channel_id=1, source_target_pairs={{0,8},{1,9},{2,10},{3,11},{4,12},{5,13},{6,14},{7,15},{8,0},{9,1},... | collective-permute-start | bytes 1572872 | tf_op jit(solution)/shard_map/ppermute | solution.py:27
  290.4 48.5 %collective-permute-start.23 = (bf16[384,2048]{1,0:T(8,128)(2,1)}, bf16[384,2048]{1,0:T(8,128)(2,1)}, u32[]{:S(2)}, u32[]{:S(2)}) collective-permute-start(bf16[384,2048]{1,0:T(8,128)(2,1)} %fusion.3), channel_id=1, source_target_pairs={{0,1},{1,0},{2,3},{3,2},{4,5},{5,4},{6,7},{7,6},{8,9},{9,8},{10,11... | collective-permute-start | bytes 4718600 | tf_op jit(solution)/shard_map/ppermute | solution.py:27
  296.2 37.5 %copy-start.18 = (bf16[128,2048]{1,0:T(8,128)(2,1)S(1)}, bf16[128,2048]{1,0:T(8,128)(2,1)}, u32[]{:S(2)}) copy-start(bf16[128,2048]{1,0:T(8,128)(2,1)} %param.16) | copy-start | bytes 1572868
  299.5 6.3 %collective-permute-start.20 = (f32[4,128]{1,0:T(4,128)}, f32[4,128]{1,0:T(4,128)S(1)}, u32[]{:S(2)}, u32[]{:S(2)}) collective-permute-start(f32[4,128]{1,0:T(4,128)} %get-tuple-element.95), channel_id=1, source_target_pairs={{0,16},{1,17},{2,18},{3,19},{4,20},{5,21},{6,22},{7,23},{8,24},{9,... | collective-permute-start | bytes 6152 | tf_op jit(solution)/shard_map/ppermute | solution.py:27
  302.8 5.1 %collective-permute-start.21 = (f32[4,128]{1,0:T(4,128)S(1)}, f32[4,128]{1,0:T(4,128)S(1)}, u32[]{:S(2)}, u32[]{:S(2)}) collective-permute-start(f32[4,128]{1,0:T(4,128)S(1)} %copy-done.81), channel_id=1, source_target_pairs={{0,24},{1,25},{2,26},{3,27},{4,28},{5,29},{6,30},{7,31},{8,16},{9,... | collective-permute-start | bytes 6152 | tf_op jit(solution)/shard_map/ppermute | solution.py:27
  304.7 21.8 %collective-permute-start.7 = (bf16[128,2048]{1,0:T(8,128)(2,1)}, bf16[128,2048]{1,0:T(8,128)(2,1)}, u32[]{:S(2)}, u32[]{:S(2)}) collective-permute-start(bf16[128,2048]{1,0:T(8,128)(2,1)} %slice.169), channel_id=1, source_target_pairs={{0,8},{1,9},{2,10},{3,11},{4,12},{5,13},{6,14},{7,15},{8,0},{9,1},... | collective-permute-start | bytes 1572872 | tf_op jit(solution)/shard_map/ppermute | solution.py:27
  305.9 27.8 %collective-permute-start.13 = (bf16[128,2048]{1,0:T(8,128)(2,1)}, bf16[128,2048]{1,0:T(8,128)(2,1)}, u32[]{:S(2)}, u32[]{:S(2)}) collective-permute-start(bf16[128,2048]{1,0:T(8,128)(2,1)} %fusion.43), channel_id=1, source_target_pairs={{0,16},{1,17},{2,18},{3,19},{4,20},{5,21},{6,22},{7,23},{8,24},{9,... | collective-permute-start | bytes 1572872 | tf_op jit(solution)/shard_map/ppermute | solution.py:27
  307.9 78.8 %collective-permute-start.32 = (bf16[512,128]{0,1:T(8,128)(2,1)}, bf16[512,128]{0,1:T(8,128)(2,1)S(1)}, u32[]{:S(2)}, u32[]{:S(2)}) collective-permute-start(bf16[512,128]{0,1:T(8,128)(2,1)} %fusion.100), channel_id=1, source_target_pairs={{0,8},{4,12},{8,16},{12,20},{16,24},{20,28},{1,9},{5,13},{9,17},{1... | collective-permute-start | bytes 393224 | tf_op jit(solution)/shard_map/ppermute | solution.py:33
  315.0 24.0 %copy-start.24 = (bf16[576,2048]{1,0:T(8,128)(2,1)S(1)}, bf16[576,2048]{1,0:T(8,128)(2,1)}, u32[]{:S(2)}) copy-start(bf16[576,2048]{1,0:T(8,128)(2,1)} %copy-done.23) | copy-start | bytes 7077892
  326.5 77.1 %collective-permute-start.33 = (bf16[512,128]{0,1:T(8,128)(2,1)}, bf16[512,128]{0,1:T(8,128)(2,1)}, u32[]{:S(2)}, u32[]{:S(2)}) collective-permute-start(bf16[512,128]{0,1:T(8,128)(2,1)} %fusion.100), channel_id=1, source_target_pairs={{0,16},{4,20},{8,24},{12,28},{1,17},{5,21},{9,25},{13,29},{2,18},{... | collective-permute-start | bytes 393224 | tf_op jit(solution)/shard_map/ppermute | solution.py:33
  335.7 1.2 collective-permute-start.14
  336.9 8.0 %collective-permute-start.15 = (f32[2048]{0:T(1024)S(1)}, f32[2048]{0:T(1024)S(1)}, u32[]{:S(2)}, u32[]{:S(2)}) collective-permute-start(f32[2048]{0:T(1024)S(1)} %add.405), channel_id=1, source_target_pairs={{0,2},{1,3},{2,0},{3,1},{4,6},{5,7},{6,4},{7,5},{8,10},{9,11},{10,... | collective-permute-start | bytes 24584 | tf_op jit(solution)/shard_map/ppermute | solution.py:27
  345.0 3.7 collective-permute-start.16
  348.7 3.7 collective-permute-start.17
  350.6 12.6 %collective-permute-start.25 = (bf16[128,2048]{1,0:T(8,128)(2,1)S(1)}, bf16[128,2048]{1,0:T(8,128)(2,1)S(1)}, u32[]{:S(2)}, u32[]{:S(2)}) collective-permute-start(bf16[128,2048]{1,0:T(8,128)(2,1)S(1)} %fusion.33), channel_id=1, source_target_pairs={{0,2},{1,3},{2,0},{3,1},{4,6},{5,7},{6,4},{7,5},{8,10},{9,11},{10,... | collective-permute-start | bytes 1572872 | tf_op jit(solution)/shard_map/ppermute | solution.py:27
  352.4 14.8 %collective-permute-start.24 = (bf16[128,2048]{1,0:T(8,128)(2,1)S(1)}, bf16[128,2048]{1,0:T(8,128)(2,1)S(1)}, u32[]{:S(2)}, u32[]{:S(2)}) collective-permute-start(bf16[128,2048]{1,0:T(8,128)(2,1)S(1)} %fusion.33), channel_id=1, source_target_pairs={{0,1},{1,0},{2,3},{3,2},{4,5},{5,4},{6,7},{7,6},{8,9},{9,8},{10,11... | collective-permute-start | bytes 1572872 | tf_op jit(solution)/shard_map/ppermute | solution.py:27
  352.4 12.9 %collective-permute-start.18 = (f32[2048]{0:T(1024)S(1)}, f32[2048]{0:T(1024)S(1)}, u32[]{:S(2)}, u32[]{:S(2)}) collective-permute-start(f32[2048]{0:T(1024)S(1)} %add.408), channel_id=1, source_target_pairs={{0,16},{4,20},{8,24},{12,28},{16,0},{20,4},{24,8},{28,12},{1,17},{... | collective-permute-start | bytes 24584 | tf_op jit(solution)/shard_map/ppermute | solution.py:27
  363.3 3.9 collective-permute-start.26
  365.3 38.3 %collective-permute-start.34 = (bf16[512,128]{0,1:T(8,128)(2,1)}, bf16[512,128]{0,1:T(8,128)(2,1)}, u32[]{:S(2)}, u32[]{:S(2)}) collective-permute-start(bf16[512,128]{0,1:T(8,128)(2,1)} %fusion.100), channel_id=1, source_target_pairs={{0,24},{4,28},{1,25},{5,29},{2,26},{6,30},{3,27},{7,31}} | collective-permute-start | bytes 393224 | tf_op jit(solution)/shard_map/ppermute | solution.py:33
  372.8 5.0 %collective-permute-start.47 = (f32[8]{0:T(128)S(1)}, f32[8]{0:T(128)S(1)}, u32[]{:S(2)}, u32[]{:S(2)}) collective-permute-start(f32[8]{0:T(128)S(1)} %convolution_reduce_fusion), channel_id=1, source_target_pairs={{0,4},{4,0},{8,12},{12,8},{16,20},{20,16},{24,28},{28,24},{1,5},{5... | collective-permute-start | bytes 104 | tf_op jit(solution)/shard_map/ppermute | solution.py:27
  375.6 6.5 %collective-permute-start.39 = (bf16[512,128]{0,1:T(8,128)(2,1)S(1)}, bf16[512,128]{0,1:T(8,128)(2,1)S(1)}, u32[]{:S(2)}, u32[]{:S(2)}) collective-permute-start(bf16[512,128]{0,1:T(8,128)(2,1)S(1)} %fusion.165), channel_id=1, source_target_pairs={{0,4},{4,0},{8,12},{12,8},{16,20},{20,16},{24,28},{28,24},{1,5},{5... | collective-permute-start | bytes 393224 | tf_op jit(solution)/shard_map/ppermute | solution.py:27
  377.8 4.2 collective-permute-start.48
  382.1 6.0 %collective-permute-start.49 = (f32[8]{0:T(128)S(1)}, f32[8]{0:T(128)S(1)}, u32[]{:S(2)}, u32[]{:S(2)}) collective-permute-start(f32[8]{0:T(128)S(1)} %add.467), channel_id=1, source_target_pairs={{0,16},{4,20},{8,24},{12,28},{16,0},{20,4},{24,8},{28,12},{1,17},{... | collective-permute-start | bytes 104 | tf_op jit(solution)/shard_map/ppermute | solution.py:27
  382.8 20.8 %collective-permute-start.40 = (bf16[512,128]{0,1:T(8,128)(2,1)}, bf16[512,128]{0,1:T(8,128)(2,1)}, u32[]{:S(2)}, u32[]{:S(2)}) collective-permute-start(bf16[512,128]{0,1:T(8,128)(2,1)} %fusion.106), channel_id=1, source_target_pairs={{8,0},{12,4},{16,8},{20,12},{24,16},{28,20},{9,1},{13,5},{17,9},{2... | collective-permute-start | bytes 393224 | tf_op jit(solution)/shard_map/ppermute | solution.py:33
  386.8 16.8 %collective-permute-start.41 = (bf16[512,128]{0,1:T(8,128)(2,1)}, bf16[512,128]{0,1:T(8,128)(2,1)}, u32[]{:S(2)}, u32[]{:S(2)}) collective-permute-start(bf16[512,128]{0,1:T(8,128)(2,1)} %fusion.106), channel_id=1, source_target_pairs={{16,0},{20,4},{24,8},{28,12},{17,1},{21,5},{25,9},{29,13},{18,2},{... | collective-permute-start | bytes 393224 | tf_op jit(solution)/shard_map/ppermute | solution.py:33
  388.6 15.0 %collective-permute-start.42 = (bf16[512,128]{0,1:T(8,128)(2,1)}, bf16[512,128]{0,1:T(8,128)(2,1)}, u32[]{:S(2)}, u32[]{:S(2)}) collective-permute-start(bf16[512,128]{0,1:T(8,128)(2,1)} %fusion.106), channel_id=1, source_target_pairs={{24,0},{28,4},{25,1},{29,5},{26,2},{30,6},{27,3},{31,7}} | collective-permute-start | bytes 393224 | tf_op jit(solution)/shard_map/ppermute | solution.py:33
  412.2 15.8 %collective-permute-start.45 = (bf16[512,128]{1,0:T(8,128)(2,1)}, bf16[512,128]{1,0:T(8,128)(2,1)}, u32[]{:S(2)}, u32[]{:S(2)}) collective-permute-start(bf16[512,128]{1,0:T(8,128)(2,1)} %fusion.26), channel_id=1, source_target_pairs={{0,1},{1,0},{2,3},{3,2},{4,5},{5,4},{6,7},{7,6},{8,9},{9,8},{10,11... | collective-permute-start | bytes 393224 | tf_op jit(solution)/shard_map/ppermute | solution.py:27
  422.8 25.7 %collective-permute-start.35 = (bf16[4,256,512]{2,1,0:T(8,128)(2,1)S(1)}, bf16[4,256,512]{2,1,0:T(8,128)(2,1)S(1)}, u32[]{:S(2)}, u32[]{:S(2)}) collective-permute-start(bf16[4,256,512]{2,1,0:T(8,128)(2,1)S(1)} %dynamic-slice_bitcast_fusion), channel_id=1, source_target_pairs={{0,4},{4,0},{8,12},{12,8},{16,20},{20,16},{24,28},{28,24},{1,5},{5... | collective-permute-start | bytes 3145736 | tf_op jit(solution)/shard_map/ppermute | solution.py:27
  424.7 4.9 %collective-permute-start.43 = (bf16[512,128]{1,0:T(8,128)(2,1)S(1)}, bf16[512,128]{1,0:T(8,128)(2,1)S(1)}, u32[]{:S(2)}, u32[]{:S(2)}) collective-permute-start(bf16[512,128]{1,0:T(8,128)(2,1)S(1)} %fusion.25), channel_id=1, source_target_pairs={{0,1},{1,0},{2,3},{3,2},{4,5},{5,4},{6,7},{7,6},{8,9},{9,8},{10,11... | collective-permute-start | bytes 393224 | tf_op jit(solution)/shard_map/ppermute | solution.py:27
  429.0 25.4 %collective-permute-start.46 = (bf16[512,128]{1,0:T(8,128)(2,1)S(1)}, bf16[512,128]{1,0:T(8,128)(2,1)S(1)}, u32[]{:S(2)}, u32[]{:S(2)}) collective-permute-start(bf16[512,128]{1,0:T(8,128)(2,1)S(1)} %add.459), channel_id=1, source_target_pairs={{0,2},{1,3},{2,0},{3,1},{4,6},{5,7},{6,4},{7,5},{8,10},{9,11},{10,... | collective-permute-start | bytes 393224 | tf_op jit(solution)/shard_map/ppermute | solution.py:27
  429.7 25.4 %collective-permute-start.44 = (bf16[512,128]{1,0:T(8,128)(2,1)S(1)}, bf16[512,128]{1,0:T(8,128)(2,1)S(1)}, u32[]{:S(2)}, u32[]{:S(2)}) collective-permute-start(bf16[512,128]{1,0:T(8,128)(2,1)S(1)} %add.456), channel_id=1, source_target_pairs={{0,2},{1,3},{2,0},{3,1},{4,6},{5,7},{6,4},{7,5},{8,10},{9,11},{10,... | collective-permute-start | bytes 393224 | tf_op jit(solution)/shard_map/ppermute | solution.py:27
  449.0 10.7 %collective-permute-start.36 = (bf16[256,512]{1,0:T(8,128)(2,1)S(1)}, bf16[256,512]{1,0:T(8,128)(2,1)S(1)}, u32[]{:S(2)}, u32[]{:S(2)}) collective-permute-start(bf16[256,512]{1,0:T(8,128)(2,1)S(1)} %get-tuple-element.60), channel_id=1, source_target_pairs={{0,8},{4,12},{8,0},{12,4},{16,24},{20,28},{24,16},{28,20},{1,9},{5... | collective-permute-start | bytes 786440 | tf_op jit(solution)/shard_map/ppermute | solution.py:27
  449.4 22.4 %collective-permute-start.37 = (bf16[256,512]{1,0:T(8,128)(2,1)S(1)}, bf16[256,512]{1,0:T(8,128)(2,1)S(1)}, u32[]{:S(2)}, u32[]{:S(2)}) collective-permute-start(bf16[256,512]{1,0:T(8,128)(2,1)S(1)} %get-tuple-element.62), channel_id=1, source_target_pairs={{0,16},{4,20},{8,24},{12,28},{16,0},{20,4},{24,8},{28,12},{1,17},{... | collective-permute-start | bytes 786440 | tf_op jit(solution)/shard_map/ppermute | solution.py:27
  453.9 23.3 %collective-permute-start.38 = (bf16[256,512]{1,0:T(8,128)(2,1)S(1)}, bf16[256,512]{1,0:T(8,128)(2,1)S(1)}, u32[]{:S(2)}, u32[]{:S(2)}) collective-permute-start(bf16[256,512]{1,0:T(8,128)(2,1)S(1)} %get-tuple-element.61), channel_id=1, source_target_pairs={{0,24},{4,28},{8,16},{12,20},{16,8},{20,12},{24,0},{28,4},{1,25},{... | collective-permute-start | bytes 786440 | tf_op jit(solution)/shard_map/ppermute | solution.py:27
  (87 other events, 497.5 us)

commit v2 on v1

v2 whole, which is shorter than its diff:
```python
import functools

import jax
import jax.numpy as jnp
from jax import lax
from jax.experimental import pallas as pl
from jax.experimental.pallas import tpu as pltpu
from jax.sharding import PartitionSpec as P

highest = lax.Precision.HIGHEST
epsilon = 1e-06
wide = jnp.float32
short = jnp.bfloat16
both = ("seq", "head")


def log2(number):
    return number.bit_length() - 1


def flipped(value, axis, mask):
    names = axis if isinstance(axis, tuple) else (axis,)
    size = 1
    for name in names:
        size = size * lax.axis_size(name)
    return lax.ppermute(value, axis, [(i, i ^ mask) for i in range(size)])


def shifted(value, axis, distance):
    size = lax.axis_size(axis)
    pairs = [(i, i + distance) for i in range(size) if 0 <= i + distance < size]
    return lax.ppermute(value, axis, pairs)


def summed(value, axis):
    size = lax.axis_size(axis)
    for bit in range(log2(size)):
        value = value + flipped(value, axis, 1 << bit)
    return value


light = pl.CostEstimate(flops=1, bytes_accessed=1, transcendentals=0)


def untouched(*refs):
    pass


def tied(value, *others):
    anywhere = pl.BlockSpec(memory_space=pl.ANY)
    return pl.pallas_call(
        untouched,
        out_shape=jax.ShapeDtypeStruct(value.shape, value.dtype),
        in_specs=[anywhere] * (1 + len(others)),
        out_specs=anywhere,
        input_output_aliases={0: 0},
        cost_estimate=light,
    )(value, *others)


def dot_nn(a, b, out=wide):
    return lax.dot_general(a, b, (((1,), (0,)), ((), ())), preferred_element_type=out)


def dot_nt(a, b, out=wide):
    return lax.dot_general(a, b, (((1,), (1,)), ((), ())), preferred_element_type=out)


def dot_tn(a, b, out=wide):
    return lax.dot_general(a, b, (((0,), (0,)), ((), ())), preferred_element_type=out)


def forward_kernel(heads, b_ref, c_ref, x_ref, row_ref, col_ref, y_ref, score_ref):
    step = pl.program_id(0)
    rows = b_ref.shape[0]

    @pl.when(step == 0)
    def _():
        score_ref[...] = dot_nt(c_ref[...], b_ref[...])

    scores = score_ref[...]
    keep = lax.broadcasted_iota(jnp.int32, (rows, rows), 0) >= lax.broadcasted_iota(
        jnp.int32, (rows, rows), 1
    )
    block = x_ref[...]
    width = block.shape[1]
    lane = lax.broadcasted_iota(jnp.int32, (rows, width), 1)
    head_lane = lax.broadcasted_iota(jnp.int32, col_ref.shape, 1)
    total = jnp.zeros((rows, width), wide)
    for k in range(heads):
        head = step * heads + k
        column = jnp.sum(jnp.where(head_lane == head, col_ref[...], 0.0), axis=1, keepdims=True)
        line = row_ref[pl.ds(head, 1), :]
        decay = jnp.where(keep, jnp.exp(jnp.minimum(column - line, 0.0)), 0.0)
        mine = (lane // (width // heads)) == k
        total = total + dot_nn(
            (decay * scores).astype(short), jnp.where(mine, block, jnp.zeros_like(block))
        )
    y_ref[...] = total


def backward_kernel(
    heads, b_ref, c_ref, x_ref, g_ref, row_ref, col_ref, *refs
):
    dx_ref, tsum_ref, ssum_ref, db_ref, dc_ref, score_ref, mask_ref = refs[-7:]
    step = pl.program_id(0)
    rows = b_ref.shape[0]

    @pl.when(step == 0)
    def _():
        score_ref[...] = dot_nt(b_ref[...], c_ref[...])
        mask_ref[...] = jnp.zeros_like(mask_ref)
        ssum_ref[...] = jnp.zeros_like(ssum_ref)

    scores = score_ref[...]
    keep = lax.broadcasted_iota(jnp.int32, (rows, rows), 0) <= lax.broadcasted_iota(
        jnp.int32, (rows, rows), 1
    )
    values = x_ref[...]
    grads = g_ref[...]
    width = values.shape[1]
    lane = lax.broadcasted_iota(jnp.int32, (rows, width), 1)
    head_lane = lax.broadcasted_iota(jnp.int32, col_ref.shape, 1)
    total = jnp.zeros((rows, width), wide)
    for k in range(heads):
        head = step * heads + k
        column = jnp.sum(jnp.where(head_lane == head, col_ref[...], 0.0), axis=1, keepdims=True)
        line = row_ref[pl.ds(head, 1), :]
        decay = jnp.where(keep, jnp.exp(jnp.minimum(line - column, 0.0)), 0.0)
        mine = (lane // (width // heads)) == k
        head_grads = jnp.where(mine, grads, jnp.zeros_like(grads))
        pair = decay * dot_nt(values, head_grads)
        mask_ref[...] += pair
        full = pair * scores
        tsum_ref[pl.ds(head, 1), :] = jnp.sum(full, axis=0, keepdims=True)
        ssum_ref[...] += jnp.where(head_lane == head, jnp.sum(full, axis=1, keepdims=True), 0.0)
        total = total + dot_nn((decay * scores).astype(short), head_grads)
    dx_ref[...] = total

    @pl.when(step == pl.num_programs(0) - 1)
    def _():
        mask = mask_ref[...].astype(short)
        db_ref[...] = dot_nn(mask, c_ref[...])
        dc_ref[...] = dot_tn(mask, b_ref[...])


inside = pl.BlockSpec(memory_space=pltpu.VMEM)
anywhere = pl.BlockSpec(memory_space=pl.ANY)
scalars = pl.BlockSpec(memory_space=pltpu.SMEM)
lanes = 128
mega = 1024 * 1024


def pack_kernel(count, cap, tok, experts, pick_ref, bundle_ref, *refs):
    outs, hit_ref = refs[-1 - count : -1], refs[-1]
    width = bundle_ref.shape[1]
    tail = bundle_ref[2 * tok :, :]
    table = [tail[:, i * tok : (i + 1) * tok] for i in range(2 * experts // 16)]
    table = jnp.concatenate(table, axis=0).astype(wide)
    line = lax.broadcasted_iota(jnp.int32, (experts, tok), 0)
    slot = lax.broadcasted_iota(jnp.int32, (cap, tok), 0).astype(wide)
    plain, scaled = [], []
    for k in range(count):
        mine = line == pick_ref[k]
        rank = jnp.sum(jnp.where(mine, table[:experts], 0.0), axis=0, keepdims=True)
        scale = jnp.sum(jnp.where(mine, table[experts:], 0.0), axis=0, keepdims=True)
        plain.append(jnp.where(rank == slot, 1.0, 0.0))
        scaled.append(jnp.where(rank == slot, scale, 0.0))
    plain = jnp.concatenate(plain, axis=0).astype(short)
    scaled = jnp.concatenate(scaled, axis=0).astype(short)
    hit_ref[...] = plain
    rows = dot_nn(plain, bundle_ref[:tok, :])
    grads = dot_nn(scaled, bundle_ref[tok : 2 * tok, :])
    for k in range(count):
        outs[k][:, :width] = rows[k * cap : (k + 1) * cap].astype(short)
        outs[k][:, width:] = grads[k * cap : (k + 1) * cap].astype(short)


def pack(pick, bundle, cap, tok, experts, ties):
    count, width = pick.shape[0], bundle.shape[1]
    out = pl.pallas_call(
        functools.partial(pack_kernel, count, cap, tok, experts),
        in_specs=[scalars, inside] + [anywhere] * len(ties),
        out_specs=[inside] * (count + 1),
        out_shape=[jax.ShapeDtypeStruct((cap, 2 * width), short)] * count
        + [jax.ShapeDtypeStruct((count * cap, tok), short)],
        compiler_params=pltpu.CompilerParams(vmem_limit_bytes=32 * mega),
        cost_estimate=light,
    )(pick, bundle, *ties)
    return list(out[:count]), out[count]


def expert_kernel(count, first, expert_ref, *refs):
    pieces, weights = refs[:count], refs[count : count + 4]
    outs = refs[-(count + 12) :]
    rows_out, outs = outs[:count], outs[count:]
    all_refs, (gu0, down0, gu1, down1), total_ref, sems = outs[:6], outs[6:10], outs[10], outs[11]
    copies = []
    for i, held in enumerate((gu0, down0, gu1, down1)):
        copies.append(pltpu.make_async_copy(weights[i], held, sems.at[i]))
        copies[i].start()
    cap = pieces[0].shape[0]
    width = pieces[0].shape[1] // 2
    half = down0.shape[0]
    both_rows = jnp.concatenate([piece[...].astype(wide) for piece in pieces], axis=0).astype(short)
    all_refs[0][...] = both_rows[:, :width]
    all_refs[1][...] = both_rows[:, width:]
    rows, grads = all_refs[0], all_refs[1]
    prob = jnp.zeros((rows.shape[0], 1), wide)
    for side in range(2):
        gate_up, down = ((gu0, down0), (gu1, down1))[side]
        copies[2 * side].wait()
        pre = dot_nn(rows[...], gate_up[...])
        copies[2 * side + 1].wait()
        back = dot_nt(grads[...], down[...])
        gate_pre, up_pre = pre[:, :half], pre[:, half:]
        sig = 1.0 / (1.0 + jnp.exp(-gate_pre))
        swish = gate_pre * sig
        active = (swish * up_pre).astype(short)
        prob = prob + jnp.sum(active.astype(wide) * back, axis=1, keepdims=True)
        all_refs[2 + side][...] = active
        d_pre = all_refs[4 + side]
        d_pre[:, :half] = (back * up_pre * sig * (1.0 + gate_pre * (1.0 - sig))).astype(short)
        d_pre[:, half:] = (back * swish).astype(short)
        term = dot_nt(d_pre[...], gate_up[...])
        if side == 0:
            total_ref[...] = term
        else:
            total_ref[...] += term
    lane = lax.broadcasted_iota(jnp.int32, (cap, lanes), 1)
    for k in range(count):
        span = slice(k * cap, (k + 1) * cap)
        rows_out[k][:, :width] = total_ref[span, :].astype(short)
        rows_out[k][:, width:] = jnp.where(lane == expert_ref[0], prob[span], 0.0).astype(short)


def expert_rows(expert, pieces, weights, index, blocks, kept, ties):
    count, cap = len(pieces), pieces[0].shape[0]
    width = pieces[0].shape[1] // 2
    rows = count * cap
    half = weights[0][1].shape[0]
    widths = (width, width, half, half, 2 * half, 2 * half)
    given = list(kept) if kept else []
    aliases = {1 + count + 4 + i: count + i for i in range(len(given))}
    out = pl.pallas_call(
        functools.partial(expert_kernel, count, not kept),
        grid=(1,),
        in_specs=[scalars]
        + [pl.BlockSpec((cap, 2 * width), lambda i: (0, 0))] * count
        + [anywhere] * (4 + len(given) + len(ties)),
        out_specs=[pl.BlockSpec((cap, width + lanes), lambda i: (0, 0))] * count
        + [pl.BlockSpec((rows, w), lambda i: (index, 0)) for w in widths],
        out_shape=[jax.ShapeDtypeStruct((cap, width + lanes), short)] * count
        + [jax.ShapeDtypeStruct((blocks * rows, w), short) for w in widths],
        scratch_shapes=[
            pltpu.VMEM((width, 2 * half), short),
            pltpu.VMEM((half, width), short),
            pltpu.VMEM((width, 2 * half), short),
            pltpu.VMEM((half, width), short),
            pltpu.VMEM((rows, width), wide),
            pltpu.SemaphoreType.DMA((4,)),
        ],
        input_output_aliases=aliases,
        compiler_params=pltpu.CompilerParams(vmem_limit_bytes=48 * mega),
        cost_estimate=light,
    )(expert, *pieces, *weights[0], *weights[1], *given, *ties)
    return out[:count], out[count:]


def weight_kernel(joined, rows_ref, grads_ref, act_ref, pre_ref, *refs):
    up = dot_tn(rows_ref[...], pre_ref[...])
    half = act_ref.shape[1]
    if joined:
        gate_out, up_out, down_out = refs[-3:]
        other = refs[0][...].astype(wide)
        up = up + other[:, : 2 * half]
        down = dot_tn(act_ref[...], grads_ref[...]) + other[:, 2 * half :].T
        gate_out[0] = up[:, :half].astype(short)
        up_out[0] = up[:, half:].astype(short)
        down_out[0] = down.astype(short)
    else:
        refs[-1][:, : 2 * half] = up.astype(short)
        refs[-1][:, 2 * half :] = dot_tn(grads_ref[...], act_ref[...]).astype(short)


def weight_terms(rows, grads, active, pre, others, ties):
    count, width = rows.shape
    half = active.shape[1]
    tile = min(256, width)
    column = pl.BlockSpec((count, tile), lambda i: (0, i))
    in_specs = [column, column]
    in_specs += [pl.BlockSpec(v.shape, lambda i: (0, 0)) for v in (active, pre)]
    term_spec = pl.BlockSpec((tile, 3 * half), lambda i: (i, 0))
    if others:
        in_specs.append(term_spec)
        out_specs = [pl.BlockSpec((1, tile, half), lambda i: (0, i, 0))] * 2
        out_specs.append(pl.BlockSpec((1, half, tile), lambda i: (0, 0, i)))
        out_shape = [(1, width, half), (1, width, half), (1, half, width)]
    else:
        out_specs = [term_spec]
        out_shape = [(width, 3 * half)]
    return pl.pallas_call(
        functools.partial(weight_kernel, bool(others)),
        grid=(width // tile,),
        in_specs=in_specs + [anywhere] * len(ties),
        out_specs=out_specs,
        out_shape=[jax.ShapeDtypeStruct(v, short) for v in out_shape],
        compiler_params=pltpu.CompilerParams(vmem_limit_bytes=40 * mega),
        cost_estimate=pl.CostEstimate(flops=4 * 10**9, bytes_accessed=1, transcendentals=0),
    )(rows, grads, active, pre, *others, *ties)


def scan_blocks(rows, state, width, heads_local):
    whole = pl.BlockSpec((rows, state), lambda i: (0, 0))
    column = pl.BlockSpec((rows, width), lambda i: (0, i))
    lines = pl.BlockSpec((heads_local, rows), lambda i: (0, 0))
    columns = pl.BlockSpec((rows, heads_local), lambda i: (0, 0))
    return whole, column, lines, columns


def scan_forward(b, c, x, lines, columns):
    rows, state = b.shape
    inner = x.shape[1]
    heads_local = columns.shape[1]
    width = 2 * (inner // heads_local)
    whole, column, line_spec, column_spec = scan_blocks(rows, state, width, heads_local)
    return pl.pallas_call(
        functools.partial(forward_kernel, 2),
        grid=(heads_local // 2,),
        in_specs=[whole, whole, column, line_spec, column_spec],
        out_specs=column,
        out_shape=jax.ShapeDtypeStruct((rows, inner), wide),
        scratch_shapes=[pltpu.VMEM((rows, rows), wide)],
        compiler_params=pltpu.CompilerParams(vmem_limit_bytes=24 * 1024 * 1024),
        cost_estimate=light,
    )(b, c, x, lines, columns)


def scan_backward(b, c, x, g, lines, columns, *ties):
    rows, state = b.shape
    inner = x.shape[1]
    heads_local = columns.shape[1]
    width = 2 * (inner // heads_local)
    whole, column, line_spec, column_spec = scan_blocks(rows, state, width, heads_local)
    return pl.pallas_call(
        functools.partial(backward_kernel, 2),
        grid=(heads_local // 2,),
        in_specs=[whole, whole, column, column, line_spec, column_spec]
        + [pl.BlockSpec(memory_space=pl.ANY)] * len(ties),
        out_specs=[column, line_spec, column_spec, whole, whole],
        out_shape=[
            jax.ShapeDtypeStruct((rows, inner), wide),
            jax.ShapeDtypeStruct((heads_local, rows), wide),
            jax.ShapeDtypeStruct((rows, heads_local), wide),
            jax.ShapeDtypeStruct((rows, state), wide),
            jax.ShapeDtypeStruct((rows, state), wide),
        ],
        scratch_shapes=[pltpu.VMEM((rows, rows), wide), pltpu.VMEM((rows, rows), wide)],
        compiler_params=pltpu.CompilerParams(vmem_limit_bytes=32 * 1024 * 1024),
        cost_estimate=pl.CostEstimate(flops=2 * 10**9, bytes_accessed=1, transcendentals=0),
    )(b, c, x, g, lines, columns, *ties)


def shards(
    hidden,
    norm_gain,
    expert_choice,
    route_weight,
    gate_weight,
    up_weight,
    down_weight,
    layer_grad,
    scan_input,
    state_input,
    state_output,
    log_decay,
    skip_gain,
    out_weight,
):
    seq_size, head_size = lax.axis_size("seq"), lax.axis_size("head")
    devices = seq_size * head_size
    experts = devices // 2
    tok, model_width = hidden.shape
    top_count = expert_choice.shape[1]
    cap = 9 * tok * top_count // (8 * experts)
    cap = (cap + 7) // 8 * 8
    groups = 1 << ((log2(devices)) // 2)
    plane = devices // groups
    plane_experts = plane // 2
    seq_place, head_place = lax.axis_index("seq"), lax.axis_index("head")
    place = seq_place * head_size + head_place
    group = place // plane

    def across(value, mask):
        return flipped(value, both, mask * plane)

    def spread(first):
        rows = [first]
        for m in range(1, groups):
            low = m & -m
            rows.append(across(rows[m ^ low], low))
        return rows

    chip = (place % plane) // 2

    def within(value, mask):
        return flipped(value, both, 2 * mask)

    seq_rows, inner_width = scan_input.shape
    heads_local = log_decay.shape[1]
    head_dim = inner_width // heads_local
    inner_seq = 1 << (log2(seq_size) // 2)
    outer_seq = seq_size // inner_seq
    inner_place, outer_place = seq_place % inner_seq, seq_place // inner_seq

    choice_t = expert_choice.T
    named = choice_t[None, :, :] == jnp.arange(experts, dtype=jnp.int32)[:, None, None]
    chosen = jnp.any(named, axis=1)
    before = jnp.arange(tok)[:, None] < jnp.arange(tok)[None, :]
    rank = dot_nn(chosen.astype(short), before.astype(short))
    rank = jnp.where(chosen, rank, -1.0).astype(short)
    route_t = route_weight.T.astype(wide)
    prob = jnp.sum(jnp.where(named, route_t[None], 0.0), axis=1).astype(short)
    tables = jnp.concatenate([rank, prob], axis=0)
    pieces = [tables[i : i + 16] for i in range(0, 2 * experts, 16)]
    pieces.append(jnp.zeros((16, model_width - tok * len(pieces)), short))
    table_rows = jnp.concatenate(pieces, axis=1)

    hidden_wide = hidden.astype(wide)
    inverse = lax.rsqrt(jnp.mean(hidden_wide * hidden_wide, axis=1, keepdims=True) + epsilon)
    normalized = hidden_wide * inverse
    normed = (normalized * norm_gain[None, :]).astype(short)
    bundles = spread(jnp.concatenate([normed, layer_grad, table_rows], axis=0))

    gate_up = jnp.concatenate([gate_weight[0], up_weight[0]], axis=1)

    order = jnp.arange(plane_experts, dtype=jnp.int32) ^ chip
    selected = group * plane_experts + order
    own_expert = selected[:1]

    hits, received, returning = [], [], []
    kept = None

    def dispatch(m):
        ties = []
        if m == 1:
            ties = [received[0][1]]
        elif m == 2:
            ties = [received[1][1]]
        elif m > 2:
            ties = [*received[m - 2], returning[m - 3][0]]
        sent, hit = pack(selected, bundles[m], cap, tok, experts, ties)
        hits.append(hit)
        pieces = [sent[0]]
        for k in range(1, plane_experts):
            outgoing = sent[k]
            if m == groups - 1 and k == plane_experts - 1:
                outgoing = tied(outgoing, returning[m - 2][0])
            pieces.append(within(outgoing, k))
        received.append(pieces)

    for m in range(min(3, groups)):
        dispatch(m)
    weights = [(gate_up, down_weight[0])]
    weights.append(
        (
            flipped(tied(gate_up, *received[0][1:]), "head", 1),
            flipped(tied(down_weight[0], *received[0][1:]), "head", 1),
        )
    )

    lower = jnp.arange(seq_rows)[:, None] >= jnp.arange(seq_rows)[None, :]
    lower_ones = lower.astype(wide)
    cumulative = jnp.dot(lower_ones, log_decay, precision=highest)
    cumulative_t = cumulative.T
    total_decay = cumulative[-1]
    head_of = (jnp.arange(inner_width) // head_dim)[None, :] == jnp.arange(heads_local)[:, None]
    expand = head_of.astype(wide)

    def expanded(value):
        return jnp.dot(value, expand, precision=highest)

    from_start = expanded(jnp.exp(cumulative))
    to_end = expanded(jnp.exp(total_decay[None, :] - cumulative))
    skip_row = expanded(skip_gain[None, :])
    values = scan_input.astype(wide)
    values_end = (values * to_end).astype(short)
    def columns_of(logs, valid):
        factors = jnp.exp(jnp.minimum(jnp.stack(logs, axis=0), 0.0))
        factors = jnp.where(jnp.stack([jnp.asarray(v) for v in valid])[:, None], factors, 0.0)
        return lax.dot_general(
            expand, factors, (((0,), (1,)), ((), ())), precision=highest,
            preferred_element_type=wide,
        )

    def combined(pieces, columns, first, step):
        total = jnp.zeros((inner_width, state_input.shape[1]), wide)
        for k, piece in enumerate(pieces):
            place_of = first + step * k
            total = total + columns[:, place_of : place_of + 1] * piece.astype(wide)
        return total

    def thirds(value, width):
        high = lax.reduce_precision(value, 8, 7)
        middle = lax.reduce_precision(value - high, 8, 7)
        rows = jnp.concatenate([high, middle, value - high - middle], axis=0)
        below = (rows.shape[0] + 15) // 16 * 16 - rows.shape[0]
        return jnp.pad(rows, ((0, below), (0, width - rows.shape[1]))).astype(short)

    def joined_thirds(rows, count, width):
        rows = rows[: 3 * count, :width].astype(wide)
        return rows[:count] + rows[count : 2 * count] + rows[2 * count :]

    start = outer_place * inner_seq
    local_state = tied(dot_tn(values_end, state_input, short), received[0][1])
    message = jnp.concatenate([local_state, thirds(total_decay[None, :], lanes)], axis=0)
    messages = [message] + [flipped(message, "seq", m) for m in range(1, inner_seq)]
    inner_totals = jnp.zeros((inner_seq, heads_local), wide)
    for m in range(inner_seq):
        piece = joined_thirds(messages[m][inner_width:], 1, heads_local)
        inner_totals = lax.dynamic_update_slice(inner_totals, piece, (inner_place ^ m, 0))
    inner_ended = jnp.concatenate(
        [jnp.zeros((1, heads_local), wide), jnp.cumsum(inner_totals, axis=0)], axis=0
    )

    def inner_before(index):
        return lax.dynamic_index_in_dim(inner_ended, index, 0, False)

    logs, valid = [], []
    for m in range(inner_seq):
        source = inner_place ^ m
        logs.append(inner_before(inner_place) - inner_before(source + 1))
        logs.append(inner_before(inner_seq) - inner_before(source + 1))
        valid.extend([source < inner_place, True])
    columns = columns_of(logs, valid)
    states = [v[:inner_width] for v in messages]
    state_in = combined(states, columns, 0, 2)
    for m in range(min(2, groups)):
        rows, kept = expert_rows(own_expert, received[m], weights, m, groups, kept, [])
        returning.append(rows)

    message = jnp.concatenate(
        [combined(states, columns, 1, 2).astype(short), thirds(inner_totals, lanes)], axis=0
    )
    message = tied(message, returning[-1][0])
    messages = [message] + [flipped(message, "seq", m * inner_seq) for m in range(1, outer_seq)]
    totals = jnp.zeros((seq_size, heads_local), wide)
    for m in range(outer_seq):
        piece = joined_thirds(messages[m][inner_width:], inner_seq, heads_local)
        totals = lax.dynamic_update_slice(totals, piece, ((outer_place ^ m) * inner_seq, 0))
    ended = jnp.concatenate(
        [jnp.zeros((1, heads_local), wide), jnp.cumsum(totals, axis=0)], axis=0
    )

    def before_of(index):
        return lax.dynamic_index_in_dim(ended, jnp.clip(index, 0, seq_size), 0, False)

    logs, valid = [], []
    for m in range(1, outer_seq):
        source = outer_place ^ m
        logs.append(before_of(seq_place) - before_of((source + 1) * inner_seq))
        valid.append(source < outer_place)
    columns = columns_of(logs, valid)
    state_in = state_in + combined([v[:inner_width] for v in messages[1:]], columns, 0, 1)

    logs, valid = [], []
    for m in range(inner_seq):
        source = start + (inner_place ^ m)
        logs.append(before_of(source) - before_of(seq_place + 1))
        logs.append(before_of(source) - before_of(start))
        valid.extend([source > seq_place, True])
    for k in range(1, outer_seq):
        logs.append(before_of(start + k * inner_seq) - before_of(seq_place + 1))
        valid.append(True)
    adjoint_columns = columns_of(logs, valid)

    state_short = state_in.astype(short)
    read_state = dot_nt(state_output, state_short) * from_start
    y_inner = scan_forward(state_input, state_output, scan_input, cumulative_t, cumulative)
    y_rounded = (y_inner + read_state + skip_row * values).astype(short)


    for m in range(2, groups):
        if m >= 3:
            dispatch(m)
        rows, kept = expert_rows(own_expert, received[m], weights, m, groups, kept, [])
        returning.append(rows)

    partial = [None] * groups
    for m in reversed(range(groups)):
        outgoing = list(returning[m])
        if m < groups - 1:
            after = partial[m + 2] if m < groups - 2 else returning[groups - 1][0]
            outgoing = outgoing[:1] + [tied(v, after) for v in outgoing[1:]]
        back = outgoing[:1] + [within(outgoing[k], k) for k in range(1, plane_experts)]
        partial[m] = dot_tn(hits[m], jnp.concatenate(back, axis=0))

    other_terms = weight_terms(kept[0], kept[1], kept[3], kept[5], (), [partial[0], y_rounded])[0]
    partial[0] = tied(partial[0], other_terms)

    bit = 1
    tree = {m: partial[m] for m in range(groups)}
    while bit < groups:
        moved = {m: across(tree[m].astype(short), bit) for m in tree if m & bit}
        tree = {m: tree[m] + moved[m ^ bit].astype(wide) for m in tree if not m & bit}
        bit = bit * 2
    d_normed = tree[0][:, :model_width]

    prob_tokens = tree[0][:, model_width : model_width + experts].T
    d_route = jnp.sum(jnp.where(named, prob_tokens[:, None, :], 0.0), axis=0)
    d_route_weight = (d_route / route_t).T.astype(short)

    gain_scaled = norm_gain[None, :] * d_normed
    centered = jnp.mean(gain_scaled * normalized, axis=1, keepdims=True)
    d_hidden = (
        layer_grad.astype(wide) + inverse * (gain_scaled - normalized * centered)
    ).astype(short)
    gain_part = jnp.sum(d_normed * normalized, axis=0)

    gain_rows = thirds(gain_part[None, :], model_width)
    blocks = {0: jnp.concatenate([d_hidden, gain_rows], axis=0)}
    for k in reversed(range(log2(head_size))):
        blocks.update({m ^ (1 << k): flipped(v, "head", 1 << k) for m, v in blocks.items()})
    cotangent = jnp.zeros((seq_rows, model_width), short)
    gains = jnp.zeros((head_size, model_width), wide)
    for m, value in blocks.items():
        spot = head_place ^ m
        cotangent = lax.dynamic_update_slice(cotangent, value[:tok], (spot * tok, 0))
        gains = lax.dynamic_update_slice(gains, joined_thirds(value[tok:], 1, model_width), (spot, 0))
    grad = dot_nn(cotangent, out_weight, short)
    grad_wide = grad.astype(wide)
    grad_start = (grad_wide * from_start).astype(short)
    local_adjoint = dot_tn(grad_start, state_output, short)

    block = model_width // seq_size
    chosen_cot = {}
    for m in range(inner_seq):
        columns = [
            lax.dynamic_slice(
                cotangent, (0, (o * inner_seq + (inner_place ^ m)) * block), (seq_rows, block)
            )
            for o in range(outer_seq)
        ]
        chosen_cot[m] = jnp.concatenate(columns, axis=1)
    adjoints = [local_adjoint] + [flipped(local_adjoint, "seq", m) for m in range(1, inner_seq)]
    adjoint = combined(adjoints, adjoint_columns, 0, 2)
    part_y = tied(y_rounded, local_adjoint)
    sent_products = [dot_tn(part_y, chosen_cot[m], short) for m in range(1, inner_seq)]
    moved = [flipped(v, "seq", m + 1) for m, v in enumerate(sent_products)]
    dx_inner, later_sum, earlier_sum, db_inner, dc_inner = scan_backward(
        state_input, state_output, scan_input, grad, cumulative_t, cumulative,
        sent_products[0],
    )
    adjoints[0] = tied(adjoints[0], dx_inner)
    joined = combined(adjoints, adjoint_columns, 1, 2).astype(short)
    later = [shifted(joined, "seq", -k * inner_seq) for k in range(1, outer_seq)]
    other_terms = flipped(tied(other_terms, cotangent), "head", 1)
    product = dot_tn(tied(part_y, joined), chosen_cot[0])
    for value in moved:
        product = product + value.astype(wide)
    adjoint = adjoint + combined(later, adjoint_columns, 2 * inner_seq, 1)
    adjoint_short = adjoint.astype(short)
    product_short = product.astype(short)
    moved = []
    for m in range(1, outer_seq):
        piece = lax.dynamic_slice(
            product_short, (0, (outer_place ^ m) * block), (inner_width, block)
        )
        moved.append(flipped(piece, "seq", m * inner_seq))

    read_adjoint = dot_nt(state_input, adjoint_short) * to_end
    d_scan_input = (dx_inner + read_adjoint + skip_row * grad_wide).astype(short)
    input_part = db_inner + dot_nn(values_end, adjoint_short)
    output_part = dc_inner + dot_nn(grad_start, state_short)
    shared = jnp.concatenate([input_part, output_part], axis=0).astype(short)
    d_gate_weight, d_up_weight, d_down_weight = weight_terms(
        kept[0], kept[1], kept[2], kept[4], (other_terms,), [shared]
    )
    for k in range(log2(head_size)):
        other = flipped(shared, "head", 1 << k)
        if k == log2(head_size) - 1:
            shared = tied(shared, d_down_weight)
        shared = shared + other
    shared = shared.astype(wide)
    d_out = lax.dynamic_slice(product, (0, outer_place * block), (inner_width, block))
    d_out = tied(d_out, d_down_weight)
    for value in moved:
        d_out = d_out + value.astype(wide)
    d_out_weight = d_out.T.astype(short)
    d_state_input, d_state_output = shared[:seq_rows], shared[seq_rows:]

    def head_sum(value):
        return jnp.dot(value, expand.T, precision=highest)

    skip_part = jnp.sum(head_sum(values * grad_wide), axis=0)
    skip_part = jnp.pad(skip_part, (0, lanes - heads_local))
    tail_sum = jnp.concatenate([jnp.sum(gains, axis=0), skip_part], axis=0)
    tail_sum = summed(tied(tail_sum, adjoint_short), "seq")
    d_norm_gain = tail_sum[:model_width]
    d_skip_gain = tail_sum[model_width : model_width + heads_local]
    growth = jnp.exp(total_decay)
    from_past = head_sum(read_state * grad_wide)
    to_future = head_sum(read_adjoint * values)
    corner = growth * jnp.sum(
        (state_in * adjoint).reshape(heads_local, head_dim * state_input.shape[1]), axis=1
    )
    forward_part = later_sum.T - earlier_sum + from_past
    d_log_decay = (
        lax.dot_general(
            lower_ones, forward_part, (((0,), (0,)), ((), ())),
            precision=highest, preferred_element_type=wide,
        )
        + jnp.dot(lower_ones - jnp.eye(seq_rows, dtype=wide), to_future, precision=highest)
        + corner[None, :]
    )
    return (
        d_hidden,
        d_norm_gain,
        d_route_weight,
        d_gate_weight,
        d_up_weight,
        d_down_weight,
        d_out_weight,
        d_scan_input,
        d_state_input,
        d_state_output,
        d_log_decay,
        d_skip_gain,
    )


def solution(mesh):
    in_specs = (
        P(("seq", "head"), None),
        P(),
        P(("seq", "head"), None),
        P(("seq", "head"), None),
        P(("seq", "head"), None, None),
        P(("seq", "head"), None, None),
        P(("seq", "head"), None, None),
        P(("seq", "head"), None),
        P("seq", "head"),
        P("seq", None),
        P("seq", None),
        P("seq", "head"),
        P("head"),
        P(None, "head"),
    )
    out_specs = (
        P(("seq", "head"), None),
        P(),
        P(("seq", "head"), None),
        P(("seq", "head"), None, None),
        P(("seq", "head"), None, None),
        P(("seq", "head"), None, None),
        P("seq", "head"),
        P("seq", "head"),
        P("seq", None),
        P("seq", None),
        P("seq", "head"),
        P("head"),
    )
    return jax.shard_map(shards, mesh=mesh, in_specs=in_specs, out_specs=out_specs, check_vma=False)
```

time: 487 us -> 391 us (0.80)
  Pallas kernels: 7.86 us -> 85 us
  matrix products: 117 us -> 40.4 us
  waiting for transfers between devices: 142 us -> 83.6 us
  starting transfers between devices: 104 us -> 60.9 us
  local copies, waits for them, and re-layouts: 49.9 us -> 67.8 us
  other arithmetic: 54.8 us -> 44 us
    pallas_call x0 -> x32, Pallas kernels: none -> 77.2 us  [the longest x4 43.7 us: expert_rows(): pl.pallas_call(functools.partial(expert_kernel, count, not kept), grid=(1...]
    unnamed x186 -> x228, local copies, waits for them, and re-layouts: 8.44 us -> 46.2 us
    ppermute x44 -> x50, waiting for transfers between devices: 117 us -> 79.4 us  [flipped(): return lax.ppermute(value, axis, [(i, i ^ mask) for i in range(size)])]
    dot_general x10 -> x2, matrix products: 41.5 us -> 6.15 us  [dot_nt(): lax.dot_general(a, b, (((1,), (1,)), ((), ())), preferred_element_type=out)]
    all_to_all x8 -> x0, starting transfers between devices: 34.3 us -> none  [exchanged(): lax.all_to_all(value, both, split_axis=0, concat_axis=0, tiled=True, axis...]
    dot_general x12 -> x4, matrix products: 34.5 us -> 5.79 us  [dot_nn(): lax.dot_general(a, b, (((1,), (0,)), ((), ())), preferred_element_type=out)]
    all_to_all x8 -> x0, waiting for transfers between devices: 25.2 us -> none  [exchanged(): lax.all_to_all(value, both, split_axis=0, concat_axis=0, tiled=True, axis...]
    dot_general x9 -> x8, matrix products: 36.7 us -> 16.4 us  [dot_tn(): lax.dot_general(a, b, (((0,), (0,)), ((), ())), preferred_element_type=out)]
  transfers between devices with their start and end apart: 58 -> 53, of which waited for: 23 -> 20; matrix products, arithmetic and copies ran while one was open for 42% -> 23% of each run, Pallas kernels for 2% -> 19%
where the time goes in v2:
time: 391 us; the launch traced here: 384 us
  Pallas kernels  85 us (22%)
  waiting for transfers between devices  83.6 us (21%)
  local copies, waits for them, and re-layouts  67.8 us (17%)
  starting transfers between devices  60.9 us (16%)
  other arithmetic  44 us (11%)
  matrix products  40.4 us (10%)
    ppermute x50, waiting for transfers between devices, flipped(): return lax.ppermute(value, axis, [(i, i ^ mask) for i in range(size)])  79.4 us
    ppermute x50, starting transfers between devices, flipped(): return lax.ppermute(value, axis, [(i, i ^ mask) for i in range(size)])  52.3 us
    unnamed x228, local copies, waits for them, and re-layouts  46.2 us
    pallas_call x4, Pallas kernels, expert_rows(): pl.pallas_call(functools.partial(expert_kernel, count, not kept), grid=(1...  43.7 us
    pallas_call x2, Pallas kernels, weight_terms(): pl.pallas_call(functools.partial(weight_kernel, bool(others)), grid=(widt...  22.1 us
    dot_general x8, matrix products, dot_tn(): lax.dot_general(a, b, (((0,), (0,)), ((), ())), preferred_element_type=out)  16.4 us
    pallas_call x4, Pallas kernels, pack(): pl.pallas_call(functools.partial(pack_kernel, count, cap, tok, experts),...  11.4 us
    ppermute x3, starting transfers between devices, shifted(): return lax.ppermute(value, axis, pairs)  8.6 us
  transfers between devices with their start and end apart: 53, of which 20 were waited for; matrix products, arithmetic and copies ran while one was open for 23% of the time, Pallas kernels for 19%

profile of v2, /device:TPU:8, one launch (start us, length us, event | category | flops | bytes accessed | tf_op | source)
XLA Modules:
  0.0 383.9 jit_solution(7740404820433707342)
XLA Ops:
  6.1 2.2 maximum_maximum_fusion.bundle_ref
  8.3 3.0 collective-permute-start.5
  11.3 3.2 shard_map.229
  18.0 2.1 pad_maximum_fusion.refs_4_
  20.2 1.7 copy.93.refs_0_
  24.2 5.9 %collective-permute-done.refs_1_.refs_0_ = bf16[72,4096]{1,0:T(8,128)(2,1)S(1)} collective-permute-done((bf16[72,4096]{1,0:T(8,128)(2,1)}, bf16[72,4096]{1,0:T(8,128)(2,1)S(1)}, u32[]{:S(2)}, u32[]{:S(2)}) %collective-permute-start) | collective-permute-done | bytes 589856 | tf_op jit(solution)/shard_map/ppermute | solution.py:26
  30.1 2.5 collective-permute-done.1.refs_2_
  32.6 10.5 %collective-permute-done.2.refs_3_ = bf16[72,4096]{1,0:T(8,128)(2,1)} collective-permute-done((bf16[72,4096]{1,0:T(8,128)(2,1)}, bf16[72,4096]{1,0:T(8,128)(2,1)}, u32[]{:S(2)}, u32[]{:S(2)}) %collective-permute-start.2) | collective-permute-done | bytes 589856 | tf_op jit(solution)/shard_map/ppermute | solution.py:26
  43.3 2.8 copy.94.refs_0_
  55.8 2.8 shard_map.246
  61.4 2.1 shard_map.233
  67.6 11.2 %collective-permute-done.7.refs_0_.refs_1_ = bf16[72,4096]{1,0:T(8,128)(2,1)S(1)} collective-permute-done((bf16[72,4096]{1,0:T(8,128)(2,1)S(1)}, bf16[72,4096]{1,0:T(8,128)(2,1)S(1)}, u32[]{:S(2)}, u32[]{:S(2)}) %collective-permute-start.7) | collective-permute-done | bytes 589856 | tf_op jit(solution)/shard_map/ppermute | solution.py:26
  80.2 3.2 shard_map.234
  88.8 10.8 %shard_map.232 = (bf16[72,2176]{1,0:T(8,128)(2,1)S(1)}, bf16[72,2176]{1,0:T(8,128)(2,1)S(1)}, bf16[72,2176]{1,0:T(8,128)(2,1)S(1)}, bf16[72,2176]{1,0:T(8,128)(2...) custom-call(s32[1]{0:T(128)S(1)} %bitcast.81, ...), custom_call_target="tpu_custom_call" | custom-call | flops 1 | bytes 1 | tf_op jit(solution)/shard_map/pallas_call | solution.py:245
  101.8 9.9 %shard_map.235 = (bf16[72,2176]{1,0:T(8,128)(2,1)S(1)}, bf16[72,2176]{1,0:T(8,128)(2,1)S(1)}, bf16[72,2176]{1,0:T(8,128)(2,1)S(1)}, bf16[72,2176]{1,0:T(8,128)(2...) custom-call(s32[1]{0:T(128)S(1)} %bitcast.82, ...), custom_call_target="tpu_custom_call", output_to_operand_aliasing={{4}: (9, {}), {5}: (10, {}), {6}: (11, {}), {7}: (12, {}), ... | custom-call | flops 1 | bytes 1 | tf_op jit(solution)/shard_map/pallas_call | solution.py:245
  123.6 2.9 shard_map.237
  137.1 11.0 %shard_map.236 = (bf16[72,2176]{1,0:T(8,128)(2,1)S(1)}, bf16[72,2176]{1,0:T(8,128)(2,1)S(1)}, bf16[72,2176]{1,0:T(8,128)(2,1)S(1)}, bf16[72,2176]{1,0:T(8,128)(2...) custom-call(s32[1]{0:T(128)S(1)} %bitcast.83, ...), custom_call_target="tpu_custom_call", output_to_operand_aliasing={{4}: (9, {}), {5}: (10, {}), {6}: (11, {}), {7}: (12, {}), ... | custom-call | flops 1 | bytes 1 | tf_op jit(solution)/shard_map/pallas_call | solution.py:245
  158.1 6.0 %collective-permute-done.15.refs_2_ = bf16[72,4096]{1,0:T(8,128)(2,1)} collective-permute-done((bf16[72,4096]{1,0:T(8,128)(2,1)}, bf16[72,4096]{1,0:T(8,128)(2,1)}, u32[]{:S(2)}, u32[]{:S(2)}) %collective-permute-start.15) | collective-permute-done | bytes 589856 | tf_op jit(solution)/shard_map/ppermute | solution.py:26
  166.3 12.0 %shard_map.239 = (bf16[72,2176]{1,0:T(8,128)(2,1)S(1)}, bf16[72,2176]{1,0:T(8,128)(2,1)}, bf16[72,2176]{1,0:T(8,128)(2,1)}, bf16[72,2176]{1,0:T(8,128)(2,1)}, bf...) custom-call(s32[1]{0:T(128)S(1)} %bitcast.84, ...), custom_call_target="tpu_custom_call", output_to_operand_aliasing={{4}: (9, {}), {5}: (10, {}), {6}: (11, {}), {7}: (12, {}), ... | custom-call | flops 1 | bytes 1 | tf_op jit(solution)/shard_map/pallas_call | solution.py:245
  181.1 2.4 collective-permute-start.29
  183.6 2.1 fusion.81
  186.8 7.6 %collective-permute-done.27 = bf16[72,2176]{1,0:T(8,128)(2,1)} collective-permute-done((bf16[72,2176]{1,0:T(8,128)(2,1)}, bf16[72,2176]{1,0:T(8,128)(2,1)}, u32[]{:S(2)}, u32[]{:S(2)}) %collective-permute-start.27) | collective-permute-done | bytes 313376 | tf_op jit(solution)/shard_map/ppermute | solution.py:26
  194.9 4.1 %collective-permute-done.29 = bf16[72,2176]{1,0:T(8,128)(2,1)} collective-permute-done((bf16[72,2176]{1,0:T(8,128)(2,1)}, bf16[72,2176]{1,0:T(8,128)(2,1)}, u32[]{:S(2)}, u32[]{:S(2)}) %collective-permute-start.29) | collective-permute-done | bytes 313376 | tf_op jit(solution)/shard_map/ppermute | solution.py:26
  199.0 3.0 fusion.195
  203.0 3.2 fusion.50
  207.8 1.7 collective-permute-start.32
  209.5 3.0 collective-permute-done.19
  212.5 2.8 fusion.6.refs_1_
  216.3 4.7 %collective-permute-done.30 = bf16[72,2176]{1,0:T(8,128)(2,1)} collective-permute-done((bf16[72,2176]{1,0:T(8,128)(2,1)}, bf16[72,2176]{1,0:T(8,128)(2,1)}, u32[]{:S(2)}, u32[]{:S(2)}) %collective-permute-start.30) | collective-permute-done | bytes 313376 | tf_op jit(solution)/shard_map/ppermute | solution.py:26
  221.6 2.5 collective-permute-start.34
  224.2 1.7 collective-permute-done.32
  225.9 2.6 convolution_convert_fusion
  228.6 2.5 collective-permute-start.33
  231.1 2.5 collective-permute-done.22
  233.6 1.7 fusion.14.refs_0_
  237.7 2.3 copy-done.1
  240.1 11.2 %shard_map.249.refs_1_.refs_0_ = bf16[2048,1152]{1,0:T(8,128)(2,1)} custom-call(bf16[1152,2048]{1,0:T(8,128)(2,1)S(1)} %copy-done.1, bf16[1152,2048]{1,0:T(8,128)(2,1)} %get-tuple-element.127.grads_ref, bf16[1152,384]{1,0:T(8,128)(2,1)S(1)} %copy-done.15, bf16[1152,768]{1,0:T(8,128)(2,1)S(1)} %copy-done.4, f32[128,2176]{1,0:T(8,128)S(1)} %fusion.14.refs_0_, ...), custom_call_target="tpu_custom_call" | custom-call | flops 4000000000 | bytes 1 | tf_op jit(solution)/shard_map/pallas_call | solution.py:302
  251.9 4.4 %collective-permute-done.35 = bf16[128,2176]{1,0:T(8,128)(2,1)} collective-permute-done((bf16[128,2176]{1,0:T(8,128)(2,1)}, bf16[128,2176]{1,0:T(8,128)(2,1)}, u32[]{:S(2)}, u32[]{:S(2)}) %collective-permute-start.35) | collective-permute-done | bytes 557088 | tf_op jit(solution)/shard_map/ppermute | solution.py:26
  256.3 1.7 convert_add_fusion.1
  259.2 1.7 broadcast_in_dim.96
  260.9 1.8 constant_dynamic-update-slice_fusion
  270.6 5.8 %collective-permute-done.36 = bf16[144,2048]{1,0:T(8,128)(2,1)} collective-permute-done((bf16[144,2048]{1,0:T(8,128)(2,1)}, bf16[144,2048]{1,0:T(8,128)(2,1)}, u32[]{:S(2)}, u32[]{:S(2)}) %collective-permute-start.36) | collective-permute-done | bytes 589856 | tf_op jit(solution)/shard_map/ppermute | solution.py:26
  278.5 1.9 slice_dynamic-update-slice_fusion.2
  281.9 1.9 slice_dynamic-update-slice_fusion.1
  283.8 1.9 slice_dynamic-update-slice_fusion.refs_1_
  285.8 2.9 fusion.197.g_ref
  292.4 2.4 fusion.90
  294.8 2.6 constant_dynamic-slice_fusion.7
  297.5 1.7 fusion.55.refs_0_
  299.2 5.1 %shard_map.255 = (f32[512,512]{1,0:T(8,128)S(1)}, f32[8,512]{1,0:T(8,128)S(1)}, f32[512,8]{1,0:T(8,128)S(1)}, f32[512,128]{1,0:T(8,128)S(1)}, f32[512,128]{1,0:T(8,128)S(1)}) custom-call(bf16[512,128]{1,0:T(8,128)(2,1)S(1)} %copy-done.39, bf16[512,128]{1,0:T(8,128)(2,1)S(1)} %copy-done.37, bf16[512,512]{1,0:T(8,128)(2,1)S(1)} %copy-done.5, ...), custom_call_target="tpu_custom_call" | custom-call | flops 2000000000 | bytes 1 | tf_op jit(solution)/shard_map/pallas_call | solution.py:345
  309.4 2.2 convolution_add_fusion
  313.5 1.8 fusion.87.refs_1_
  315.2 6.0 %collective-permute-start.40 = (bf16[512,128]{1,0:T(8,128)(2,1)}, bf16[512,128]{1,0:T(8,128)(2,1)}, u32[]{:S(2)}, u32[]{:S(2)}) collective-permute-start(bf16[512,128]{1,0:T(8,128)(2,1)} %fusion.87.refs_1_), channel_id=1, source_target_pairs={{8,0},{12,4},{16,8},{20,12},{24,16},{28,20},{9,1},{13,5},{17,9},{2... | collective-permute-start | bytes 393224 | tf_op jit(solution)/shard_map/ppermute | solution.py:32
  326.8 3.9 %collective-permute-done.41 = bf16[512,128]{1,0:T(8,128)(2,1)} collective-permute-done((bf16[512,128]{1,0:T(8,128)(2,1)}, bf16[512,128]{1,0:T(8,128)(2,1)}, u32[]{:S(2)}, u32[]{:S(2)}) %collective-permute-start.41) | collective-permute-done | bytes 131104 | tf_op jit(solution)/shard_map/ppermute | solution.py:32
  330.8 2.3 multiply_reduce_fusion
  333.8 2.9 fusion.54
  339.5 4.6 %collective-permute-start.44 = (f32[2176]{0:T(1024)S(1)}, f32[2176]{0:T(1024)S(1)}, u32[]{:S(2)}, u32[]{:S(2)}) collective-permute-start(f32[2176]{0:T(1024)S(1)} %add.454), channel_id=1, source_target_pairs={{0,8},{4,12},{8,0},{12,4},{16,24},{20,28},{24,16},{28,20},{1,9},{5... | collective-permute-start | bytes 26120 | tf_op jit(solution)/shard_map/ppermute | solution.py:26
  345.8 2.3 fusion.38
  348.0 2.3 collective-permute-done.45
  353.1 2.4 fusion.196
  356.5 2.0 collective-permute-start.48
  360.8 2.3 copy-done.2
  363.2 10.9 %shard_map.259 = (bf16[1,2048,384]{2,1,0:T(8,128)(2,1)}, bf16[1,2048,384]{2,1,0:T(8,128)(2,1)}, bf16[1,384,2048]{2,1,0:T(8,128)(2,1)}) custom-call(bf16[1152,2048]{1,0:T(8,128)(2,1)S(1)} %bitcast.78, bf16[1152,2048]{1,0:T(8,128)(2,1)S(1)} %copy-done.2, bf16[1152,384]{1,0:T(8,128)(2,1)S(1)} %get-tuple-element.139.act_ref, bf16[1152,768]{1,0:T(8,128)(2,1)S(1)} %copy-done.3, ...), custom_call_target="tpu_custom_call" | custom-call | flops 4000000000 | bytes 1 | tf_op jit(solution)/shard_map/pallas_call | solution.py:302
  377.5 3.7 collective-permute-done.50
  (430 shorter events, 128.7 us)
Async XLA Ops:
  0.6 285.1 %copy-start = (bf16[2048,512]{1,0:T(8,128)(2,1)S(1)}, bf16[2048,512]{1,0:T(8,128)(2,1)}, u32[]{:S(2)}) copy-start(bf16[2048,512]{1,0:T(8,128)(2,1)} %param.27) | copy-start | bytes 6291460
  8.3 53.2 %collective-permute-start.6 = (bf16[272,2048]{1,0:T(8,128)(2,1)}, bf16[272,2048]{1,0:T(8,128)(2,1)}, u32[]{:S(2)}, u32[]{:S(2)}) collective-permute-start(bf16[272,2048]{1,0:T(8,128)(2,1)} %maximum_maximum_fusion.bundle_ref), channel_id=1, source_target_pairs={{0,8},{1,9},{2,10},{3,11},{4,12},{5,13},{6,14},{7,15},{8,0},{9,1},... | collective-permute-start | bytes 3342344 | tf_op jit(solution)/shard_map/ppermute | solution.py:26
  8.3 57.5 %collective-permute-start.5 = (bf16[272,2048]{1,0:T(8,128)(2,1)}, bf16[272,2048]{1,0:T(8,128)(2,1)}, u32[]{:S(2)}, u32[]{:S(2)}) collective-permute-start(bf16[272,2048]{1,0:T(8,128)(2,1)} %maximum_maximum_fusion.bundle_ref), channel_id=1, source_target_pairs={{0,16},{1,17},{2,18},{3,19},{4,20},{5,21},{6,22},{7,23},{8,24},{9,... | collective-permute-start | bytes 3342344 | tf_op jit(solution)/shard_map/ppermute | solution.py:26
  14.5 15.6 %collective-permute-start = (bf16[72,4096]{1,0:T(8,128)(2,1)}, bf16[72,4096]{1,0:T(8,128)(2,1)S(1)}, u32[]{:S(2)}, u32[]{:S(2)}) collective-permute-start(bf16[72,4096]{1,0:T(8,128)(2,1)} %get-tuple-element.82), channel_id=1, source_target_pairs={{0,2},{1,3},{2,0},{3,1},{4,6},{5,7},{6,4},{7,5},{8,10},{9,11},{10,... | collective-permute-start | bytes 1769480 | tf_op jit(solution)/shard_map/ppermute | solution.py:26
  16.0 16.6 %collective-permute-start.1 = (bf16[72,4096]{1,0:T(8,128)(2,1)}, bf16[72,4096]{1,0:T(8,128)(2,1)}, u32[]{:S(2)}, u32[]{:S(2)}) collective-permute-start(bf16[72,4096]{1,0:T(8,128)(2,1)} %get-tuple-element.83), channel_id=1, source_target_pairs={{0,4},{1,5},{2,6},{3,7},{4,0},{5,1},{6,2},{7,3},{8,12},{9,13},{10,... | collective-permute-start | bytes 1769480 | tf_op jit(solution)/shard_map/ppermute | solution.py:26
  17.5 25.6 %collective-permute-start.2 = (bf16[72,4096]{1,0:T(8,128)(2,1)}, bf16[72,4096]{1,0:T(8,128)(2,1)}, u32[]{:S(2)}, u32[]{:S(2)}) collective-permute-start(bf16[72,4096]{1,0:T(8,128)(2,1)} %get-tuple-element.84), channel_id=1, source_target_pairs={{0,6},{1,7},{2,4},{3,5},{4,2},{5,3},{6,0},{7,1},{8,14},{9,15},{10,... | collective-permute-start | bytes 1769480 | tf_op jit(solution)/shard_map/ppermute | solution.py:26
  43.2 43.3 %collective-permute-start.3 = (bf16[2048,768]{1,0:T(8,128)(2,1)}, bf16[2048,768]{1,0:T(8,128)(2,1)}, u32[]{:S(2)}, u32[]{:S(2)}) collective-permute-start(bf16[2048,768]{1,0:T(8,128)(2,1)} %shard_map.230), channel_id=1, source_target_pairs={{0,1},{1,0},{2,3},{3,2},{4,5},{5,4},{6,7},{7,6},{8,9},{9,8},{10,11... | collective-permute-start | bytes 9437192 | tf_op jit(solution)/shard_map/ppermute | solution.py:26
  43.2 180.8 %copy-start.98 = (s32[512]{0:T(512)}, s32[512]{0:T(512)S(1)}, u32[]{:S(2)}) copy-start(s32[512]{0:T(512)S(1)} %add_select_fusion) | copy-start | bytes 6148
  46.2 156.8 %copy-start.100 = (f32[1,512]{1,0:T(1,128)}, f32[1,512]{1,0:T(1,128)S(1)}, u32[]{:S(2)}) copy-start(f32[1,512]{1,0:T(1,128)S(1)} %fusion.100) | copy-start | bytes 6148
  50.7 34.2 %collective-permute-start.4 = (bf16[384,2048]{1,0:T(8,128)(2,1)}, bf16[384,2048]{1,0:T(8,128)(2,1)}, u32[]{:S(2)}, u32[]{:S(2)}) collective-permute-start(bf16[384,2048]{1,0:T(8,128)(2,1)} %shard_map.231), channel_id=1, source_target_pairs={{0,1},{1,0},{2,3},{3,2},{4,5},{5,4},{6,7},{7,6},{8,9},{9,8},{10,11... | collective-permute-start | bytes 4718600 | tf_op jit(solution)/shard_map/ppermute | solution.py:26
  52.8 7.4 %collective-permute-start.23 = (bf16[528,128]{1,0:T(8,128)(2,1)}, bf16[528,128]{1,0:T(8,128)(2,1)}, u32[]{:S(2)}, u32[]{:S(2)}) collective-permute-start(bf16[528,128]{1,0:T(8,128)(2,1)} %fusion.89), channel_id=1, source_target_pairs={{0,4},{4,0},{8,12},{12,8},{16,20},{20,16},{24,28},{28,24},{1,5},{5... | collective-permute-start | bytes 405512 | tf_op jit(solution)/shard_map/ppermute | solution.py:26
  59.6 27.5 %copy-start.79 = (bf16[512,128]{1,0:T(8,128)(2,1)S(1)}, bf16[512,128]{1,0:T(8,128)(2,1)}, u32[]{:S(2)}) copy-start(bf16[512,128]{1,0:T(8,128)(2,1)} %shard_map.247) | copy-start | bytes 393220
  61.4 27.4 %copy-start.45 = (bf16[72,4096]{1,0:T(8,128)(2,1)S(1)}, bf16[72,4096]{1,0:T(8,128)(2,1)}, u32[]{:S(2)}) copy-start(bf16[72,4096]{1,0:T(8,128)(2,1)} %copy-done.44) | copy-start | bytes 1769476
  63.5 36.0 %copy-start.70 = (bf16[288,128]{1,0:T(8,128)(2,1)}, bf16[288,128]{1,0:T(8,128)(2,1)S(1)}, u32[]{:S(2)}) copy-start(bf16[288,128]{1,0:T(8,128)(2,1)S(1)} %get-tuple-element.130) | copy-start | bytes 221188
  63.5 38.2 %copy-start.28 = (bf16[72,4096]{1,0:T(8,128)(2,1)}, bf16[72,4096]{1,0:T(8,128)(2,1)S(1)}, u32[]{:S(2)}) copy-start(bf16[72,4096]{1,0:T(8,128)(2,1)S(1)} %get-tuple-element.93.refs_0_) | copy-start | bytes 1769476
  63.5 15.2 %collective-permute-start.7 = (bf16[72,4096]{1,0:T(8,128)(2,1)S(1)}, bf16[72,4096]{1,0:T(8,128)(2,1)S(1)}, u32[]{:S(2)}, u32[]{:S(2)}) collective-permute-start(bf16[72,4096]{1,0:T(8,128)(2,1)S(1)} %get-tuple-element.87), channel_id=1, source_target_pairs={{0,2},{1,3},{2,0},{3,1},{4,6},{5,7},{6,4},{7,5},{8,10},{9,11},{10,... | collective-permute-start | bytes 1769480 | tf_op jit(solution)/shard_map/ppermute | solution.py:26
  65.2 18.3 %collective-permute-start.11 = (bf16[72,4096]{1,0:T(8,128)(2,1)S(1)}, bf16[72,4096]{1,0:T(8,128)(2,1)S(1)}, u32[]{:S(2)}, u32[]{:S(2)}) collective-permute-start(bf16[72,4096]{1,0:T(8,128)(2,1)S(1)} %get-tuple-element.94), channel_id=1, source_target_pairs={{0,4},{1,5},{2,6},{3,7},{4,0},{5,1},{6,2},{7,3},{8,12},{9,13},{10,... | collective-permute-start | bytes 1769480 | tf_op jit(solution)/shard_map/ppermute | solution.py:26
  65.8 52.3 %collective-permute-start.13 = (bf16[272,2048]{1,0:T(8,128)(2,1)}, bf16[272,2048]{1,0:T(8,128)(2,1)}, u32[]{:S(2)}, u32[]{:S(2)}) collective-permute-start(bf16[272,2048]{1,0:T(8,128)(2,1)} %collective-permute-done.5.bundle_ref), channel_id=1, source_target_pairs={{0,8},{1,9},{2,10},{3,11},{4,12},{5,13},{6,14},{7,15},{8,0},{9,1},... | collective-permute-start | bytes 3342344 | tf_op jit(solution)/shard_map/ppermute | solution.py:26
  78.7 23.1 %copy-start.23 = (bf16[72,4096]{1,0:T(8,128)(2,1)}, bf16[72,4096]{1,0:T(8,128)(2,1)S(1)}, u32[]{:S(2)}) copy-start(bf16[72,4096]{1,0:T(8,128)(2,1)S(1)} %collective-permute-done.7.refs_0_.refs_1_) | copy-start | bytes 1769476
  78.7 23.0 %collective-permute-start.12 = (bf16[72,4096]{1,0:T(8,128)(2,1)S(1)}, bf16[72,4096]{1,0:T(8,128)(2,1)S(1)}, u32[]{:S(2)}, u32[]{:S(2)}) collective-permute-start(bf16[72,4096]{1,0:T(8,128)(2,1)S(1)} %get-tuple-element.95), channel_id=1, source_target_pairs={{0,6},{1,7},{2,4},{3,5},{4,2},{5,3},{6,0},{7,1},{8,14},{9,15},{10,... | collective-permute-start | bytes 1769480 | tf_op jit(solution)/shard_map/ppermute | solution.py:26
  83.4 18.4 %copy-start.30 = (bf16[72,4096]{1,0:T(8,128)(2,1)}, bf16[72,4096]{1,0:T(8,128)(2,1)S(1)}, u32[]{:S(2)}) copy-start(bf16[72,4096]{1,0:T(8,128)(2,1)S(1)} %collective-permute-done.11.refs_2_) | copy-start | bytes 1769476
  83.4 46.9 %collective-permute-start.10 = (bf16[72,4096]{1,0:T(8,128)(2,1)}, bf16[72,4096]{1,0:T(8,128)(2,1)}, u32[]{:S(2)}, u32[]{:S(2)}) collective-permute-start(bf16[72,4096]{1,0:T(8,128)(2,1)} %get-tuple-element.92), channel_id=1, source_target_pairs={{0,6},{1,7},{2,4},{3,5},{4,2},{5,3},{6,0},{7,1},{8,14},{9,15},{10,... | collective-permute-start | bytes 1769480 | tf_op jit(solution)/shard_map/ppermute | solution.py:26
  84.9 47.0 %collective-permute-start.8 = (bf16[72,4096]{1,0:T(8,128)(2,1)}, bf16[72,4096]{1,0:T(8,128)(2,1)}, u32[]{:S(2)}, u32[]{:S(2)}) collective-permute-start(bf16[72,4096]{1,0:T(8,128)(2,1)} %get-tuple-element.90), channel_id=1, source_target_pairs={{0,2},{1,3},{2,0},{3,1},{4,6},{5,7},{6,4},{7,5},{8,10},{9,11},{10,... | collective-permute-start | bytes 1769480 | tf_op jit(solution)/shard_map/ppermute | solution.py:26
  86.5 46.9 %collective-permute-start.9 = (bf16[72,4096]{1,0:T(8,128)(2,1)}, bf16[72,4096]{1,0:T(8,128)(2,1)}, u32[]{:S(2)}, u32[]{:S(2)}) collective-permute-start(bf16[72,4096]{1,0:T(8,128)(2,1)} %get-tuple-element.91), channel_id=1, source_target_pairs={{0,4},{1,5},{2,6},{3,7},{4,0},{5,1},{6,2},{7,3},{8,12},{9,13},{10,... | collective-permute-start | bytes 1769480 | tf_op jit(solution)/shard_map/ppermute | solution.py:26
  116.5 35.4 %collective-permute-start.24 = (bf16[528,128]{1,0:T(8,128)(2,1)}, bf16[528,128]{1,0:T(8,128)(2,1)}, u32[]{:S(2)}, u32[]{:S(2)}) collective-permute-start(bf16[528,128]{1,0:T(8,128)(2,1)} %shard_map.248), channel_id=1, source_target_pairs={{0,8},{4,12},{8,0},{12,4},{16,24},{20,28},{24,16},{28,20},{1,9},{5... | collective-permute-start | bytes 405512 | tf_op jit(solution)/shard_map/ppermute | solution.py:26
  118.0 35.1 %collective-permute-start.25 = (bf16[528,128]{1,0:T(8,128)(2,1)}, bf16[528,128]{1,0:T(8,128)(2,1)}, u32[]{:S(2)}, u32[]{:S(2)}) collective-permute-start(bf16[528,128]{1,0:T(8,128)(2,1)} %shard_map.248), channel_id=1, source_target_pairs={{0,16},{4,20},{8,24},{12,28},{16,0},{20,4},{24,8},{28,12},{1,17},{... | collective-permute-start | bytes 405512 | tf_op jit(solution)/shard_map/ppermute | solution.py:26
  130.3 23.6 %collective-permute-start.26 = (bf16[528,128]{1,0:T(8,128)(2,1)}, bf16[528,128]{1,0:T(8,128)(2,1)S(1)}, u32[]{:S(2)}, u32[]{:S(2)}) collective-permute-start(bf16[528,128]{1,0:T(8,128)(2,1)} %shard_map.248), channel_id=1, source_target_pairs={{0,24},{4,28},{8,16},{12,20},{16,8},{20,12},{24,0},{28,4},{1,25},{... | collective-permute-start | bytes 405512 | tf_op jit(solution)/shard_map/ppermute | solution.py:26
  131.9 24.6 %collective-permute-start.16 = (bf16[72,4096]{1,0:T(8,128)(2,1)}, bf16[72,4096]{1,0:T(8,128)(2,1)}, u32[]{:S(2)}, u32[]{:S(2)}) collective-permute-start(bf16[72,4096]{1,0:T(8,128)(2,1)} %shard_map.238), channel_id=1, source_target_pairs={{0,6},{1,7},{2,4},{3,5},{4,2},{5,3},{6,0},{7,1},{8,14},{9,15},{10,... | collective-permute-start | bytes 1769480 | tf_op jit(solution)/shard_map/ppermute | solution.py:26
  133.3 24.8 %collective-permute-start.14 = (bf16[72,4096]{1,0:T(8,128)(2,1)}, bf16[72,4096]{1,0:T(8,128)(2,1)}, u32[]{:S(2)}, u32[]{:S(2)}) collective-permute-start(bf16[72,4096]{1,0:T(8,128)(2,1)} %copy-done.66), channel_id=1, source_target_pairs={{0,2},{1,3},{2,0},{3,1},{4,6},{5,7},{6,4},{7,5},{8,10},{9,11},{10,... | collective-permute-start | bytes 1769480 | tf_op jit(solution)/shard_map/ppermute | solution.py:26
  151.9 12.2 %collective-permute-start.15 = (bf16[72,4096]{1,0:T(8,128)(2,1)}, bf16[72,4096]{1,0:T(8,128)(2,1)}, u32[]{:S(2)}, u32[]{:S(2)}) collective-permute-start(bf16[72,4096]{1,0:T(8,128)(2,1)} %get-tuple-element.112), channel_id=1, source_target_pairs={{0,4},{1,5},{2,6},{3,7},{4,0},{5,1},{6,2},{7,3},{8,12},{9,13},{10,... | collective-permute-start | bytes 1769480 | tf_op jit(solution)/shard_map/ppermute | solution.py:26
  166.3 17.2 %copy-start.93 = (bf16[528,128]{1,0:T(8,128)(2,1)S(1)}, bf16[528,128]{1,0:T(8,128)(2,1)}, u32[]{:S(2)}) copy-start(bf16[528,128]{1,0:T(8,128)(2,1)} %copy-done.92) | copy-start | bytes 405508
  180.1 14.3 %collective-permute-start.27 = (bf16[72,2176]{1,0:T(8,128)(2,1)}, bf16[72,2176]{1,0:T(8,128)(2,1)}, u32[]{:S(2)}, u32[]{:S(2)}) collective-permute-start(bf16[72,2176]{1,0:T(8,128)(2,1)} %get-tuple-element.133), channel_id=1, source_target_pairs={{0,2},{1,3},{2,0},{3,1},{4,6},{5,7},{6,4},{7,5},{8,10},{9,11},{10,... | collective-permute-start | bytes 940040 | tf_op jit(solution)/shard_map/ppermute | solution.py:26
  180.6 14.3 %collective-permute-start.28 = (bf16[72,2176]{1,0:T(8,128)(2,1)}, bf16[72,2176]{1,0:T(8,128)(2,1)}, u32[]{:S(2)}, u32[]{:S(2)}) collective-permute-start(bf16[72,2176]{1,0:T(8,128)(2,1)} %get-tuple-element.134), channel_id=1, source_target_pairs={{0,4},{1,5},{2,6},{3,7},{4,0},{5,1},{6,2},{7,3},{8,12},{9,13},{10,... | collective-permute-start | bytes 940040 | tf_op jit(solution)/shard_map/ppermute | solution.py:26
  181.1 17.9 %collective-permute-start.29 = (bf16[72,2176]{1,0:T(8,128)(2,1)}, bf16[72,2176]{1,0:T(8,128)(2,1)}, u32[]{:S(2)}, u32[]{:S(2)}) collective-permute-start(bf16[72,2176]{1,0:T(8,128)(2,1)} %get-tuple-element.135), channel_id=1, source_target_pairs={{0,6},{1,7},{2,4},{3,5},{4,2},{5,3},{6,0},{7,1},{8,14},{9,15},{10,... | collective-permute-start | bytes 940040 | tf_op jit(solution)/shard_map/ppermute | solution.py:26
  185.7 22.0 %collective-permute-start.17 = (bf16[72,2176]{1,0:T(8,128)(2,1)}, bf16[72,2176]{1,0:T(8,128)(2,1)}, u32[]{:S(2)}, u32[]{:S(2)}) collective-permute-start(bf16[72,2176]{1,0:T(8,128)(2,1)} %shard_map.240), channel_id=1, source_target_pairs={{0,2},{1,3},{2,0},{3,1},{4,6},{5,7},{6,4},{7,5},{8,10},{9,11},{10,... | collective-permute-start | bytes 940040 | tf_op jit(solution)/shard_map/ppermute | solution.py:26
  186.3 23.2 %collective-permute-start.18 = (bf16[72,2176]{1,0:T(8,128)(2,1)}, bf16[72,2176]{1,0:T(8,128)(2,1)}, u32[]{:S(2)}, u32[]{:S(2)}) collective-permute-start(bf16[72,2176]{1,0:T(8,128)(2,1)} %shard_map.241), channel_id=1, source_target_pairs={{0,4},{1,5},{2,6},{3,7},{4,0},{5,1},{6,2},{7,3},{8,12},{9,13},{10,... | collective-permute-start | bytes 940040 | tf_op jit(solution)/shard_map/ppermute | solution.py:26
  194.4 18.1 %collective-permute-start.19 = (bf16[72,2176]{1,0:T(8,128)(2,1)}, bf16[72,2176]{1,0:T(8,128)(2,1)}, u32[]{:S(2)}, u32[]{:S(2)}) collective-permute-start(bf16[72,2176]{1,0:T(8,128)(2,1)} %shard_map.242), channel_id=1, source_target_pairs={{0,6},{1,7},{2,4},{3,5},{4,2},{5,3},{6,0},{7,1},{8,14},{9,15},{10,... | collective-permute-start | bytes 940040 | tf_op jit(solution)/shard_map/ppermute | solution.py:26
  202.0 19.1 %collective-permute-start.30 = (bf16[72,2176]{1,0:T(8,128)(2,1)}, bf16[72,2176]{1,0:T(8,128)(2,1)}, u32[]{:S(2)}, u32[]{:S(2)}) collective-permute-start(bf16[72,2176]{1,0:T(8,128)(2,1)} %shard_map.251), channel_id=1, source_target_pairs={{0,2},{1,3},{2,0},{3,1},{4,6},{5,7},{6,4},{7,5},{8,10},{9,11},{10,... | collective-permute-start | bytes 940040 | tf_op jit(solution)/shard_map/ppermute | solution.py:26
  202.5 19.0 %collective-permute-start.31 = (bf16[72,2176]{1,0:T(8,128)(2,1)}, bf16[72,2176]{1,0:T(8,128)(2,1)}, u32[]{:S(2)}, u32[]{:S(2)}) collective-permute-start(bf16[72,2176]{1,0:T(8,128)(2,1)} %shard_map.252), channel_id=1, source_target_pairs={{0,4},{1,5},{2,6},{3,7},{4,0},{5,1},{6,2},{7,3},{8,12},{9,13},{10,... | collective-permute-start | bytes 940040 | tf_op jit(solution)/shard_map/ppermute | solution.py:26
  207.8 18.2 %collective-permute-start.32 = (bf16[72,2176]{1,0:T(8,128)(2,1)}, bf16[72,2176]{1,0:T(8,128)(2,1)}, u32[]{:S(2)}, u32[]{:S(2)}) collective-permute-start(bf16[72,2176]{1,0:T(8,128)(2,1)} %shard_map.253), channel_id=1, source_target_pairs={{0,6},{1,7},{2,4},{3,5},{4,2},{5,3},{6,0},{7,1},{8,14},{9,15},{10,... | collective-permute-start | bytes 940040 | tf_op jit(solution)/shard_map/ppermute | solution.py:26
  215.2 15.8 %collective-permute-start.20 = (bf16[72,2176]{1,0:T(8,128)(2,1)}, bf16[72,2176]{1,0:T(8,128)(2,1)}, u32[]{:S(2)}, u32[]{:S(2)}) collective-permute-start(bf16[72,2176]{1,0:T(8,128)(2,1)} %shard_map.243), channel_id=1, source_target_pairs={{0,2},{1,3},{2,0},{3,1},{4,6},{5,7},{6,4},{7,5},{8,10},{9,11},{10,... | collective-permute-start | bytes 940040 | tf_op jit(solution)/shard_map/ppermute | solution.py:26
  215.8 15.3 %collective-permute-start.21 = (bf16[72,2176]{1,0:T(8,128)(2,1)}, bf16[72,2176]{1,0:T(8,128)(2,1)}, u32[]{:S(2)}, u32[]{:S(2)}) collective-permute-start(bf16[72,2176]{1,0:T(8,128)(2,1)} %shard_map.244), channel_id=1, source_target_pairs={{0,4},{1,5},{2,6},{3,7},{4,0},{5,1},{6,2},{7,3},{8,12},{9,13},{10,... | collective-permute-start | bytes 940040 | tf_op jit(solution)/shard_map/ppermute | solution.py:26
  221.0 12.5 %collective-permute-start.22 = (bf16[72,2176]{1,0:T(8,128)(2,1)}, bf16[72,2176]{1,0:T(8,128)(2,1)S(1)}, u32[]{:S(2)}, u32[]{:S(2)}) collective-permute-start(bf16[72,2176]{1,0:T(8,128)(2,1)} %shard_map.245), channel_id=1, source_target_pairs={{0,6},{1,7},{2,4},{3,5},{4,2},{5,3},{6,0},{7,1},{8,14},{9,15},{10,... | collective-permute-start | bytes 940040 | tf_op jit(solution)/shard_map/ppermute | solution.py:26
  221.6 13.8 %collective-permute-start.34 = (bf16[128,2176]{1,0:T(8,128)(2,1)}, bf16[128,2176]{1,0:T(8,128)(2,1)S(1)}, u32[]{:S(2)}, u32[]{:S(2)}) collective-permute-start(bf16[128,2176]{1,0:T(8,128)(2,1)} %get-tuple-element.234), channel_id=1, source_target_pairs={{0,8},{1,9},{2,10},{3,11},{4,12},{5,13},{6,14},{7,15},{8,0},{9,1},... | collective-permute-start | bytes 1671176 | tf_op jit(solution)/shard_map/ppermute | solution.py:26
  228.6 23.3 %collective-permute-start.33 = (bf16[128,2176]{1,0:T(8,128)(2,1)}, bf16[128,2176]{1,0:T(8,128)(2,1)}, u32[]{:S(2)}, u32[]{:S(2)}) collective-permute-start(bf16[128,2176]{1,0:T(8,128)(2,1)} %convolution_convert_fusion), channel_id=1, source_target_pairs={{0,8},{1,9},{2,10},{3,11},{4,12},{5,13},{6,14},{7,15},{8,0},{9,1},... | collective-permute-start | bytes 1671176 | tf_op jit(solution)/shard_map/ppermute | solution.py:26
  236.3 20.0 %collective-permute-start.35 = (bf16[128,2176]{1,0:T(8,128)(2,1)}, bf16[128,2176]{1,0:T(8,128)(2,1)}, u32[]{:S(2)}, u32[]{:S(2)}) collective-permute-start(bf16[128,2176]{1,0:T(8,128)(2,1)} %add_convert_fusion), channel_id=1, source_target_pairs={{0,16},{1,17},{2,18},{3,19},{4,20},{5,21},{6,22},{7,23},{8,24},{9,... | collective-permute-start | bytes 1671176 | tf_op jit(solution)/shard_map/ppermute | solution.py:26
  264.4 12.0 %collective-permute-start.36 = (bf16[144,2048]{1,0:T(8,128)(2,1)}, bf16[144,2048]{1,0:T(8,128)(2,1)}, u32[]{:S(2)}, u32[]{:S(2)}) collective-permute-start(bf16[144,2048]{1,0:T(8,128)(2,1)} %fusion.78), channel_id=1, source_target_pairs={{0,2},{1,3},{2,0},{3,1},{4,6},{5,7},{6,4},{7,5},{8,10},{9,11},{10,... | collective-permute-start | bytes 1769480 | tf_op jit(solution)/shard_map/ppermute | solution.py:26
  265.1 12.7 %collective-permute-start.37 = (bf16[144,2048]{1,0:T(8,128)(2,1)}, bf16[144,2048]{1,0:T(8,128)(2,1)}, u32[]{:S(2)}, u32[]{:S(2)}) collective-permute-start(bf16[144,2048]{1,0:T(8,128)(2,1)} %fusion.78), channel_id=1, source_target_pairs={{0,1},{1,0},{2,3},{3,2},{4,5},{5,4},{6,7},{7,6},{8,9},{9,8},{10,11... | collective-permute-start | bytes 1769480 | tf_op jit(solution)/shard_map/ppermute | solution.py:26
  276.4 7.4 %collective-permute-start.38 = (bf16[144,2048]{1,0:T(8,128)(2,1)}, bf16[144,2048]{1,0:T(8,128)(2,1)}, u32[]{:S(2)}, u32[]{:S(2)}) collective-permute-start(bf16[144,2048]{1,0:T(8,128)(2,1)} %collective-permute-done.36), channel_id=1, source_target_pairs={{0,1},{1,0},{2,3},{3,2},{4,5},{5,4},{6,7},{7,6},{8,9},{9,8},{10,11... | collective-permute-start | bytes 1769480 | tf_op jit(solution)/shard_map/ppermute | solution.py:26
  291.6 21.8 %collective-permute-start.39 = (bf16[512,128]{1,0:T(8,128)(2,1)}, bf16[512,128]{1,0:T(8,128)(2,1)}, u32[]{:S(2)}, u32[]{:S(2)}) collective-permute-start(bf16[512,128]{1,0:T(8,128)(2,1)} %fusion.180.refs_1_), channel_id=1, source_target_pairs={{0,4},{4,0},{8,12},{12,8},{16,20},{20,16},{24,28},{28,24},{1,5},{5... | collective-permute-start | bytes 393224 | tf_op jit(solution)/shard_map/ppermute | solution.py:26
  306.0 47.1 %collective-permute-start.47 = (bf16[512,1024]{1,0:T(8,128)(2,1)}, bf16[512,1024]{1,0:T(8,128)(2,1)}, u32[]{:S(2)}, u32[]{:S(2)}) collective-permute-start(bf16[512,1024]{1,0:T(8,128)(2,1)} %fusion.55.refs_0_), channel_id=1, source_target_pairs={{0,4},{4,0},{8,12},{12,8},{16,20},{20,16},{24,28},{28,24},{1,5},{5... | collective-permute-start | bytes 3145736 | tf_op jit(solution)/shard_map/ppermute | solution.py:26
  307.3 53.5 %collective-permute-start.46 = (bf16[2048,1152]{1,0:T(8,128)(2,1)}, bf16[2048,1152]{1,0:T(8,128)(2,1)}, u32[]{:S(2)}, u32[]{:S(2)}) collective-permute-start(bf16[2048,1152]{1,0:T(8,128)(2,1)} %shard_map.258), channel_id=1, source_target_pairs={{0,1},{1,0},{2,3},{3,2},{4,5},{5,4},{6,7},{7,6},{8,9},{9,8},{10,11... | collective-permute-start | bytes 14155784 | tf_op jit(solution)/shard_map/ppermute | solution.py:26
  312.4 21.3 %copy-start.101 = (f32[1,512]{1,0:T(1,128)S(1)}, f32[1,512]{1,0:T(1,128)}, u32[]{:S(2)}) copy-start(f32[1,512]{1,0:T(1,128)} %copy-done.100) | copy-start | bytes 6148
  315.2 11.6 %collective-permute-start.40 = (bf16[512,128]{1,0:T(8,128)(2,1)}, bf16[512,128]{1,0:T(8,128)(2,1)}, u32[]{:S(2)}, u32[]{:S(2)}) collective-permute-start(bf16[512,128]{1,0:T(8,128)(2,1)} %fusion.87.refs_1_), channel_id=1, source_target_pairs={{8,0},{12,4},{16,8},{20,12},{24,16},{28,20},{9,1},{13,5},{17,9},{2... | collective-permute-start | bytes 393224 | tf_op jit(solution)/shard_map/ppermute | solution.py:32
  321.2 9.5 %collective-permute-start.41 = (bf16[512,128]{1,0:T(8,128)(2,1)}, bf16[512,128]{1,0:T(8,128)(2,1)}, u32[]{:S(2)}, u32[]{:S(2)}) collective-permute-start(bf16[512,128]{1,0:T(8,128)(2,1)} %fusion.87.refs_1_), channel_id=1, source_target_pairs={{16,0},{20,4},{24,8},{28,12},{17,1},{21,5},{25,9},{29,13},{18,2},{... | collective-permute-start | bytes 393224 | tf_op jit(solution)/shard_map/ppermute | solution.py:32
  322.5 8.2 %collective-permute-start.42 = (bf16[512,128]{1,0:T(8,128)(2,1)}, bf16[512,128]{1,0:T(8,128)(2,1)}, u32[]{:S(2)}, u32[]{:S(2)}) collective-permute-start(bf16[512,128]{1,0:T(8,128)(2,1)} %fusion.87.refs_1_), channel_id=1, source_target_pairs={{24,0},{28,4},{25,1},{29,5},{26,2},{30,6},{27,3},{31,7}} | collective-permute-start | bytes 393224 | tf_op jit(solution)/shard_map/ppermute | solution.py:32
  333.1 6.3 %collective-permute-start.43 = (f32[2176]{0:T(1024)}, f32[2176]{0:T(1024)S(1)}, u32[]{:S(2)}, u32[]{:S(2)}) collective-permute-start(f32[2176]{0:T(1024)} %shard_map.257), channel_id=1, source_target_pairs={{0,4},{4,0},{8,12},{12,8},{16,20},{20,16},{24,28},{28,24},{1,5},{5... | collective-permute-start | bytes 26120 | tf_op jit(solution)/shard_map/ppermute | solution.py:26
  339.4 12.1 %collective-permute-start.51 = (bf16[1024,128]{1,0:T(8,128)(2,1)}, bf16[1024,128]{1,0:T(8,128)(2,1)S(1)}, u32[]{:S(2)}, u32[]{:S(2)}) collective-permute-start(bf16[1024,128]{1,0:T(8,128)(2,1)} %pad_maximum_fusion.1.refs_1_), channel_id=1, source_target_pairs={{0,1},{1,0},{2,3},{3,2},{4,5},{5,4},{6,7},{7,6},{8,9},{9,8},{10,11... | collective-permute-start | bytes 786440 | tf_op jit(solution)/shard_map/ppermute | solution.py:26
  339.5 6.3 %collective-permute-start.44 = (f32[2176]{0:T(1024)S(1)}, f32[2176]{0:T(1024)S(1)}, u32[]{:S(2)}, u32[]{:S(2)}) collective-permute-start(f32[2176]{0:T(1024)S(1)} %add.454), channel_id=1, source_target_pairs={{0,8},{4,12},{8,0},{12,4},{16,24},{20,28},{24,16},{28,20},{1,9},{5... | collective-permute-start | bytes 26120 | tf_op jit(solution)/shard_map/ppermute | solution.py:26
  345.8 4.6 %collective-permute-start.45 = (f32[2176]{0:T(1024)S(1)}, f32[2176]{0:T(1024)S(1)}, u32[]{:S(2)}, u32[]{:S(2)}) collective-permute-start(f32[2176]{0:T(1024)S(1)} %add.455), channel_id=1, source_target_pairs={{0,16},{4,20},{8,24},{12,28},{16,0},{20,4},{24,8},{28,12},{1,17},{... | collective-permute-start | bytes 26120 | tf_op jit(solution)/shard_map/ppermute | solution.py:26
  352.5 21.5 %collective-permute-start.52 = (bf16[1024,128]{1,0:T(8,128)(2,1)S(1)}, bf16[1024,128]{1,0:T(8,128)(2,1)S(1)}, u32[]{:S(2)}, u32[]{:S(2)}) collective-permute-start(bf16[1024,128]{1,0:T(8,128)(2,1)S(1)} %fusion.186.refs_0_), channel_id=1, source_target_pairs={{0,2},{1,3},{2,0},{3,1},{4,6},{5,7},{6,4},{7,5},{8,10},{9,11},{10,... | collective-permute-start | bytes 786440 | tf_op jit(solution)/shard_map/ppermute | solution.py:26
  356.5 21.0 %collective-permute-start.48 = (bf16[512,256]{1,0:T(8,128)(2,1)}, bf16[512,256]{1,0:T(8,128)(2,1)}, u32[]{:S(2)}, u32[]{:S(2)}) collective-permute-start(bf16[512,256]{1,0:T(8,128)(2,1)} %get-tuple-element.192), channel_id=1, source_target_pairs={{0,8},{4,12},{8,0},{12,4},{16,24},{20,28},{24,16},{28,20},{1,9},{5... | collective-permute-start | bytes 786440 | tf_op jit(solution)/shard_map/ppermute | solution.py:26
  358.5 19.0 %collective-permute-start.49 = (bf16[512,256]{1,0:T(8,128)(2,1)}, bf16[512,256]{1,0:T(8,128)(2,1)}, u32[]{:S(2)}, u32[]{:S(2)}) collective-permute-start(bf16[512,256]{1,0:T(8,128)(2,1)} %get-tuple-element.194), channel_id=1, source_target_pairs={{0,16},{4,20},{8,24},{12,28},{16,0},{20,4},{24,8},{28,12},{1,17},{... | collective-permute-start | bytes 786440 | tf_op jit(solution)/shard_map/ppermute | solution.py:26
  359.1 22.1 %collective-permute-start.50 = (bf16[512,256]{1,0:T(8,128)(2,1)}, bf16[512,256]{1,0:T(8,128)(2,1)}, u32[]{:S(2)}, u32[]{:S(2)}) collective-permute-start(bf16[512,256]{1,0:T(8,128)(2,1)} %get-tuple-element.193), channel_id=1, source_target_pairs={{0,24},{4,28},{8,16},{12,20},{16,8},{20,12},{24,0},{28,4},{1,25},{... | collective-permute-start | bytes 786440 | tf_op jit(solution)/shard_map/ppermute | solution.py:26
  (101 other events, 394.4 us)
